TPU v7x, 128 devices: a whole 4x4x4 slice. The times are simulated.
128 devices in a mesh: patch: 32 (over x, z, core), grp: 4 (over y).
Axes of the slice: x: 4, y: 4, z: 4, core: 2. Of those that a mesh axis runs over, the one named last changes fastest.
Arguments:
- incident: float32 [16, 262144], P(None, ('patch', 'grp')), may hold values from -6 to 6
- self_term: float32 [262144], P(('patch', 'grp')), may hold values from 1 to 3
- near_field: bfloat16 [262144, 2304], P(('patch', 'grp')), may hold values from -0.125 to 0.125
- history: bfloat16 [8, 16, 262144], P(None, None, 'patch'), may hold values from -6 to 6
- ret_values: bfloat16 [32768, 128, 128], P(('patch', 'grp')), may hold values from -0.125 to 0.125
- slot_row: int32 [32768], P(('patch', 'grp')), may hold values from 0 to 15
- slot_col: int32 [32768], P(('patch', 'grp')), may hold values from 0 to 191
- slot_delay: int32 [32768], P(('patch', 'grp')), may hold values from 0 to 7
- live_count: int32 [128], P(('patch', 'grp')), may hold values from 32 to 256, as said below
Outputs:
- current: float32 [16, 262144], P(None, ('patch', 'grp'))
- newest: bfloat16 [16, 262144], P(None, 'patch')
Inputs may be any that keep to these rules, and one draw needn't show every extreme that they name: The first live_count[d] slots of shard d are live, the rest ignored; some shard has all 256 slots live.
All inputs are finite; a program needn't handle non-finite values.
Results may differ from a plain program's by a relative error of at most 0.0055.
Values may be sent and summed in bfloat16 or wider, within the bound.
No kernel may reach another device: no remote copies, remote signals or barrier semaphores. Data moves between devices by JAX's collectives and lax.ppermute only.
A program may use at most 128 MiB of HBM per device.

v0:
```python
import jax
import jax.numpy as jnp
from jax import lax
from jax.sharding import PartitionSpec as P

BLK = 128
DELAYS = 8
SWEEPS = 4
RB = 16
SLOTS = 256


def extended_2(block, sides, width):
    for axis, dim in sides:
        count = lax.axis_size(axis)
        forward = [(i, i + 1) for i in range(count - 1)]
        backward = [(target, source) for source, target in forward]
        low = lax.ppermute(
            lax.slice_in_dim(block, block.shape[dim] - width, None, axis=dim), axis, forward
        )
        high = lax.ppermute(lax.slice_in_dim(block, 0, width, axis=dim), axis, backward)
        block = jnp.concatenate([low, block, high], axis=dim)
    return block


def body(
    incident, self_term, near_field, history, ret_values, slot_row, slot_col, slot_delay, live_count
):
    waves = incident.shape[0]
    own_cols = incident.shape[1]
    group_idx = lax.axis_index("grp")
    window = extended_2(history, (("patch", 2),), history.shape[2])
    grouped = window.reshape(DELAYS, waves, window.shape[2] // BLK, BLK)
    limit = live_count[0]
    blocks = grouped[slot_delay, :, slot_col, :]
    prods = jnp.einsum("swj,sij->swi", blocks, ret_values, preferred_element_type=jnp.float32)
    alive = (jnp.arange(SLOTS, dtype=jnp.int32) < limit).astype(jnp.float32)
    onehot = (slot_row[None, :] == jnp.arange(RB, dtype=jnp.int32)[:, None]).astype(
        jnp.float32
    ) * alive[None, :]
    retarded = jnp.einsum("rs,swi->wri", onehot, prods, precision=lax.Precision.HIGHEST)
    rhs = incident - retarded.reshape(waves, own_cols)
    sweep_in = lax.dynamic_slice_in_dim(history[0], group_idx * own_cols, own_cols, 1)
    current = sweep_in.astype(jnp.float32)
    for sweep in range(SWEEPS):
        extended = extended_2(sweep_in, (("patch", 1),), BLK)
        coupling = lax.dot_general(
            extended, near_field, (((1,), (1,)), ((), ())), preferred_element_type=jnp.float32
        )
        current = (rhs - coupling) / self_term[None, :]
        sweep_in = current.astype(jnp.bfloat16)
    newest = lax.all_gather(sweep_in, "grp", axis=1, tiled=True)
    return (current, newest)


def solution(mesh):
    placed = (
        P(None, ("patch", "grp")),
        P(("patch", "grp")),
        P(("patch", "grp"), None),
        P(None, None, "patch"),
        P(("patch", "grp"), None, None),
        P(("patch", "grp")),
        P(("patch", "grp")),
        P(("patch", "grp")),
        P(("patch", "grp")),
    )
    return jax.shard_map(
        body,
        mesh=mesh,
        in_specs=placed,
        out_specs=(P(None, ("patch", "grp")), P(None, "patch")),
        check_vma=False,
    )
```

profile of v0, /device:TPU:6, one launch (start us, length us, event | category | flops | bytes accessed | tf_op | source)
XLA Modules:
  0.0 111.1 jit_solution(12761360910164445370)
XLA Ops:
  0.6 5.7 %collective-permute-start.1 = (bf16[8,16,8192]{2,1,0:T(8,128)(2,1)}, bf16[8,16,8192]{2,1,0:T(8,128)(2,1)S(1)}, u32[]{:S(2)}, u32[]{:S(2)}) collective-permute-start(bf16[8,16,8192]{2,1,0:T(8,128)(2,1)} %param.12), channel_id=1, source_target_pairs={{4,0},{8,4},{12,8},{16,12},{20,16},{24,20},{28,24},{32,28},{36,32}... | collective-permute-start | bytes 6291464 | tf_op jit(solution)/shard_map/ppermute | solution.py:21
  6.3 1.9 %collective-permute-start = (bf16[8,16,8192]{2,1,0:T(8,128)(2,1)}, bf16[8,16,8192]{2,1,0:T(8,128)(2,1)}, u32[]{:S(2)}, u32[]{:S(2)}) collective-permute-start(bf16[8,16,8192]{2,1,0:T(8,128)(2,1)} %param.12), channel_id=1, source_target_pairs={{0,4},{4,8},{8,12},{12,16},{16,20},{20,24},{24,28},{28,32},{32,36}... | collective-permute-start | bytes 6291464 | tf_op jit(solution)/shard_map/ppermute | solution.py:18
  8.2 1.0 slice.27
  9.2 5.8 %collective-permute-start.3 = (bf16[16,128]{1,0:T(8,128)(2,1)S(1)}, bf16[16,128]{1,0:T(8,128)(2,1)S(1)}, u32[]{:S(2)}, u32[]{:S(2)}) collective-permute-start(bf16[16,128]{1,0:T(8,128)(2,1)S(1)} %get-tuple-element.9), channel_id=1, source_target_pairs={{4,0},{8,4},{12,8},{16,12},{20,16},{24,20},{28,24},{32,28},{36,32}... | collective-permute-start | bytes 12296 | tf_op jit(solution)/shard_map/ppermute | solution.py:21
  15.0 1.9 %collective-permute-start.2 = (bf16[16,128]{1,0:T(8,128)(2,1)S(1)}, bf16[16,128]{1,0:T(8,128)(2,1)S(1)}, u32[]{:S(2)}, u32[]{:S(2)}) collective-permute-start(bf16[16,128]{1,0:T(8,128)(2,1)S(1)} %get-tuple-element.8), channel_id=1, source_target_pairs={{0,4},{4,8},{8,12},{12,16},{16,20},{20,24},{24,28},{28,32},{32,36}... | collective-permute-start | bytes 12296 | tf_op jit(solution)/shard_map/ppermute | solution.py:18
  17.6 0.7 fusion.36
  18.3 11.8 %collective-permute-done.1 = bf16[8,16,8192]{2,1,0:T(8,128)(2,1)S(1)} collective-permute-done((bf16[8,16,8192]{2,1,0:T(8,128)(2,1)}, bf16[8,16,8192]{2,1,0:T(8,128)(2,1)S(1)}, u32[]{:S(2)}, u32[]{:S(2)}) %collective-permute-start.1) | collective-permute-done | bytes 2097184 | tf_op jit(solution)/shard_map/ppermute | solution.py:21
  30.1 5.9 %collective-permute-done = bf16[8,16,8192]{2,1,0:T(8,128)(2,1)} collective-permute-done((bf16[8,16,8192]{2,1,0:T(8,128)(2,1)}, bf16[8,16,8192]{2,1,0:T(8,128)(2,1)}, u32[]{:S(2)}, u32[]{:S(2)}) %collective-permute-start) | collective-permute-done | bytes 2097184 | tf_op jit(solution)/shard_map/ppermute | solution.py:18
  36.1 7.2 %copy_bitcast_fusion = bf16[8,16,192,128]{3,1,2,0:T(8,128)(2,1)} fusion(bf16[8,16,8192]{2,1,0:T(8,128)(2,1)S(1)} %collective-permute-done.1, bf16[8,16,8192]{2,1,0:T(8,128)(2,1)} %param.12, bf16[8,16,8192]{2,1,0:T(8,128)(2,1)} %collective-permute-done), kind=kLoop, calls=%fused_computation.1 | loop fusion | flops 18874368 | bytes 12582912 | tf_op jit(solution)/shard_map/reshape | solution.py:33
  43.2 4.0 %gather_fusion = bf16[256,16,128]{2,1,0:T(8,128)(2,1)S(1)} fusion(bf16[8,16,192,128]{3,1,2,0:T(8,128)(2,1)} %copy_bitcast_fusion, s32[256]{0:T(256)S(1)} %fusion.36), kind=kCustom, calls=%fused_computation | custom fusion | bytes 2099200 | tf_op jit(solution)/shard_map/gather | solution.py:35
  47.3 0.0 copy-start.1
  47.3 0.0 slice-start
  47.3 6.9 %fusion.49 = f32[256,16,128]{2,1,0:T(8,128)S(1)} fusion(bf16[256,16,128]{2,1,0:T(8,128)(2,1)S(1)} %gather_fusion, bf16[256,128,128]{2,1,0:T(8,128)(2,1)} %param.13), kind=kOutput, calls=%fused_computation.62 | convolution fusion | flops 134217728 | bytes 11534336 | tf_op jit(solution)/shard_map/swj,sij->swi/dot_general | solution.py:36
  54.2 1.8 %fusion.7 = f32[16,128,16]{1,2,0:T(8,128)S(1)} fusion(f32[256,16,128]{2,1,0:T(8,128)S(1)} %fusion.49, f32[256]{0:T(256)S(1)} %compare_convert_fusion, s32[256]{0:T(256)S(1)} %copy-done.2), kind=kOutput, calls=%fused_computation.14 | convolution fusion | flops 100671488 | bytes 2230272 | tf_op jit(solution)/shard_map/rs,swi->wri/dot_general | solution.py:41
  56.0 0.0 copy-done.1
  56.0 0.1 bitcast_subtract_fusion
  56.0 0.0 slice-start.2
  56.1 6.3 %fusion.4 = bf16[16,2048]{1,0:T(8,128)(2,1)S(1)} fusion(f32[16,2048]{1,0:T(8,128)S(1)} %bitcast_subtract_fusion, bf16[2048,2304]{1,0:T(8,128)(2,1)} %param.11, bf16[16,128]{1,0:T(8,128)(2,1)S(1)} %collective-permute-done.3, bf16[16,2048]{1,0:T(8,128)(2,1)S(1)} %dynamic-slice_bitcast_fusion, bf16[16,128]{1,0:T(8,128)(2,1)S(1)} %collective-permute-done.2, ...), kind=kOutput, calls=%fused_computation.11 | convolution fusion | flops 151314432 | bytes 9715712 | tf_op jit(solution)/shard_map/dot_general | solution.py:47
  62.4 1.9 %collective-permute-start.5 = (bf16[16,128]{1,0:T(8,128)(2,1)S(1)}, bf16[16,128]{1,0:T(8,128)(2,1)S(1)}, u32[]{:S(2)}, u32[]{:S(2)}) collective-permute-start(bf16[16,128]{1,0:T(8,128)(2,1)S(1)} %get-tuple-element.7), channel_id=1, source_target_pairs={{4,0},{8,4},{12,8},{16,12},{20,16},{24,20},{28,24},{32,28},{36,32}... | collective-permute-start | bytes 12296 | tf_op jit(solution)/shard_map/ppermute | solution.py:21
  64.3 2.4 %collective-permute-start.4 = (bf16[16,128]{1,0:T(8,128)(2,1)S(1)}, bf16[16,128]{1,0:T(8,128)(2,1)S(1)}, u32[]{:S(2)}, u32[]{:S(2)}) collective-permute-start(bf16[16,128]{1,0:T(8,128)(2,1)S(1)} %get-tuple-element.6), channel_id=1, source_target_pairs={{0,4},{4,8},{8,12},{12,16},{16,20},{20,24},{24,28},{28,32},{32,36}... | collective-permute-start | bytes 12296 | tf_op jit(solution)/shard_map/ppermute | solution.py:18
  66.8 4.6 %collective-permute-done.4 = bf16[16,128]{1,0:T(8,128)(2,1)S(1)} collective-permute-done((bf16[16,128]{1,0:T(8,128)(2,1)S(1)}, bf16[16,128]{1,0:T(8,128)(2,1)S(1)}, u32[]{:S(2)}, u32[]{:S(2)}) %collective-permute-start.4) | collective-permute-done | bytes 4128 | tf_op jit(solution)/shard_map/ppermute | solution.py:18
  71.4 2.5 %fusion.5 = bf16[16,2048]{1,0:T(8,128)(2,1)S(1)} fusion(f32[16,2048]{1,0:T(8,128)S(1)} %bitcast_subtract_fusion, bf16[2048,2304]{1,0:T(8,128)(2,1)S(1)} %bitcast.23, bf16[16,128]{1,0:T(8,128)(2,1)S(1)} %collective-permute-done.5, bf16[16,2048]{1,0:T(8,128)(2,1)S(1)} %fusion.4, bf16[16,128]{1,0:T(8,128)(2,1)S(1)} %collective-permute-done.4, f32[2048]{0:T(1024)S(1)} %copy-done), kind=kOutput, calls=%fused_computation.12 | convolution fusion | flops 151314432 | bytes 9715712 | tf_op jit(solution)/shard_map/dot_general | solution.py:47
  73.9 1.9 %collective-permute-start.7 = (bf16[16,128]{1,0:T(8,128)(2,1)S(1)}, bf16[16,128]{1,0:T(8,128)(2,1)S(1)}, u32[]{:S(2)}, u32[]{:S(2)}) collective-permute-start(bf16[16,128]{1,0:T(8,128)(2,1)S(1)} %get-tuple-element.5), channel_id=1, source_target_pairs={{4,0},{8,4},{12,8},{16,12},{20,16},{24,20},{28,24},{32,28},{36,32}... | collective-permute-start | bytes 12296 | tf_op jit(solution)/shard_map/ppermute | solution.py:21
  75.9 2.4 %collective-permute-start.6 = (bf16[16,128]{1,0:T(8,128)(2,1)S(1)}, bf16[16,128]{1,0:T(8,128)(2,1)S(1)}, u32[]{:S(2)}, u32[]{:S(2)}) collective-permute-start(bf16[16,128]{1,0:T(8,128)(2,1)S(1)} %get-tuple-element.4), channel_id=1, source_target_pairs={{0,4},{4,8},{8,12},{12,16},{16,20},{20,24},{24,28},{28,32},{32,36}... | collective-permute-start | bytes 12296 | tf_op jit(solution)/shard_map/ppermute | solution.py:18
  78.3 4.6 %collective-permute-done.6 = bf16[16,128]{1,0:T(8,128)(2,1)S(1)} collective-permute-done((bf16[16,128]{1,0:T(8,128)(2,1)S(1)}, bf16[16,128]{1,0:T(8,128)(2,1)S(1)}, u32[]{:S(2)}, u32[]{:S(2)}) %collective-permute-start.6) | collective-permute-done | bytes 4128 | tf_op jit(solution)/shard_map/ppermute | solution.py:18
  82.9 2.5 %fusion.6 = bf16[16,2048]{1,0:T(8,128)(2,1)S(1)} fusion(f32[16,2048]{1,0:T(8,128)S(1)} %bitcast_subtract_fusion, bf16[2048,2304]{1,0:T(8,128)(2,1)S(1)} %bitcast.23, bf16[16,128]{1,0:T(8,128)(2,1)S(1)} %collective-permute-done.7, bf16[16,2048]{1,0:T(8,128)(2,1)S(1)} %fusion.5, bf16[16,128]{1,0:T(8,128)(2,1)S(1)} %collective-permute-done.6, f32[2048]{0:T(1024)S(1)} %copy-done), kind=kOutput, calls=%fused_computation.13 | convolution fusion | flops 151314432 | bytes 9715712 | tf_op jit(solution)/shard_map/dot_general | solution.py:47
  85.5 1.9 %collective-permute-start.9 = (bf16[16,128]{1,0:T(8,128)(2,1)S(1)}, bf16[16,128]{1,0:T(8,128)(2,1)S(1)}, u32[]{:S(2)}, u32[]{:S(2)}) collective-permute-start(bf16[16,128]{1,0:T(8,128)(2,1)S(1)} %get-tuple-element.3), channel_id=1, source_target_pairs={{4,0},{8,4},{12,8},{16,12},{20,16},{24,20},{28,24},{32,28},{36,32}... | collective-permute-start | bytes 12296 | tf_op jit(solution)/shard_map/ppermute | solution.py:21
  87.4 2.4 %collective-permute-start.8 = (bf16[16,128]{1,0:T(8,128)(2,1)S(1)}, bf16[16,128]{1,0:T(8,128)(2,1)S(1)}, u32[]{:S(2)}, u32[]{:S(2)}) collective-permute-start(bf16[16,128]{1,0:T(8,128)(2,1)S(1)} %get-tuple-element.2), channel_id=1, source_target_pairs={{0,4},{4,8},{8,12},{12,16},{16,20},{20,24},{24,28},{28,32},{32,36}... | collective-permute-start | bytes 12296 | tf_op jit(solution)/shard_map/ppermute | solution.py:18
  89.8 4.6 %collective-permute-done.8 = bf16[16,128]{1,0:T(8,128)(2,1)S(1)} collective-permute-done((bf16[16,128]{1,0:T(8,128)(2,1)S(1)}, bf16[16,128]{1,0:T(8,128)(2,1)S(1)}, u32[]{:S(2)}, u32[]{:S(2)}) %collective-permute-start.8) | collective-permute-done | bytes 4128 | tf_op jit(solution)/shard_map/ppermute | solution.py:18
  94.4 3.2 %fusion.48 = (bf16[16,2048]{1,0:T(8,128)(2,1)S(1)}, f32[16,2048]{1,0:T(8,128)}) fusion(f32[2048]{0:T(1024)S(1)} %copy-done, f32[16,2048]{1,0:T(8,128)S(1)} %bitcast_subtract_fusion, bf16[2048,2304]{1,0:T(8,128)(2,1)S(1)} %bitcast.23, bf16[16,128]{1,0:T(8,128)(2,1)S(1)} %collective-permute-done.9, bf16[16,2048]{1,0:T(8,128)(2,1)S(1)} %fusion.6, ...), kind=kOutput, calls=%fused_computation.61 | convolution fusion | flops 151314432 | bytes 9846784 | tf_op jit(solution)/shard_map/dot_general | solution.py:47
  97.6 12.8 %all_gather.3 = bf16[16,8192]{1,0:T(8,128)(2,1)S(1)} all-gather(bf16[16,2048]{1,0:T(8,128)(2,1)S(1)} %get-tuple-element.10), channel_id=1, replica_groups=mesh['patch'=32,'grp'=4] {'grp'}, dimensions={1}, use_global_device_ids=true | all-gather | bytes 327680 | tf_op jit(solution)/shard_map/all_gather | solution.py:52
  110.4 0.7 copy.21
  (20 shorter events, 0.1 us)
Async XLA Ops:
  0.6 29.5 %collective-permute-start.1 = (bf16[8,16,8192]{2,1,0:T(8,128)(2,1)}, bf16[8,16,8192]{2,1,0:T(8,128)(2,1)S(1)}, u32[]{:S(2)}, u32[]{:S(2)}) collective-permute-start(bf16[8,16,8192]{2,1,0:T(8,128)(2,1)} %param.12), channel_id=1, source_target_pairs={{4,0},{8,4},{12,8},{16,12},{20,16},{24,20},{28,24},{32,28},{36,32}... | collective-permute-start | bytes 6291464 | tf_op jit(solution)/shard_map/ppermute | solution.py:21
  6.3 29.8 %collective-permute-start = (bf16[8,16,8192]{2,1,0:T(8,128)(2,1)}, bf16[8,16,8192]{2,1,0:T(8,128)(2,1)}, u32[]{:S(2)}, u32[]{:S(2)}) collective-permute-start(bf16[8,16,8192]{2,1,0:T(8,128)(2,1)} %param.12), channel_id=1, source_target_pairs={{0,4},{4,8},{8,12},{12,16},{16,20},{20,24},{24,28},{28,32},{32,36}... | collective-permute-start | bytes 6291464 | tf_op jit(solution)/shard_map/ppermute | solution.py:18
  9.2 46.8 %collective-permute-start.3 = (bf16[16,128]{1,0:T(8,128)(2,1)S(1)}, bf16[16,128]{1,0:T(8,128)(2,1)S(1)}, u32[]{:S(2)}, u32[]{:S(2)}) collective-permute-start(bf16[16,128]{1,0:T(8,128)(2,1)S(1)} %get-tuple-element.9), channel_id=1, source_target_pairs={{4,0},{8,4},{12,8},{16,12},{20,16},{24,20},{28,24},{32,28},{36,32}... | collective-permute-start | bytes 12296 | tf_op jit(solution)/shard_map/ppermute | solution.py:21
  15.0 41.1 %collective-permute-start.2 = (bf16[16,128]{1,0:T(8,128)(2,1)S(1)}, bf16[16,128]{1,0:T(8,128)(2,1)S(1)}, u32[]{:S(2)}, u32[]{:S(2)}) collective-permute-start(bf16[16,128]{1,0:T(8,128)(2,1)S(1)} %get-tuple-element.8), channel_id=1, source_target_pairs={{0,4},{4,8},{8,12},{12,16},{16,20},{20,24},{24,28},{28,32},{32,36}... | collective-permute-start | bytes 12296 | tf_op jit(solution)/shard_map/ppermute | solution.py:18
  47.2 7.0 %copy-start.2 = (s32[256]{0:T(256)S(1)}, s32[256]{0:T(256)}, u32[]{:S(2)}) copy-start(s32[256]{0:T(256)} %param.14) | copy-start | bytes 3076
  47.3 8.7 %copy-start.1 = (f32[16,2048]{1,0:T(8,128)S(1)}, f32[16,2048]{1,0:T(8,128)}, u32[]{:S(2)}) copy-start(f32[16,2048]{1,0:T(8,128)} %param.9) | copy-start | bytes 393220
  47.3 8.8 %copy-start = (f32[2048]{0:T(1024)S(1)}, f32[2048]{0:T(1024)}, u32[]{:S(2)}) copy-start(f32[2048]{0:T(1024)} %param.10) | copy-start | bytes 24580
  47.3 24.1 %slice-start = ((s8[9437184]{0:T(1024)(128)(4,1)}), s8[4194304]{0:T(1024)(128)(4,1)S(1)}, s32[]{:S(2)}) async-start(s8[9437184]{0:T(1024)(128)(4,1)} %bitcast.22), calls=%async_computation | async-start | bytes 8388608
  47.3 24.1 %slice-start.1 = ((s8[9437184]{0:T(1024)(128)(4,1)}), s8[4194304]{0:T(1024)(128)(4,1)S(1)}, s32[]{:S(2)}) async-start(s8[9437184]{0:T(1024)(128)(4,1)} %bitcast.22), calls=%async_computation.1 | async-start | bytes 8388608
  56.0 15.3 %slice-start.2 = ((s8[9437184]{0:T(1024)(128)(4,1)}), s8[1048576]{0:T(1024)(128)(4,1)S(1)}, s32[]{:S(2)}) async-start(s8[9437184]{0:T(1024)(128)(4,1)} %bitcast.22), calls=%async_computation.2 | async-start | bytes 2097152
  62.4 4.3 %collective-permute-start.5 = (bf16[16,128]{1,0:T(8,128)(2,1)S(1)}, bf16[16,128]{1,0:T(8,128)(2,1)S(1)}, u32[]{:S(2)}, u32[]{:S(2)}) collective-permute-start(bf16[16,128]{1,0:T(8,128)(2,1)S(1)} %get-tuple-element.7), channel_id=1, source_target_pairs={{4,0},{8,4},{12,8},{16,12},{20,16},{24,20},{28,24},{32,28},{36,32}... | collective-permute-start | bytes 12296 | tf_op jit(solution)/shard_map/ppermute | solution.py:21
  64.3 7.0 %collective-permute-start.4 = (bf16[16,128]{1,0:T(8,128)(2,1)S(1)}, bf16[16,128]{1,0:T(8,128)(2,1)S(1)}, u32[]{:S(2)}, u32[]{:S(2)}) collective-permute-start(bf16[16,128]{1,0:T(8,128)(2,1)S(1)} %get-tuple-element.6), channel_id=1, source_target_pairs={{0,4},{4,8},{8,12},{12,16},{16,20},{20,24},{24,28},{28,32},{32,36}... | collective-permute-start | bytes 12296 | tf_op jit(solution)/shard_map/ppermute | solution.py:18
  73.9 4.3 %collective-permute-start.7 = (bf16[16,128]{1,0:T(8,128)(2,1)S(1)}, bf16[16,128]{1,0:T(8,128)(2,1)S(1)}, u32[]{:S(2)}, u32[]{:S(2)}) collective-permute-start(bf16[16,128]{1,0:T(8,128)(2,1)S(1)} %get-tuple-element.5), channel_id=1, source_target_pairs={{4,0},{8,4},{12,8},{16,12},{20,16},{24,20},{28,24},{32,28},{36,32}... | collective-permute-start | bytes 12296 | tf_op jit(solution)/shard_map/ppermute | solution.py:21
  75.9 7.0 %collective-permute-start.6 = (bf16[16,128]{1,0:T(8,128)(2,1)S(1)}, bf16[16,128]{1,0:T(8,128)(2,1)S(1)}, u32[]{:S(2)}, u32[]{:S(2)}) collective-permute-start(bf16[16,128]{1,0:T(8,128)(2,1)S(1)} %get-tuple-element.4), channel_id=1, source_target_pairs={{0,4},{4,8},{8,12},{12,16},{16,20},{20,24},{24,28},{28,32},{32,36}... | collective-permute-start | bytes 12296 | tf_op jit(solution)/shard_map/ppermute | solution.py:18
  85.5 4.3 %collective-permute-start.9 = (bf16[16,128]{1,0:T(8,128)(2,1)S(1)}, bf16[16,128]{1,0:T(8,128)(2,1)S(1)}, u32[]{:S(2)}, u32[]{:S(2)}) collective-permute-start(bf16[16,128]{1,0:T(8,128)(2,1)S(1)} %get-tuple-element.3), channel_id=1, source_target_pairs={{4,0},{8,4},{12,8},{16,12},{20,16},{24,20},{28,24},{32,28},{36,32}... | collective-permute-start | bytes 12296 | tf_op jit(solution)/shard_map/ppermute | solution.py:21
  87.4 7.0 %collective-permute-start.8 = (bf16[16,128]{1,0:T(8,128)(2,1)S(1)}, bf16[16,128]{1,0:T(8,128)(2,1)S(1)}, u32[]{:S(2)}, u32[]{:S(2)}) collective-permute-start(bf16[16,128]{1,0:T(8,128)(2,1)S(1)} %get-tuple-element.2), channel_id=1, source_target_pairs={{0,4},{4,8},{8,12},{12,16},{16,20},{20,24},{24,28},{28,32},{32,36}... | collective-permute-start | bytes 12296 | tf_op jit(solution)/shard_map/ppermute | solution.py:18
where the time goes:
time: 112 us; the launch traced here: 111 us
  waiting for transfers between devices  31.6 us (28%)
  starting transfers between devices  28.2 us (25%)
  matrix products  23.2 us (21%)
  blocking collectives  12.8 us (11%)
  other arithmetic  7.93 us (7%)
  local copies, waits for them, and re-layouts  5.77 us (5%)
  between operations  1.54 us (1%)
    ppermute x5, waiting for transfers between devices, extended_2(): lax.ppermute(lax.slice_in_dim(block, block.shape[dim] - width, None, axis...  19.8 us
    ppermute x5, starting transfers between devices, extended_2(): lax.ppermute(lax.slice_in_dim(block, 0, width, axis=dim), axis, backward)  17.2 us
    dot_general x4, matrix products, body(): lax.dot_general(extended, near_field, (((1,), (1,)), ((), ())), preferred...  14.6 us
    all_gather x1, blocking collectives, body(): newest = lax.all_gather(sweep_in, 'grp', axis=1, tiled=True)  12.8 us
    ppermute x5, waiting for transfers between devices, extended_2(): lax.ppermute(lax.slice_in_dim(block, 0, width, axis=dim), axis, backward)  11.9 us
    ppermute x5, starting transfers between devices, extended_2(): lax.ppermute(lax.slice_in_dim(block, block.shape[dim] - width, None, axis...  11.1 us
    reshape x1, other arithmetic, body(): grouped = window.reshape(DELAYS, waves, window.shape[2] // BLK, BLK)  7.16 us
    dot_general x1, matrix products, body(): jnp.einsum('swj,sij->swi', blocks, ret_values, preferred_element_type=jnp...  6.91 us
  transfers between devices with their start and end apart: 10, of which 5 were waited for; matrix products, arithmetic and copies ran while one was open for 19% of the time, Pallas kernels for 0%

commit v1 on v0

v1 whole, which is shorter than its diff:
```python
import jax
import jax.numpy as jnp
from jax import lax
from jax.experimental import pallas as pl
from jax.experimental.pallas import tpu as pltpu
from jax.sharding import PartitionSpec as P

BLK = 128
WAVES = 16
DELAYS = 8
SWEEPS = 4
RB = 16
SLOTS = 256
OWN = RB * BLK
EDGE = OWN + BLK
PATCH = 4 * OWN
COLS = PATCH // BLK
UNROLL = 8
ROWS = 256
NT = (((1,), (1,)), ((), ()))

VMEM = pl.BlockSpec(memory_space=pltpu.VMEM)
SMEM = pl.BlockSpec(memory_space=pltpu.SMEM)


def f32(*shape):
    return jax.ShapeDtypeStruct(shape, jnp.float32)


def bf16(*shape):
    return jax.ShapeDtypeStruct(shape, jnp.bfloat16)


def in_vmem(x):
    return pltpu.with_memory_space_constraint(x, pltpu.VMEM)


def call(body, out, ins, outs, args, flops, touched, scratch=()):
    return pl.pallas_call(
        body,
        out_shape=out,
        in_specs=ins,
        out_specs=outs,
        scratch_shapes=scratch,
        compiler_params=pltpu.CompilerParams(vmem_limit_bytes=30 * 2**20),
        cost_estimate=pl.CostEstimate(flops=flops, bytes_accessed=touched, transcendentals=0),
    )(*args)


def add_slots(count, codes, values, acc, block_of):
    def step(i, carry):
        found = []
        for j in range(0, UNROLL, 2):
            pair = []
            for k in (j, j + 1):
                at = i * UNROLL + k
                code = codes[at]
                block = block_of(code)
                block = jnp.where(at < count, block, jnp.zeros_like(block))
                pair.append((code, block))
            (code_a, a), (code_b, b) = pair
            zero = jnp.zeros_like(a)
            left = jnp.concatenate(
                [jnp.concatenate([a, zero], axis=1), jnp.concatenate([zero, b], axis=1)], axis=0
            )
            right = jnp.concatenate([values[code_a & 255], values[code_b & 255]], axis=1)
            both = lax.dot_general(left, right, NT, preferred_element_type=jnp.float32)
            found.append((code_a, both[:WAVES]))
            found.append((code_b, both[WAVES:]))
        for code, part in found:
            row = (code >> 8) & 15
            acc[row] = acc[row] + part
        return carry

    lax.fori_loop(0, (count + UNROLL - 1) // UNROLL, step, 0)


def own_coupling(x, near, out):
    def step(i, carry):
        at = pl.multiple_of(i * ROWS, ROWS)
        rows = near[pl.ds(at, ROWS), BLK:EDGE]
        out[:, pl.ds(at, ROWS)] = lax.dot_general(x, rows, NT, preferred_element_type=jnp.float32)
        return carry

    lax.fori_loop(0, OWN // ROWS, step, 0)


def edge_coupling(parity, cross, near_side, near):
    left = jnp.where(parity == 0, cross, near_side)
    right = jnp.where(parity == 0, near_side, cross)
    both = jnp.concatenate([left, right], axis=1)
    out = []
    for at in range(0, OWN, ROWS):
        rows = jnp.concatenate(
            [near[at : at + ROWS, :BLK], near[at : at + ROWS, EDGE:]], axis=1
        )
        out.append(lax.dot_general(both, rows, NT, preferred_element_type=jnp.float32))
    return out


def first_body(
    who, live, slot_row, slot_col, slot_delay, values, near, own, side,
    acc, coupling, codes_out, codes,
):
    parity, group = who[0], who[1]
    limit = live[0]

    def sort(s, counts):
        home, far = counts
        col = slot_col[s]
        third = jnp.where(col >= 2 * COLS, 2, jnp.where(col >= COLS, 1, 0))
        is_far = third == jnp.where(parity == 0, 0, 2)
        code = (
            s
            | (slot_row[s] << 8)
            | (slot_delay[s] << 12)
            | ((col - third * COLS) << 15)
            | (jnp.where(third == 1, 0, 1) << 21)
        )
        codes[home] = code
        codes_out[1 + far] = code
        alive = s < limit
        home = home + jnp.where(alive & jnp.logical_not(is_far), 1, 0)
        far = far + jnp.where(alive & is_far, 1, 0)
        return home, far

    home, far = lax.fori_loop(0, SLOTS, sort, (0, 0))
    for k in range(UNROLL):
        codes[home + k] = 0
        codes_out[1 + far + k] = 0
    codes_out[0] = far
    acc[...] = jnp.zeros_like(acc)

    def block_of(code):
        delay = (code >> 12) & 7
        at = pl.multiple_of(((code >> 15) & 63) * BLK, BLK)
        return jnp.where(
            ((code >> 21) & 1) == 1,
            side[delay, :, pl.ds(at, BLK)],
            own[delay, :, pl.ds(at, BLK)],
        )

    add_slots(home, codes, values, acc, block_of)
    start = pl.multiple_of(group * OWN, OWN)
    own_coupling(own[0, :, pl.ds(start, OWN)], near, coupling)


def finish(rhs, coupling, parts, self_term):
    out = []
    for i, part in enumerate(parts):
        at = slice(i * ROWS, (i + 1) * ROWS)
        out.append((rhs[:, at] - (coupling[:, at] + part)) / self_term[:, at])
    return jnp.concatenate(out, axis=1)


def give_edges(parity, x, to_cross, to_side):
    first, last = x[:, :BLK], x[:, OWN - BLK :]
    to_cross[...] = jnp.where(parity == 0, first, last)
    to_side[...] = jnp.where(parity == 0, last, first)


def second_body(
    who, codes, values, near, cross, side, acc, coupling, incident, self_term,
    rhs, x_out, to_cross, to_side, total,
):
    parity, group = who[0], who[1]
    total[...] = acc[...]

    def block_of(code):
        delay = (code >> 12) & 7
        at = pl.multiple_of(((code >> 15) & 63) * BLK, BLK)
        return cross[delay, :, pl.ds(at, BLK)]

    add_slots(codes[0], _Shifted(codes), values, total, block_of)
    for r in range(RB):
        at = slice(r * BLK, (r + 1) * BLK)
        rhs[:, at] = incident[:, at] - total[r]
    first = pl.multiple_of(group * OWN, BLK)
    last = pl.multiple_of(group * OWN + OWN - BLK, BLK)
    cross_at = pl.multiple_of(jnp.where(parity == 0, last, first), BLK)
    side_at = pl.multiple_of(jnp.where(parity == 0, first, last), BLK)
    parts = edge_coupling(
        parity, cross[0, :, pl.ds(cross_at, BLK)], side[0, :, pl.ds(side_at, BLK)], near
    )
    x = finish(rhs, coupling, parts, self_term).astype(jnp.bfloat16)
    x_out[...] = x
    give_edges(parity, x, to_cross, to_side)


class _Shifted:
    def __init__(self, ref):
        self.ref = ref

    def __getitem__(self, at):
        return self.ref[at + 1]


def own_body(x, near, out):
    own_coupling(x[...], near, out)


def sweep_body(who, near, cross, side, coupling, rhs, self_term, x_out, to_cross, to_side):
    parity = who[0]
    parts = edge_coupling(parity, cross[...], side[...], near)
    x = finish(rhs, coupling, parts, self_term).astype(jnp.bfloat16)
    x_out[...] = x
    give_edges(parity, x, to_cross, to_side)


def last_body(who, near, cross, side, coupling, rhs, self_term, current, x_out):
    parts = edge_coupling(who[0], cross[...], side[...], near)
    x = finish(rhs, coupling, parts, self_term)
    current[...] = x
    x_out[...] = x.astype(jnp.bfloat16)


def join_body(who, x, after, opposite, before, out):
    group = who[1]
    for shift, part in enumerate((x, after, opposite, before)):
        owner = (group + shift) % 4
        out[:, pl.ds(pl.multiple_of(owner * OWN, OWN), OWN)] = part[...]


def body(
    incident, self_term, near_field, history, ret_values, slot_row, slot_col, slot_delay, live_count
):
    count = lax.axis_size("patch")
    patch, group = lax.axis_index("patch"), lax.axis_index("grp")
    who = jnp.stack([patch % 2, group]).astype(jnp.int32)
    diag = self_term[None, :]
    chip = [(i, i ^ 1) for i in range(count)]
    links = [(i, i + 1) for i in range(1, count - 1, 2)]
    links = links + [(b, a) for a, b in links]

    cross = lax.ppermute(history, "patch", links)
    side = lax.ppermute(history, "patch", chip)
    values, near = in_vmem(ret_values), in_vmem(near_field)

    acc, coupling, codes = call(
        first_body,
        (f32(RB, WAVES, BLK), f32(WAVES, OWN), jax.ShapeDtypeStruct((SLOTS + 2 * UNROLL,), jnp.int32)),
        [SMEM] * 5 + [VMEM] * 4,
        (VMEM, VMEM, SMEM),
        (who, live_count, slot_row, slot_col, slot_delay, values, near, history, side),
        2 * 10**9,
        20 * 10**6,
        [pltpu.SMEM((SLOTS + 2 * UNROLL,), jnp.int32)],
    )
    rhs, x, to_cross, to_side = call(
        second_body,
        (f32(WAVES, OWN), bf16(WAVES, OWN), bf16(WAVES, BLK), bf16(WAVES, BLK)),
        [SMEM] * 2 + [VMEM] * 8,
        (VMEM,) * 4,
        (who, codes, values, near, cross, side, acc, coupling, incident, diag),
        10**9,
        10**6,
        [pltpu.VMEM((RB, WAVES, BLK), jnp.float32)],
    )
    for sweep in range(1, SWEEPS):
        edge_cross = lax.ppermute(to_cross, "patch", links)
        edge_side = lax.ppermute(to_side, "patch", chip)
        coupling = call(
            own_body, f32(WAVES, OWN), [VMEM] * 2, VMEM, (x, near), 2 * WAVES * OWN * OWN, 8 * 2**20
        )
        last = sweep == SWEEPS - 1
        made = call(
            last_body if last else sweep_body,
            (f32(WAVES, OWN), bf16(WAVES, OWN))
            if last
            else (bf16(WAVES, OWN), bf16(WAVES, BLK), bf16(WAVES, BLK)),
            [SMEM] + [VMEM] * 6,
            (VMEM,) * (2 if last else 3),
            (who, near, edge_cross, edge_side, coupling, rhs, diag),
            2 * WAVES * OWN * 2 * BLK,
            2**20,
        )
        if last:
            current, x = made
        else:
            x, to_cross, to_side = made
    turns = [
        lax.ppermute(x, "grp", [((i + shift) % 4, i) for i in range(4)]) for shift in (1, 2, 3)
    ]
    newest = call(
        join_body, bf16(WAVES, PATCH), [SMEM] + [VMEM] * 4, VMEM, (who, x, *turns), 0, 2**20
    )
    return current, newest


def solution(mesh):
    placed = (
        P(None, ("patch", "grp")),
        P(("patch", "grp")),
        P(("patch", "grp"), None),
        P(None, None, "patch"),
        P(("patch", "grp"), None, None),
        P(("patch", "grp")),
        P(("patch", "grp")),
        P(("patch", "grp")),
        P(("patch", "grp")),
    )
    return jax.shard_map(
        body,
        mesh=mesh,
        in_specs=placed,
        out_specs=(P(None, ("patch", "grp")), P(None, "patch")),
        check_vma=False,
    )
```

time: 112 us -> 71.3 us (0.64)
  Pallas kernels: 0 us -> 27.2 us
  waiting for transfers between devices: 31.6 us -> 4.77 us
  matrix products: 23.2 us -> 0 us
  blocking collectives: 12.8 us -> 0 us
  other arithmetic: 7.93 us -> 0.08 us
  local copies, waits for them, and re-layouts: 5.77 us -> 10.7 us
  starting transfers between devices: 28.2 us -> 26.3 us
    pallas_call x0 -> x9, Pallas kernels: none -> 27.2 us  [call(): pl.pallas_call(body, out_shape=out, in_specs=ins, out_specs=outs, scratch...]
    ppermute x10 -> x11, waiting for transfers between devices: 31.6 us -> 4.77 us  [the longest x3 2.52 us: body(): lax.ppermute(x, 'grp', [((i + shift) % 4, i) for i in range(4)])]
    dot_general x6 -> x0, matrix products: 23.2 us -> none  [the longest x4 14.6 us: body(): lax.dot_general(extended, near_field, (((1,), (1,)), ((), ())), preferred...]
    all_gather x1 -> x0, blocking collectives: 12.8 us -> none  [body(): newest = lax.all_gather(sweep_in, 'grp', axis=1, tiled=True)]
    unnamed x13 -> x18, local copies, waits for them, and re-layouts: 0.75 us -> 10.7 us
    reshape x1 -> x0, other arithmetic: 7.16 us -> none  [body(): grouped = window.reshape(DELAYS, waves, window.shape[2] // BLK, BLK)]
    gather x1 -> x0, local copies, waits for them, and re-layouts: 4.01 us -> none  [body(): blocks = grouped[slot_delay, :, slot_col, :]]
    ppermute x10 -> x11, starting transfers between devices: 28.2 us -> 26.3 us  [the longest x3 14.1 us: body(): edge_cross = lax.ppermute(to_cross, 'patch', links)]
  transfers between devices with their start and end apart: 10 -> 11, of which waited for: 5 -> 4; matrix products, arithmetic and copies ran while one was open for 19% -> 0% of each run, Pallas kernels for 0% -> 28%
where the time goes in v1:
time: 71.3 us; the launch traced here: 70.5 us
  Pallas kernels  27.2 us (38%)
  starting transfers between devices  26.3 us (37%)
  local copies, waits for them, and re-layouts  10.7 us (15%)
  waiting for transfers between devices  4.77 us (7%)
  between operations  1.41 us (2%)
    pallas_call x9, Pallas kernels, call(): pl.pallas_call(body, out_shape=out, in_specs=ins, out_specs=outs, scratch...  27.2 us
    ppermute x3, starting transfers between devices, body(): edge_cross = lax.ppermute(to_cross, 'patch', links)  14.1 us
    unnamed x18, local copies, waits for them, and re-layouts  10.7 us
    ppermute x1, starting transfers between devices, body(): cross = lax.ppermute(history, 'patch', links)  6.3 us
    ppermute x3, starting transfers between devices, body(): lax.ppermute(x, 'grp', [((i + shift) % 4, i) for i in range(4)])  5.61 us
    ppermute x3, waiting for transfers between devices, body(): lax.ppermute(x, 'grp', [((i + shift) % 4, i) for i in range(4)])  2.52 us
    ppermute x1, waiting for transfers between devices, body(): cross = lax.ppermute(history, 'patch', links)  2.18 us
  transfers between devices with their start and end apart: 11, of which 4 were waited for; matrix products, arithmetic and copies ran while one was open for 0% of the time, Pallas kernels for 28%

profile of v1, /device:TPU:6, one launch (start us, length us, event | category | flops | bytes accessed | tf_op | source)
XLA Modules:
  0.0 70.5 jit_solution(3215061331615611896)
XLA Ops:
  0.6 0.1 collective-permute-start
  0.7 6.3 %collective-permute-start.1 = (bf16[8,16,8192]{2,1,0:T(8,128)(2,1)}, bf16[8,16,8192]{2,1,0:T(8,128)(2,1)}, u32[]{:S(2)}, u32[]{:S(2)}) collective-permute-start(bf16[8,16,8192]{2,1,0:T(8,128)(2,1)} %own.1), channel_id=1, source_target_pairs={{4,8},{12,16},{20,24},{28,32},{36,40},{44,48},{52,56},{60,64},{68,... | collective-permute-start | bytes 6291464 | tf_op jit(solution)/shard_map/ppermute | solution.py:235
  7.7 0.1 pad_add_fusion.who
  7.8 3.7 %copy-done = bf16[2048,2304]{1,0:T(8,128)(2,1)S(1)} copy-done((bf16[2048,2304]{1,0:T(8,128)(2,1)S(1)}, bf16[2048,2304]{1,0:T(8,128)(2,1)}, u32[]{:S(2)}) %copy-start) | copy-done | bytes 9437208
  11.5 3.4 %copy-done.2 = bf16[256,128,128]{2,1,0:T(8,128)(2,1)S(1)} copy-done((bf16[256,128,128]{2,1,0:T(8,128)(2,1)S(1)}, bf16[256,128,128]{2,1,0:T(8,128)(2,1)}, u32[]{:S(2)}) %copy-start.2) | copy-done | bytes 8388632
  14.8 1.6 %copy-done.3 = bf16[8,16,8192]{2,1,0:T(8,128)(2,1)S(1)} copy-done((bf16[8,16,8192]{2,1,0:T(8,128)(2,1)S(1)}, bf16[8,16,8192]{2,1,0:T(8,128)(2,1)}, u32[]{:S(2)}) %copy-start.3) | copy-done | bytes 2097176
  16.4 0.7 copy-done.6
  17.1 0.7 copy-done.7
  17.8 0.7 copy-done.8
  18.5 10.4 %shard_map.104 = (f32[16,16,128]{2,1,0:T(8,128)S(1)}, f32[16,2048]{1,0:T(8,128)S(1)}, s32[272]{0:T(512)S(1)}) custom-call(s32[2]{0:T(128)S(1)} %pad_add_fusion.who, s32[1]{0:T(128)S(6)} %copy.11.live, s32[256]{0:T(256)S(1)} %copy-done.6, s32[256]{0:T(256)S(1)} %copy-done.7, s32[256]{0:T(256)S(1)} %copy-done.8, bf16[256,128,128]{2,1,0:T(8,128)(2,1)S(1)} %copy-done.2, ...), custom_call_target="tpu_custom_call" | custom-call | flops 2000000000 | bytes 20000000 | tf_op jit(solution)/shard_map/pallas_call | solution.py:39
  28.9 2.2 %collective-permute-done.1.cross = bf16[8,16,8192]{2,1,0:T(8,128)(2,1)} collective-permute-done((bf16[8,16,8192]{2,1,0:T(8,128)(2,1)}, bf16[8,16,8192]{2,1,0:T(8,128)(2,1)}, u32[]{:S(2)}, u32[]{:S(2)}) %collective-permute-start.1) | collective-permute-done | bytes 2097184 | tf_op jit(solution)/shard_map/ppermute | solution.py:235
  31.1 2.8 %shard_map.105 = (f32[16,2048]{1,0:T(8,128)S(1)}, bf16[16,2048]{1,0:T(8,128)(2,1)S(1)}, bf16[16,128]{1,0:T(8,128)(2,1)S(1)}, bf16[16,128]{1,0:T(8,128)(2,1)S(1)}) custom-call(s32[2]{0:T(128)S(1)} %pad_add_fusion.who, s32[272]{0:T(512)S(1)} %get-tuple-element.17.codes, bf16[256,128,128]{2,1,0:T(8,128)(2,1)S(1)} %copy-done.2, ...), custom_call_target="tpu_custom_call" | custom-call | flops 1000000000 | bytes 1000000 | tf_op jit(solution)/shard_map/pallas_call | solution.py:39
  33.9 6.4 %collective-permute-start.2 = (bf16[16,128]{1,0:T(8,128)(2,1)S(1)}, bf16[16,128]{1,0:T(8,128)(2,1)S(1)}, u32[]{:S(2)}, u32[]{:S(2)}) collective-permute-start(bf16[16,128]{1,0:T(8,128)(2,1)S(1)} %get-tuple-element.20), channel_id=1, source_target_pairs={{4,8},{12,16},{20,24},{28,32},{36,40},{44,48},{52,56},{60,64},{68,... | collective-permute-start | bytes 12296 | tf_op jit(solution)/shard_map/ppermute | solution.py:260
  40.3 0.1 collective-permute-start.3
  40.4 3.1 %shard_map.106.coupling = f32[16,2048]{1,0:T(8,128)S(1)} custom-call(bf16[16,2048]{1,0:T(8,128)(2,1)S(1)} %get-tuple-element.22.x, bf16[2048,2304]{1,0:T(8,128)(2,1)S(1)} %copy-done.1), custom_call_target="tpu_custom_call" | custom-call | flops 134217728 | bytes 8388608 | tf_op jit(solution)/shard_map/pallas_call | solution.py:39
  43.5 0.9 %shard_map.107 = (bf16[16,2048]{1,0:T(8,128)(2,1)S(1)}, bf16[16,128]{1,0:T(8,128)(2,1)S(1)}, bf16[16,128]{1,0:T(8,128)(2,1)S(1)}) custom-call(s32[2]{0:T(128)S(1)} %pad_add_fusion.who, bf16[2048,2304]{1,0:T(8,128)(2,1)S(1)} %copy-done.1, bf16[16,128]{1,0:T(8,128)(2,1)S(1)} %collective-permute-done.2.cross, bf16[16,128]{1,0:T(8,128)(2,1)S(1)} %collective-permute-done.3.side, ...), custom_call_target="tpu_custom_call" | custom-call | flops 16777216 | bytes 1048576 | tf_op jit(solution)/shard_map/pallas_call | solution.py:39
  44.5 3.8 %collective-permute-start.4 = (bf16[16,128]{1,0:T(8,128)(2,1)S(1)}, bf16[16,128]{1,0:T(8,128)(2,1)S(1)}, u32[]{:S(2)}, u32[]{:S(2)}) collective-permute-start(bf16[16,128]{1,0:T(8,128)(2,1)S(1)} %get-tuple-element.24), channel_id=1, source_target_pairs={{4,8},{12,16},{20,24},{28,32},{36,40},{44,48},{52,56},{60,64},{68,... | collective-permute-start | bytes 12296 | tf_op jit(solution)/shard_map/ppermute | solution.py:260
  48.3 0.1 collective-permute-start.5
  48.4 3.1 %shard_map.108.coupling = f32[16,2048]{1,0:T(8,128)S(1)} custom-call(bf16[16,2048]{1,0:T(8,128)(2,1)S(1)} %get-tuple-element.26.x, bf16[2048,2304]{1,0:T(8,128)(2,1)S(1)} %copy-done.1), custom_call_target="tpu_custom_call" | custom-call | flops 134217728 | bytes 8388608 | tf_op jit(solution)/shard_map/pallas_call | solution.py:39
  51.5 0.0 collective-permute-done.4.cross
  51.5 0.9 %shard_map.109 = (bf16[16,2048]{1,0:T(8,128)(2,1)S(1)}, bf16[16,128]{1,0:T(8,128)(2,1)S(1)}, bf16[16,128]{1,0:T(8,128)(2,1)S(1)}) custom-call(s32[2]{0:T(128)S(1)} %pad_add_fusion.who, bf16[2048,2304]{1,0:T(8,128)(2,1)S(1)} %copy-done.1, bf16[16,128]{1,0:T(8,128)(2,1)S(1)} %collective-permute-done.4.cross, bf16[16,128]{1,0:T(8,128)(2,1)S(1)} %collective-permute-done.5.side, ...), custom_call_target="tpu_custom_call" | custom-call | flops 16777216 | bytes 1048576 | tf_op jit(solution)/shard_map/pallas_call | solution.py:39
  52.4 3.9 %collective-permute-start.6 = (bf16[16,128]{1,0:T(8,128)(2,1)S(1)}, bf16[16,128]{1,0:T(8,128)(2,1)S(1)}, u32[]{:S(2)}, u32[]{:S(2)}) collective-permute-start(bf16[16,128]{1,0:T(8,128)(2,1)S(1)} %get-tuple-element.27), channel_id=1, source_target_pairs={{4,8},{12,16},{20,24},{28,32},{36,40},{44,48},{52,56},{60,64},{68,... | collective-permute-start | bytes 12296 | tf_op jit(solution)/shard_map/ppermute | solution.py:260
  56.3 0.1 collective-permute-start.7
  56.4 3.1 %shard_map.110.coupling = f32[16,2048]{1,0:T(8,128)S(1)} custom-call(bf16[16,2048]{1,0:T(8,128)(2,1)S(1)} %get-tuple-element.29.x, bf16[2048,2304]{1,0:T(8,128)(2,1)S(1)} %copy-done.1), custom_call_target="tpu_custom_call" | custom-call | flops 134217728 | bytes 8388608 | tf_op jit(solution)/shard_map/pallas_call | solution.py:39
  59.5 1.6 %shard_map.111 = (f32[16,2048]{1,0:T(8,128)}, bf16[16,2048]{1,0:T(8,128)(2,1)S(1)}) custom-call(s32[2]{0:T(128)S(1)} %pad_add_fusion.who, bf16[2048,2304]{1,0:T(8,128)(2,1)S(1)} %copy-done.1, bf16[16,128]{1,0:T(8,128)(2,1)S(1)} %collective-permute-done.6.cross, bf16[16,128]{1,0:T(8,128)(2,1)S(1)} %collective-permute-done.7.side, ...), custom_call_target="tpu_custom_call" | custom-call | flops 16777216 | bytes 1048576 | tf_op jit(solution)/shard_map/pallas_call | solution.py:39
  61.1 1.0 %collective-permute-start.10 = (bf16[16,2048]{1,0:T(8,128)(2,1)S(1)}, bf16[16,2048]{1,0:T(8,128)(2,1)S(1)}, u32[]{:S(2)}, u32[]{:S(2)}) collective-permute-start(bf16[16,2048]{1,0:T(8,128)(2,1)S(1)} %get-tuple-element.31.x), channel_id=1, source_target_pairs={{3,0},{0,1},{1,2},{2,3},{7,4},{4,5},{5,6},{6,7},{11,8},{8,9},{9,10... | collective-permute-start | bytes 196616 | tf_op jit(solution)/shard_map/ppermute | solution.py:282
  62.1 2.9 %collective-permute-start.9 = (bf16[16,2048]{1,0:T(8,128)(2,1)S(1)}, bf16[16,2048]{1,0:T(8,128)(2,1)S(1)}, u32[]{:S(2)}, u32[]{:S(2)}) collective-permute-start(bf16[16,2048]{1,0:T(8,128)(2,1)S(1)} %get-tuple-element.31.x), channel_id=1, source_target_pairs={{2,0},{3,1},{0,2},{1,3},{6,4},{7,5},{4,6},{5,7},{10,8},{11,9},{8,1... | collective-permute-start | bytes 196616 | tf_op jit(solution)/shard_map/ppermute | solution.py:282
  65.0 1.7 %collective-permute-start.8 = (bf16[16,2048]{1,0:T(8,128)(2,1)S(1)}, bf16[16,2048]{1,0:T(8,128)(2,1)S(1)}, u32[]{:S(2)}, u32[]{:S(2)}) collective-permute-start(bf16[16,2048]{1,0:T(8,128)(2,1)S(1)} %get-tuple-element.31.x), channel_id=1, source_target_pairs={{1,0},{2,1},{3,2},{0,3},{5,4},{6,5},{7,6},{4,7},{9,8},{10,9},{11,1... | collective-permute-start | bytes 196616 | tf_op jit(solution)/shard_map/ppermute | solution.py:282
  66.7 0.1 collective-permute-done.10.before
  66.8 2.0 %collective-permute-done.9.opposite = bf16[16,2048]{1,0:T(8,128)(2,1)S(1)} collective-permute-done((bf16[16,2048]{1,0:T(8,128)(2,1)S(1)}, bf16[16,2048]{1,0:T(8,128)(2,1)S(1)}, u32[]{:S(2)}, u32[]{:S(2)}) %collective-permute-start.9) | collective-permute-done | bytes 65568 | tf_op jit(solution)/shard_map/ppermute | solution.py:282
  68.8 0.4 collective-permute-done.8.after
  69.2 1.3 %shard_map.112 = bf16[16,8192]{1,0:T(8,128)(2,1)} custom-call(s32[2]{0:T(128)S(1)} %pad_add_fusion.who, bf16[16,2048]{1,0:T(8,128)(2,1)S(1)} %get-tuple-element.31.x, bf16[16,2048]{1,0:T(8,128)(2,1)S(1)} %collective-permute-done.8.after, bf16[16,2048]{1,0:T(8,128)(2,1)S(1)} %collective-permute-done.9.opposite, ...), custom_call_target="tpu_custom_call" | custom-call | bytes 1048576 | tf_op jit(solution)/shard_map/pallas_call | solution.py:39
  (18 shorter events, 0.1 us)
Async XLA Ops:
  0.6 7.1 %collective-permute-start = (bf16[8,16,8192]{2,1,0:T(8,128)(2,1)}, bf16[8,16,8192]{2,1,0:T(8,128)(2,1)S(1)}, u32[]{:S(2)}, u32[]{:S(2)}) collective-permute-start(bf16[8,16,8192]{2,1,0:T(8,128)(2,1)} %own.1), channel_id=1, source_target_pairs={{0,4},{4,0},{8,12},{12,8},{16,20},{20,16},{24,28},{28,24},{32,36},... | collective-permute-start | bytes 6291464 | tf_op jit(solution)/shard_map/ppermute | solution.py:236
  0.7 30.3 %collective-permute-start.1 = (bf16[8,16,8192]{2,1,0:T(8,128)(2,1)}, bf16[8,16,8192]{2,1,0:T(8,128)(2,1)}, u32[]{:S(2)}, u32[]{:S(2)}) collective-permute-start(bf16[8,16,8192]{2,1,0:T(8,128)(2,1)} %own.1), channel_id=1, source_target_pairs={{4,8},{12,16},{20,24},{28,32},{36,40},{44,48},{52,56},{60,64},{68,... | collective-permute-start | bytes 6291464 | tf_op jit(solution)/shard_map/ppermute | solution.py:235
  7.8 3.7 %copy-start = (bf16[2048,2304]{1,0:T(8,128)(2,1)S(1)}, bf16[2048,2304]{1,0:T(8,128)(2,1)}, u32[]{:S(2)}) copy-start(bf16[2048,2304]{1,0:T(8,128)(2,1)} %near.15) | copy-start | bytes 28311556
  11.5 3.4 %copy-start.2 = (bf16[256,128,128]{2,1,0:T(8,128)(2,1)S(1)}, bf16[256,128,128]{2,1,0:T(8,128)(2,1)}, u32[]{:S(2)}) copy-start(bf16[256,128,128]{2,1,0:T(8,128)(2,1)} %values.3) | copy-start | bytes 25165828
  14.8 1.6 %copy-start.3 = (bf16[8,16,8192]{2,1,0:T(8,128)(2,1)S(1)}, bf16[8,16,8192]{2,1,0:T(8,128)(2,1)}, u32[]{:S(2)}) copy-start(bf16[8,16,8192]{2,1,0:T(8,128)(2,1)} %own.1) | copy-start | bytes 6291460
  16.4 0.7 copy-start.6
  17.1 0.7 copy-start.7
  17.8 0.7 copy-start.8
  18.5 12.6 %copy-start.1 = (bf16[2048,2304]{1,0:T(8,128)(2,1)S(1)}, bf16[2048,2304]{1,0:T(8,128)(2,1)}, u32[]{:S(2)}) copy-start(bf16[2048,2304]{1,0:T(8,128)(2,1)} %near.15) | copy-start | bytes 28311556
  18.5 12.6 %copy-start.4 = (f32[16,2048]{1,0:T(8,128)S(1)}, f32[16,2048]{1,0:T(8,128)}, u32[]{:S(2)}) copy-start(f32[16,2048]{1,0:T(8,128)} %incident.1) | copy-start | bytes 393220
  18.5 12.6 %copy-start.5 = (f32[2048]{0:T(1024)S(1)}, f32[2048]{0:T(1024)}, u32[]{:S(2)}) copy-start(f32[2048]{0:T(1024)} %param.10) | copy-start | bytes 24580
  33.9 9.6 %collective-permute-start.2 = (bf16[16,128]{1,0:T(8,128)(2,1)S(1)}, bf16[16,128]{1,0:T(8,128)(2,1)S(1)}, u32[]{:S(2)}, u32[]{:S(2)}) collective-permute-start(bf16[16,128]{1,0:T(8,128)(2,1)S(1)} %get-tuple-element.20), channel_id=1, source_target_pairs={{4,8},{12,16},{20,24},{28,32},{36,40},{44,48},{52,56},{60,64},{68,... | collective-permute-start | bytes 12296 | tf_op jit(solution)/shard_map/ppermute | solution.py:260
  40.3 3.2 %collective-permute-start.3 = (bf16[16,128]{1,0:T(8,128)(2,1)S(1)}, bf16[16,128]{1,0:T(8,128)(2,1)S(1)}, u32[]{:S(2)}, u32[]{:S(2)}) collective-permute-start(bf16[16,128]{1,0:T(8,128)(2,1)S(1)} %get-tuple-element.21), channel_id=1, source_target_pairs={{0,4},{4,0},{8,12},{12,8},{16,20},{20,16},{24,28},{28,24},{32,36},... | collective-permute-start | bytes 12296 | tf_op jit(solution)/shard_map/ppermute | solution.py:261
  44.5 7.0 %collective-permute-start.4 = (bf16[16,128]{1,0:T(8,128)(2,1)S(1)}, bf16[16,128]{1,0:T(8,128)(2,1)S(1)}, u32[]{:S(2)}, u32[]{:S(2)}) collective-permute-start(bf16[16,128]{1,0:T(8,128)(2,1)S(1)} %get-tuple-element.24), channel_id=1, source_target_pairs={{4,8},{12,16},{20,24},{28,32},{36,40},{44,48},{52,56},{60,64},{68,... | collective-permute-start | bytes 12296 | tf_op jit(solution)/shard_map/ppermute | solution.py:260
  48.3 3.2 %collective-permute-start.5 = (bf16[16,128]{1,0:T(8,128)(2,1)S(1)}, bf16[16,128]{1,0:T(8,128)(2,1)S(1)}, u32[]{:S(2)}, u32[]{:S(2)}) collective-permute-start(bf16[16,128]{1,0:T(8,128)(2,1)S(1)} %get-tuple-element.25), channel_id=1, source_target_pairs={{0,4},{4,0},{8,12},{12,8},{16,20},{20,16},{24,28},{28,24},{32,36},... | collective-permute-start | bytes 12296 | tf_op jit(solution)/shard_map/ppermute | solution.py:261
  52.4 7.1 %collective-permute-start.6 = (bf16[16,128]{1,0:T(8,128)(2,1)S(1)}, bf16[16,128]{1,0:T(8,128)(2,1)S(1)}, u32[]{:S(2)}, u32[]{:S(2)}) collective-permute-start(bf16[16,128]{1,0:T(8,128)(2,1)S(1)} %get-tuple-element.27), channel_id=1, source_target_pairs={{4,8},{12,16},{20,24},{28,32},{36,40},{44,48},{52,56},{60,64},{68,... | collective-permute-start | bytes 12296 | tf_op jit(solution)/shard_map/ppermute | solution.py:260
  56.3 3.2 %collective-permute-start.7 = (bf16[16,128]{1,0:T(8,128)(2,1)S(1)}, bf16[16,128]{1,0:T(8,128)(2,1)S(1)}, u32[]{:S(2)}, u32[]{:S(2)}) collective-permute-start(bf16[16,128]{1,0:T(8,128)(2,1)S(1)} %get-tuple-element.28), channel_id=1, source_target_pairs={{0,4},{4,0},{8,12},{12,8},{16,20},{20,16},{24,28},{28,24},{32,36},... | collective-permute-start | bytes 12296 | tf_op jit(solution)/shard_map/ppermute | solution.py:261
  61.1 5.7 %collective-permute-start.10 = (bf16[16,2048]{1,0:T(8,128)(2,1)S(1)}, bf16[16,2048]{1,0:T(8,128)(2,1)S(1)}, u32[]{:S(2)}, u32[]{:S(2)}) collective-permute-start(bf16[16,2048]{1,0:T(8,128)(2,1)S(1)} %get-tuple-element.31.x), channel_id=1, source_target_pairs={{3,0},{0,1},{1,2},{2,3},{7,4},{4,5},{5,6},{6,7},{11,8},{8,9},{9,10... | collective-permute-start | bytes 196616 | tf_op jit(solution)/shard_map/ppermute | solution.py:282
  62.1 6.8 %collective-permute-start.9 = (bf16[16,2048]{1,0:T(8,128)(2,1)S(1)}, bf16[16,2048]{1,0:T(8,128)(2,1)S(1)}, u32[]{:S(2)}, u32[]{:S(2)}) collective-permute-start(bf16[16,2048]{1,0:T(8,128)(2,1)S(1)} %get-tuple-element.31.x), channel_id=1, source_target_pairs={{2,0},{3,1},{0,2},{1,3},{6,4},{7,5},{4,6},{5,7},{10,8},{11,9},{8,1... | collective-permute-start | bytes 196616 | tf_op jit(solution)/shard_map/ppermute | solution.py:282
  65.0 4.3 %collective-permute-start.8 = (bf16[16,2048]{1,0:T(8,128)(2,1)S(1)}, bf16[16,2048]{1,0:T(8,128)(2,1)S(1)}, u32[]{:S(2)}, u32[]{:S(2)}) collective-permute-start(bf16[16,2048]{1,0:T(8,128)(2,1)S(1)} %get-tuple-element.31.x), channel_id=1, source_target_pairs={{1,0},{2,1},{3,2},{0,3},{5,4},{6,5},{7,6},{4,7},{9,8},{10,9},{11,1... | collective-permute-start | bytes 196616 | tf_op jit(solution)/shard_map/ppermute | solution.py:282

commit v2 on v1

v2 whole, which is shorter than its diff:
```python
import jax
import jax.numpy as jnp
from jax import lax
from jax.experimental import pallas as pl
from jax.experimental.pallas import tpu as pltpu
from jax.sharding import PartitionSpec as P

BLK = 128
WAVES = 16
DELAYS = 8
SWEEPS = 4
RB = 16
SLOTS = 256
OWN = RB * BLK
EDGE = OWN + BLK
PATCH = 4 * OWN
COLS = PATCH // BLK
UNROLL = 32
ROWS = 256
NT = (((1,), (1,)), ((), ()))

VMEM = pl.BlockSpec(memory_space=pltpu.VMEM)
HBM = pl.BlockSpec(memory_space=pl.ANY)
SMEM = pl.BlockSpec(memory_space=pltpu.SMEM)


def f32(*shape):
    return jax.ShapeDtypeStruct(shape, jnp.float32)


def bf16(*shape):
    return jax.ShapeDtypeStruct(shape, jnp.bfloat16)


def in_vmem(x):
    return pltpu.with_memory_space_constraint(x, pltpu.VMEM)


def in_hbm(x):
    return pltpu.with_memory_space_constraint(x, pltpu.HBM)


def call(body, out, ins, outs, args, flops, touched, scratch=()):
    return pl.pallas_call(
        body,
        out_shape=out,
        in_specs=ins,
        out_specs=outs,
        scratch_shapes=scratch,
        compiler_params=pltpu.CompilerParams(vmem_limit_bytes=16 * 2**20),
        cost_estimate=pl.CostEstimate(flops=flops, bytes_accessed=touched, transcendentals=0),
    )(*args)


def add_slots(count, codes, values, acc, block_of):
    def step(i, carry):
        found = []
        for j in range(0, UNROLL, 2):
            pair = []
            for k in (j, j + 1):
                at = i * UNROLL + k
                code = codes[at]
                block = block_of(code)
                block = jnp.where(at < count, block, jnp.zeros_like(block))
                pair.append((code, block))
            (code_a, a), (code_b, b) = pair
            zero = jnp.zeros_like(a)
            left = jnp.concatenate(
                [jnp.concatenate([a, zero], axis=1), jnp.concatenate([zero, b], axis=1)], axis=0
            )
            right = jnp.concatenate([values[code_a & 255], values[code_b & 255]], axis=1)
            both = lax.dot_general(left, right, NT, preferred_element_type=jnp.float32)
            found.append((code_a, both[:WAVES]))
            found.append((code_b, both[WAVES:]))
        for code, part in found:
            row = (code >> 8) & 15
            acc[row] = acc[row] + part
        return carry

    lax.fori_loop(0, (count + UNROLL - 1) // UNROLL, step, 0)


def own_coupling(x, near, out):
    for at in range(0, OWN, ROWS):
        rows = near[at : at + ROWS, BLK:EDGE]
        out[:, at : at + ROWS] = lax.dot_general(x, rows, NT, preferred_element_type=jnp.float32)


def edge_coupling(parity, cross, near_side, near):
    left = jnp.where(parity == 0, cross, near_side)
    right = jnp.where(parity == 0, near_side, cross)
    both = jnp.concatenate([left, right], axis=1)
    out = []
    for at in range(0, OWN, ROWS):
        rows = jnp.concatenate(
            [near[at : at + ROWS, :BLK], near[at : at + ROWS, EDGE:]], axis=1
        )
        out.append(lax.dot_general(both, rows, NT, preferred_element_type=jnp.float32))
    return out


def home_body(codes, values, own, side, acc):
    acc[...] = jnp.zeros_like(acc)

    def block_of(code):
        delay = (code >> 12) & 7
        at = pl.multiple_of(((code >> 15) & 63) * BLK, BLK)
        return jnp.where(
            ((code >> 21) & 1) == 1,
            side[delay, :, pl.ds(at, BLK)],
            own[delay, :, pl.ds(at, BLK)],
        )

    add_slots(codes[0], _Shifted(codes), values, acc, block_of)


def sort_slots(span, parity, limit, counts, slot_row, slot_col, slot_delay, home_codes, far_codes):
    home, far = counts
    for s in span:
        col = slot_col[s]
        third = jnp.where(col >= 2 * COLS, 2, jnp.where(col >= COLS, 1, 0))
        is_far = third == 2 * parity
        code = (
            s
            | (slot_row[s] << 8)
            | (slot_delay[s] << 12)
            | ((col - third * COLS) << 15)
            | (jnp.where(third == 1, 0, 1) << 21)
        )
        home_codes[1 + home] = code
        far_codes[1 + far] = code
        alive = jnp.where(s < limit, 1, 0)
        passed = jnp.where(is_far, alive, 0)
        home, far = home + alive - passed, far + passed
    return home, far


def close_lists(counts, home_codes, far_codes):
    home, far = counts
    home_codes[0] = home
    far_codes[0] = far

    def clear(k, carry):
        home_codes[1 + home + k] = 0
        far_codes[1 + far + k] = 0
        return carry

    lax.fori_loop(0, UNROLL, clear, 0)


class _Shifted:
    def __init__(self, ref):
        self.ref = ref

    def __getitem__(self, at):
        return self.ref[at + 1]


def core_parity():
    return lax.rem(lax.axis_index("patch"), 2)


def lanes(at):
    return pl.ds(pl.multiple_of(at, BLK), BLK)


def places():
    parity = core_parity()
    return {
        "cross_cols": lanes(parity * EDGE),
        "side_cols": lanes((1 - parity) * EDGE),
        "outer": lanes(parity * (OWN - BLK)),
        "inner": lanes((1 - parity) * (OWN - BLK)),
    }


def chunks():
    return [slice(at, at + ROWS) for at in range(0, OWN, ROWS)]


def spans():
    return [pl.ds(at, ROWS) for at in range(0, OWN, ROWS)]


def nt(a, b):
    return lax.dot_general(a, b, NT, preferred_element_type=jnp.float32)


def nn(a, b):
    return jnp.dot(a, b, preferred_element_type=jnp.float32)


def response_1_body(
    live, row_hbm, col_hbm, delay_hbm, self_hbm, near_hbm, history,
    near, coupling, first, second, inner, inv, home_codes, far_codes,
    edge, newest, slot_row, slot_col, slot_delay, sems,
):
    parity, group = core_parity(), lax.axis_index("grp")
    at = places()
    start = pl.multiple_of(group * OWN, OWN)
    pairs = [
        (near_hbm.at[:, at["cross_cols"]], edge),
        (self_hbm, inv),
        (history.at[0, :, pl.ds(start, OWN)], newest),
        (row_hbm, slot_row),
        (col_hbm, slot_col),
        (delay_hbm, slot_delay),
    ] + [(near_hbm.at[rows], near.at[rows]) for rows in spans()]
    copies = [pltpu.make_async_copy(a, b, sems.at[i]) for i, (a, b) in enumerate(pairs)]
    for copy in copies:
        copy.start()
    eye = jnp.where(
        lax.broadcasted_iota(jnp.int32, (BLK, BLK), 0) == lax.broadcasted_iota(jnp.int32, (BLK, BLK), 1), 1.0, 0.0
    ).astype(jnp.bfloat16)
    copies[1].wait()
    inv[...] = 1.0 / inv[...]
    copies[0].wait()
    for rows in chunks():
        first[:, rows] = (-nt(eye, edge[rows]) * inv[:, rows]).astype(jnp.bfloat16)
    for copy in copies[2:6]:
        copy.wait()
    inner[...] = first[:, at["inner"]]
    limit = live[0]
    counts = (jnp.int32(0), jnp.int32(0))
    both = jnp.concatenate([first[...], newest[...]], axis=0)
    share = SLOTS // len(chunks())
    for i, (rows, copy) in enumerate(zip(chunks(), copies[6:])):
        copy.wait()
        counts = sort_slots(
            range(i * share, (i + 1) * share), parity, limit, counts,
            slot_row, slot_col, slot_delay, home_codes, far_codes,
        )
        made = nt(both, near[rows, BLK:EDGE])
        second[:, rows] = (-made[:BLK] * inv[:, rows]).astype(jnp.bfloat16)
        coupling[:, rows] = made[BLK:]
    close_lists(counts, home_codes, far_codes)


def response_2_body(near, inv, first, second, side, both, inner, corners):
    at = places()
    both[:BLK] = second[...]
    for rows in chunks():
        both[BLK:, rows] = (-nt(side[...], near[rows, at["side_cols"]]) * inv[:, rows]).astype(jnp.bfloat16)
    inner[...] = both[:, at["inner"]]
    corners[:BLK] = first[:, at["outer"]]
    corners[BLK:] = both[:, at["outer"]]


def response_3_body(near, inv, both, side, third):
    at = places()
    turned = jnp.concatenate([side[BLK:], side[:BLK]], axis=0)
    for rows in chunks():
        made = nt(both[...], near[rows, BLK:EDGE]) + nt(turned, near[rows, at["side_cols"]])
        third[:, rows] = (-made * inv[:, rows]).astype(jnp.bfloat16)


def second_body(
    codes, values, near, cross, side, acc, coupling, incident, inv, after,
    rhs, x_out, inner, total,
):
    parity, group = core_parity(), lax.axis_index("grp")
    total[...] = acc[...]

    def block_of(code):
        delay = (code >> 12) & 7
        at = pl.multiple_of(((code >> 15) & 63) * BLK, BLK)
        return cross[delay, :, pl.ds(at, BLK)]

    add_slots(codes[0], _Shifted(codes), values, total, block_of)
    for r in range(RB):
        at = slice(r * BLK, (r + 1) * BLK)
        rhs[:, at] = incident[:, at] - total[r]
    first = group * OWN
    last = group * OWN + OWN - BLK
    from_cross = cross[0, :, lanes(jnp.where(parity == 0, last, first))]
    from_side = side[0, :, lanes(jnp.where(parity == 0, first, last))]
    parts = edge_coupling(parity, from_cross, from_side, near)
    for rows, part in zip(chunks(), parts):
        x_out[:, rows] = ((rhs[:, rows] - (coupling[:, rows] + part)) * inv[:, rows]).astype(jnp.bfloat16)
    inner[...] = x_out[:, places()["inner"]]


def own_body(x, near, out):
    own_coupling(x[...], near, out)


def side_body(near, side, coupling, rhs, inv, y_out, inner):
    at = places()
    for rows in chunks():
        part = coupling[:, rows] + nt(side[...], near[rows, at["side_cols"]])
        y_out[:, rows] = ((rhs[:, rows] - part) * inv[:, rows]).astype(jnp.bfloat16)
    inner[...] = y_out[:, at["inner"]]


def early_body(near, x, y, side, rhs, inv, corners, near_by, far):
    at = places()
    rows = pl.ds(pl.multiple_of(core_parity() * (OWN - BLK), BLK), BLK)
    part = nt(y[...], near[rows, BLK:EDGE]) + nt(side[...], near[rows, at["side_cols"]])
    third = (rhs[:, at["outer"]] - part) * inv[:, at["outer"]]
    near_by[:WAVES] = x[:, at["outer"]]
    near_by[WAVES : 2 * WAVES] = y[:, at["outer"]]
    near_by[2 * WAVES : 3 * WAVES] = third.astype(jnp.bfloat16)
    near_by[3 * WAVES :] = corners[...]
    far[...] = x[:, at["outer"]]


def whole_body(near, x, side, rhs, inv, y_out, inner):
    at = places()
    for rows in chunks():
        part = nt(x[...], near[rows, BLK:EDGE]) + nt(side[...], near[rows, at["side_cols"]])
        y_out[:, rows] = ((rhs[:, rows] - part) * inv[:, rows]).astype(jnp.bfloat16)
    inner[...] = y_out[:, at["inner"]]


def edges_body(near_by, far, first, x, y, shared, third):
    at = places()
    one, mine = near_by[:WAVES], x[:, at["outer"]]
    mine_2 = y[:, at["outer"]].astype(jnp.float32) + nn(one, first[:, at["outer"]])
    corners = near_by[3 * WAVES :]
    two = near_by[WAVES : 2 * WAVES].astype(jnp.float32) + nn(mine, corners[:BLK])
    three = near_by[2 * WAVES : 3 * WAVES].astype(jnp.float32) + nn(mine, corners[BLK : 2 * BLK])
    three = three + nn(far[...], corners[2 * BLK :]) + nn(mine_2.astype(jnp.bfloat16), corners[:BLK])
    shared[:WAVES] = one
    shared[WAVES:] = two.astype(jnp.bfloat16)
    third[...] = three.astype(jnp.bfloat16)


def last_body(
    near, side, coupling, rhs, inv, mine, mine_3, other, first, both, third, current, x_out
):
    at = places()
    one = jnp.concatenate([mine[:WAVES], other[:WAVES]], axis=1)
    two = jnp.concatenate([mine[WAVES:], other[WAVES:]], axis=1)
    for rows in chunks():
        part = coupling[:, rows] + nt(side[...], near[rows, at["side_cols"]])
        y = (rhs[:, rows] - part) * inv[:, rows]
        x = y + (nn(one, third[:, rows]) + nn(two, both[:, rows]) + nn(mine_3[...], first[:, rows]))
        current[:, rows] = x
        x_out[:, rows] = x.astype(jnp.bfloat16)


def join_body(x, one, two, three, out):
    group = lax.axis_index("grp")
    for k, part in enumerate((x, one, two, three)):
        owner = group ^ k
        out[:, pl.ds(pl.multiple_of(owner * OWN, OWN), OWN)] = part[...]


def body(
    incident, self_term, near_field, history, ret_values, slot_row, slot_col, slot_delay, live_count
):
    count = lax.axis_size("patch")
    inv = self_term[None, :]
    chip = [(i, i ^ 1) for i in range(count)]
    links = [(i, i + 1) for i in range(1, count - 1, 2)]
    links = links + [(b, a) for a, b in links]
    beyond = [(i, i + 3) for i in range(1, count - 3, 2)]
    beyond = beyond + [(b, a) for a, b in beyond]
    product = 2 * OWN * OWN

    cross = lax.ppermute(history, "patch", links)
    side = lax.ppermute(history, "patch", chip)
    values = in_vmem(ret_values)
    codes = pltpu.SMEM((SLOTS + 2 * UNROLL,), jnp.int32)

    near, coupling, first, second, inner, inv, home_codes, far_codes = call(
        response_1_body,
        (pltpu.VMEM((OWN, EDGE + BLK), jnp.bfloat16), f32(WAVES, OWN), bf16(BLK, OWN), bf16(BLK, OWN),
         bf16(BLK, BLK), f32(1, OWN), codes, codes),
        [SMEM] + [HBM] * 6,
        (VMEM,) * 6 + (SMEM,) * 2,
        (live_count,) + tuple(in_hbm(x) for x in (slot_row, slot_col, slot_delay, inv, near_field, history)),
        product * 144,
        8 * 2**20,
        [
            pltpu.VMEM((OWN, BLK), jnp.bfloat16),
            pltpu.VMEM((WAVES, OWN), jnp.bfloat16),
            pltpu.SMEM((SLOTS,), jnp.int32),
            pltpu.SMEM((SLOTS,), jnp.int32),
            pltpu.SMEM((SLOTS,), jnp.int32),
            pltpu.SemaphoreType.DMA((6 + OWN // ROWS,)),
        ],
    )
    near = in_vmem(near)
    home_codes, far_codes = (pltpu.with_memory_space_constraint(x, pltpu.SMEM) for x in (home_codes, far_codes))
    both, inner, corners = call(
        response_2_body,
        (bf16(2 * BLK, OWN), bf16(2 * BLK, BLK), bf16(3 * BLK, BLK)),
        [VMEM] * 5,
        (VMEM,) * 3,
        (near, inv, first, second, lax.ppermute(inner, "patch", chip)),
        product * 16,
        2**20,
    )
    third = call(
        response_3_body,
        bf16(2 * BLK, OWN),
        [VMEM] * 4,
        VMEM,
        (near, inv, both, lax.ppermute(inner, "patch", chip)),
        product * 256,
        8 * 2**20,
    )
    acc = call(
        home_body,
        f32(RB, WAVES, BLK),
        [SMEM] + [VMEM] * 3,
        VMEM,
        (home_codes, values, in_vmem(history), in_vmem(side)),
        2 * 10**9,
        10 * 10**6,
    )
    rhs, x, inner = call(
        second_body,
        (f32(WAVES, OWN), bf16(WAVES, OWN), bf16(WAVES, BLK)),
        [SMEM] + [VMEM] * 8 + [HBM],
        (VMEM,) * 3,
        (far_codes, values, near, in_vmem(cross), in_vmem(side), acc, coupling, incident, inv, third),
        10**9,
        10**6,
        [pltpu.VMEM((RB, WAVES, BLK), jnp.float32)],
    )
    edge = lax.ppermute(inner, "patch", chip)
    coupling = call(own_body, f32(WAVES, OWN), [VMEM] * 2, VMEM, (x, near), product * 16, 8 * 2**20)
    y, inner = call(
        side_body,
        (bf16(WAVES, OWN), bf16(WAVES, BLK)),
        [VMEM] * 5,
        (VMEM,) * 2,
        (near, edge, coupling, rhs, inv),
        product,
        2**19,
    )
    edge = lax.ppermute(inner, "patch", chip)
    near_by, far = call(
        early_body,
        (bf16(3 * WAVES + 3 * BLK, BLK), bf16(WAVES, BLK)),
        [VMEM] * 7,
        (VMEM,) * 2,
        (near, x, y, edge, rhs, inv, corners),
        product,
        2**19,
    )
    near_by = lax.ppermute(near_by, "patch", links)
    far = lax.ppermute(far, "patch", beyond)
    y_3, inner = call(
        whole_body,
        (bf16(WAVES, OWN), bf16(WAVES, BLK)),
        [VMEM] * 5,
        (VMEM,) * 2,
        (near, y, edge, rhs, inv),
        product * 16,
        8 * 2**20,
    )
    edge = lax.ppermute(inner, "patch", chip)
    coupling = call(
        own_body, f32(WAVES, OWN), [VMEM] * 2, VMEM, (y_3, near), product * 16, 8 * 2**20
    )
    shared, mine_3 = call(
        edges_body,
        (bf16(2 * WAVES, BLK), bf16(WAVES, BLK)),
        [VMEM] * 5,
        (VMEM,) * 2,
        (near_by, far, first, x, y),
        product // 100,
        2**17,
    )
    other = lax.ppermute(shared, "patch", chip)
    current, x = call(
        last_body,
        (f32(WAVES, OWN), bf16(WAVES, OWN)),
        [VMEM] * 11,
        (VMEM,) * 2,
        (near, edge, coupling, rhs, inv, shared, mine_3, other, first, both, third),
        product * 4,
        2**21,
    )
    turns = [
        lax.ppermute(x, "grp", [(i, i ^ k) for i in range(4)]) for k in (1, 2, 3)
    ]
    newest = call(
        join_body, bf16(WAVES, PATCH), [VMEM] * 4, VMEM, (x, *turns), 0, 2**20
    )
    return current, newest


def solution(mesh):
    placed = (
        P(None, ("patch", "grp")),
        P(("patch", "grp")),
        P(("patch", "grp"), None),
        P(None, None, "patch"),
        P(("patch", "grp"), None, None),
        P(("patch", "grp")),
        P(("patch", "grp")),
        P(("patch", "grp")),
        P(("patch", "grp")),
    )
    return jax.shard_map(
        body,
        mesh=mesh,
        in_specs=placed,
        out_specs=(P(None, ("patch", "grp")), P(None, "patch")),
        check_vma=False,
    )
```

time: 71.3 us -> 63.8 us (0.89)
  waiting for transfers between devices: 4.77 us -> 18.5 us
  local copies, waits for them, and re-layouts: 10.7 us -> 0.02 us
  starting transfers between devices: 26.3 us -> 21.1 us
  Pallas kernels: 27.2 us -> 22.1 us
    unnamed x18 -> x8, local copies, waits for them, and re-layouts: 10.7 us -> 0.02 us
    ppermute x1, waiting for transfers between devices: 2.18 us -> 9.09 us  [body(): cross = lax.ppermute(history, 'patch', links)]
    ppermute x9 -> x11, waiting for transfers between devices: 2.59 us -> 9.4 us  [the longest x3 4.73 us: body(): lax.ppermute(x, 'grp', [(i, i ^ k) for i in range(4)])]
    ppermute x9 -> x11, starting transfers between devices: 19.9 us -> 14.7 us  [the longest x1 6.28 us: body(): near_by = lax.ppermute(near_by, 'patch', links)]
    pallas_call x9 -> x13, Pallas kernels: 27.2 us -> 22.1 us  [call(): pl.pallas_call(body, out_shape=out, in_specs=ins, out_specs=outs, scratch...]
  transfers between devices with their start and end apart: 11 -> 13, of which waited for: 4 -> 7; matrix products, arithmetic and copies ran while one was open for 0% -> 0% of each run, Pallas kernels for 28% -> 30%
where the time goes in v2:
time: 63.8 us; the launch traced here: 63.1 us
  Pallas kernels  22.1 us (35%)
  starting transfers between devices  21.1 us (33%)
  waiting for transfers between devices  18.5 us (29%)
  between operations  1.44 us (2%)
    pallas_call x13, Pallas kernels, call(): pl.pallas_call(body, out_shape=out, in_specs=ins, out_specs=outs, scratch...  22.1 us
    ppermute x1, waiting for transfers between devices, body(): cross = lax.ppermute(history, 'patch', links)  9.09 us
    ppermute x1, starting transfers between devices, body(): cross = lax.ppermute(history, 'patch', links)  6.3 us
    ppermute x1, starting transfers between devices, body(): near_by = lax.ppermute(near_by, 'patch', links)  6.28 us
    ppermute x3, waiting for transfers between devices, body(): lax.ppermute(x, 'grp', [(i, i ^ k) for i in range(4)])  4.73 us
    ppermute x3, starting transfers between devices, body(): lax.ppermute(x, 'grp', [(i, i ^ k) for i in range(4)])  4.09 us
    ppermute x1, starting transfers between devices, body(): far = lax.ppermute(far, 'patch', beyond)  3.32 us
    ppermute x2, waiting for transfers between devices, body(): lax.ppermute(inner, 'patch', chip)  2.29 us
  transfers between devices with their start and end apart: 13, of which 7 were waited for; matrix products, arithmetic and copies ran while one was open for 0% of the time, Pallas kernels for 30%

profile of v2, /device:TPU:6, one launch (start us, length us, event | category | flops | bytes accessed | tf_op | source)
XLA Modules:
  0.0 63.1 jit_solution(5701976075159091778)
XLA Ops:
  0.6 0.1 collective-permute-start.1
  0.7 6.3 %collective-permute-start = (bf16[8,16,8192]{2,1,0:T(8,128)(2,1)}, bf16[8,16,8192]{2,1,0:T(8,128)(2,1)S(1)}, u32[]{:S(2)}, u32[]{:S(2)}) collective-permute-start(bf16[8,16,8192]{2,1,0:T(8,128)(2,1)} %own.1), channel_id=1, source_target_pairs={{4,8},{12,16},{20,24},{28,32},{36,40},{44,48},{52,56},{60,64},{68,... | collective-permute-start | bytes 6291464 | tf_op jit(solution)/shard_map/ppermute | solution.py:361
  7.7 7.5 %shard_map.104 = (bf16[2048,2304]{1,0:T(8,128)(2,1)S(1)}, f32[16,2048]{1,0:T(8,128)S(1)}, bf16[128,2048]{1,0:T(8,128)(2,1)S(1)}, bf16[128,2048]{1,0:T(8,128)(2,1...) custom-call(s32[1]{0:T(128)S(6)} %copy.11.live, s32[256]{0:T(256)} %row_hbm.1, ...), custom_call_target="tpu_custom_call" | custom-call | flops 1207959552 | bytes 8388608 | tf_op jit(solution)/shard_map/pallas_call | solution.py:44
  15.2 0.1 collective-permute-start.2
  15.3 1.2 %collective-permute-done.2.side = bf16[128,128]{1,0:T(8,128)(2,1)S(1)} collective-permute-done((bf16[128,128]{1,0:T(8,128)(2,1)S(1)}, bf16[128,128]{1,0:T(8,128)(2,1)S(1)}, u32[]{:S(2)}, u32[]{:S(2)}) %collective-permute-start.2) | collective-permute-done | bytes 32800 | tf_op jit(solution)/shard_map/ppermute | solution.py:391
  16.5 0.3 shard_map.106
  16.8 0.2 collective-permute-start.3
  17.1 1.1 %collective-permute-done.3.side = bf16[256,128]{1,0:T(8,128)(2,1)S(1)} collective-permute-done((bf16[256,128]{1,0:T(8,128)(2,1)S(1)}, bf16[256,128]{1,0:T(8,128)(2,1)S(1)}, u32[]{:S(2)}, u32[]{:S(2)}) %collective-permute-start.3) | collective-permute-done | bytes 65568 | tf_op jit(solution)/shard_map/ppermute | solution.py:400
  18.2 2.6 %shard_map.107.after.third = bf16[256,2048]{1,0:T(8,128)(2,1)S(1)} custom-call(bf16[2048,2304]{1,0:T(8,128)(2,1)S(1)} %get-tuple-element.26.near, f32[1,2048]{1,0:T(1,128)S(1)} %get-tuple-element.30.inv, bf16[256,2048]{1,0:T(8,128)(2,1)S(1)} %get-tuple-element.34.both, bf16[256,128]{1,0:T(8,128)(2,1)S(1)} %collective-permute-done.3.side), custom_call_target="tpu_custom_call" | custom-call | flops 2147483648 | bytes 8388608 | tf_op jit(solution)/shard_map/pallas_call | solution.py:44
  20.9 1.0 %shard_map.105.acc = f32[16,16,128]{2,1,0:T(8,128)S(1)} custom-call(s32[320]{0:T(512)S(4)} %get-tuple-element.28.codes, bf16[256,128,128]{2,1,0:T(8,128)(2,1)S(1)} %bitcast.2, bf16[8,16,8192]{2,1,0:T(8,128)(2,1)S(1)} %copy-done, bf16[8,16,8192]{2,1,0:T(8,128)(2,1)S(1)} %collective-permute-done.1.side), custom_call_target="tpu_custom_call" | custom-call | flops 2000000000 | bytes 10000000 | tf_op jit(solution)/shard_map/pallas_call | solution.py:44
  21.9 9.1 %collective-permute-done.cross = bf16[8,16,8192]{2,1,0:T(8,128)(2,1)S(1)} collective-permute-done((bf16[8,16,8192]{2,1,0:T(8,128)(2,1)}, bf16[8,16,8192]{2,1,0:T(8,128)(2,1)S(1)}, u32[]{:S(2)}, u32[]{:S(2)}) %collective-permute-start) | collective-permute-done | bytes 2097184 | tf_op jit(solution)/shard_map/ppermute | solution.py:361
  31.0 0.9 %shard_map.108 = (f32[16,2048]{1,0:T(8,128)S(1)}, bf16[16,2048]{1,0:T(8,128)(2,1)S(1)}, bf16[16,128]{1,0:T(8,128)(2,1)S(1)}) custom-call(s32[320]{0:T(512)S(4)} %get-tuple-element.27.codes, bf16[256,128,128]{2,1,0:T(8,128)(2,1)S(1)} %bitcast.2, bf16[2048,2304]{1,0:T(8,128)(2,1)S(1)} %get-tuple-element.26.near, ...), custom_call_target="tpu_custom_call" | custom-call | flops 1000000000 | bytes 1000000 | tf_op jit(solution)/shard_map/pallas_call | solution.py:44
  31.8 0.1 collective-permute-start.4
  31.9 2.3 %shard_map.109.coupling = f32[16,2048]{1,0:T(8,128)S(1)} custom-call(bf16[16,2048]{1,0:T(8,128)(2,1)S(1)} %get-tuple-element.37.x, bf16[2048,2304]{1,0:T(8,128)(2,1)S(1)} %get-tuple-element.26.near), custom_call_target="tpu_custom_call" | custom-call | flops 134217728 | bytes 8388608 | tf_op jit(solution)/shard_map/pallas_call | solution.py:44
  34.2 0.3 shard_map.110
  34.4 0.6 collective-permute-start.5
  35.0 0.8 %collective-permute-done.5.side = bf16[16,128]{1,0:T(8,128)(2,1)S(1)} collective-permute-done((bf16[16,128]{1,0:T(8,128)(2,1)S(1)}, bf16[16,128]{1,0:T(8,128)(2,1)S(1)}, u32[]{:S(2)}, u32[]{:S(2)}) %collective-permute-start.5) | collective-permute-done | bytes 4128 | tf_op jit(solution)/shard_map/ppermute | solution.py:434
  35.8 0.2 shard_map.113
  36.1 6.3 %collective-permute-start.7 = (bf16[432,128]{1,0:T(8,128)(2,1)S(1)}, bf16[432,128]{1,0:T(8,128)(2,1)S(1)}, u32[]{:S(2)}, u32[]{:S(2)}) collective-permute-start(bf16[432,128]{1,0:T(8,128)(2,1)S(1)} %get-tuple-element.44), channel_id=1, source_target_pairs={{4,8},{12,16},{20,24},{28,32},{36,40},{44,48},{52,56},{60,64},{68,... | collective-permute-start | bytes 331784 | tf_op jit(solution)/shard_map/ppermute | solution.py:444
  42.4 3.3 %collective-permute-start.8 = (bf16[16,128]{1,0:T(8,128)(2,1)S(1)}, bf16[16,128]{1,0:T(8,128)(2,1)S(1)}, u32[]{:S(2)}, u32[]{:S(2)}) collective-permute-start(bf16[16,128]{1,0:T(8,128)(2,1)S(1)} %get-tuple-element.45), channel_id=1, source_target_pairs={{4,16},{12,24},{20,32},{28,40},{36,48},{44,56},{52,64},{60,72},{68... | collective-permute-start | bytes 12296 | tf_op jit(solution)/shard_map/ppermute | solution.py:445
  45.7 2.4 %shard_map.111 = (bf16[16,2048]{1,0:T(8,128)(2,1)S(1)}, bf16[16,128]{1,0:T(8,128)(2,1)S(1)}) custom-call(bf16[2048,2304]{1,0:T(8,128)(2,1)S(1)} %get-tuple-element.26.near, bf16[16,2048]{1,0:T(8,128)(2,1)S(1)} %get-tuple-element.39.x.y, bf16[16,128]{1,0:T(8,128)(2,1)S(1)} %collective-permute-done.5.side, f32[16,2048]{1,0:T(8,128)S(1)} %get-tuple-element.38.rhs, ...), custom_call_target="tpu_custom_call" | custom-call | flops 134217728 | bytes 8388608 | tf_op jit(solution)/shard_map/pallas_call | solution.py:44
  48.1 0.0 collective-permute-start.6
  48.1 1.6 %collective-permute-done.8.far = bf16[16,128]{1,0:T(8,128)(2,1)S(1)} collective-permute-done((bf16[16,128]{1,0:T(8,128)(2,1)S(1)}, bf16[16,128]{1,0:T(8,128)(2,1)S(1)}, u32[]{:S(2)}, u32[]{:S(2)}) %collective-permute-start.8) | collective-permute-done | bytes 4128 | tf_op jit(solution)/shard_map/ppermute | solution.py:445
  49.7 0.3 shard_map.114
  50.0 2.3 %shard_map.112.coupling = f32[16,2048]{1,0:T(8,128)S(1)} custom-call(bf16[16,2048]{1,0:T(8,128)(2,1)S(1)} %get-tuple-element.42.x, bf16[2048,2304]{1,0:T(8,128)(2,1)S(1)} %get-tuple-element.26.near), custom_call_target="tpu_custom_call" | custom-call | flops 134217728 | bytes 8388608 | tf_op jit(solution)/shard_map/pallas_call | solution.py:44
  52.2 1.3 %shard_map.115 = (f32[16,2048]{1,0:T(8,128)}, bf16[16,2048]{1,0:T(8,128)(2,1)S(1)}) custom-call(bf16[2048,2304]{1,0:T(8,128)(2,1)S(1)} %get-tuple-element.26.near, bf16[16,128]{1,0:T(8,128)(2,1)S(1)} %collective-permute-done.6.side, f32[16,2048]{1,0:T(8,128)S(1)} %shard_map.112.coupling, f32[16,2048]{1,0:T(8,128)S(1)} %get-tuple-element.38.rhs, ...), custom_call_target="tpu_custom_call" | custom-call | flops 33554432 | bytes 2097152 | tf_op jit(solution)/shard_map/pallas_call | solution.py:44
  53.5 2.5 %collective-permute-start.12 = (bf16[16,2048]{1,0:T(8,128)(2,1)S(1)}, bf16[16,2048]{1,0:T(8,128)(2,1)S(1)}, u32[]{:S(2)}, u32[]{:S(2)}) collective-permute-start(bf16[16,2048]{1,0:T(8,128)(2,1)S(1)} %get-tuple-element.49.x), channel_id=1, source_target_pairs={{0,3},{1,2},{2,1},{3,0},{4,7},{5,6},{6,5},{7,4},{8,11},{9,10},{10,... | collective-permute-start | bytes 196616 | tf_op jit(solution)/shard_map/ppermute | solution.py:479
  56.1 0.7 %collective-permute-start.11 = (bf16[16,2048]{1,0:T(8,128)(2,1)S(1)}, bf16[16,2048]{1,0:T(8,128)(2,1)S(1)}, u32[]{:S(2)}, u32[]{:S(2)}) collective-permute-start(bf16[16,2048]{1,0:T(8,128)(2,1)S(1)} %get-tuple-element.49.x), channel_id=1, source_target_pairs={{0,2},{1,3},{2,0},{3,1},{4,6},{5,7},{6,4},{7,5},{8,10},{9,11},{10,... | collective-permute-start | bytes 196616 | tf_op jit(solution)/shard_map/ppermute | solution.py:479
  56.7 0.9 %collective-permute-start.10 = (bf16[16,2048]{1,0:T(8,128)(2,1)S(1)}, bf16[16,2048]{1,0:T(8,128)(2,1)S(1)}, u32[]{:S(2)}, u32[]{:S(2)}) collective-permute-start(bf16[16,2048]{1,0:T(8,128)(2,1)S(1)} %get-tuple-element.49.x), channel_id=1, source_target_pairs={{0,1},{1,0},{2,3},{3,2},{4,5},{5,4},{6,7},{7,6},{8,9},{9,8},{10,11... | collective-permute-start | bytes 196616 | tf_op jit(solution)/shard_map/ppermute | solution.py:479
  57.6 1.9 %collective-permute-done.12.three = bf16[16,2048]{1,0:T(8,128)(2,1)S(1)} collective-permute-done((bf16[16,2048]{1,0:T(8,128)(2,1)S(1)}, bf16[16,2048]{1,0:T(8,128)(2,1)S(1)}, u32[]{:S(2)}, u32[]{:S(2)}) %collective-permute-start.12) | collective-permute-done | bytes 65568 | tf_op jit(solution)/shard_map/ppermute | solution.py:479
  59.5 2.8 %collective-permute-done.11.two = bf16[16,2048]{1,0:T(8,128)(2,1)S(1)} collective-permute-done((bf16[16,2048]{1,0:T(8,128)(2,1)S(1)}, bf16[16,2048]{1,0:T(8,128)(2,1)S(1)}, u32[]{:S(2)}, u32[]{:S(2)}) %collective-permute-start.11) | collective-permute-done | bytes 65568 | tf_op jit(solution)/shard_map/ppermute | solution.py:479
  62.3 0.7 %shard_map.116 = bf16[16,8192]{1,0:T(8,128)(2,1)} custom-call(bf16[16,2048]{1,0:T(8,128)(2,1)S(1)} %get-tuple-element.49.x, bf16[16,2048]{1,0:T(8,128)(2,1)S(1)} %collective-permute-done.10.one, bf16[16,2048]{1,0:T(8,128)(2,1)S(1)} %collective-permute-done.11.two, bf16[16,2048]{1,0:T(8,128)(2,1)S(1)} %collective-permute-done.12.three), custom_call_target="tpu_custom_call" | custom-call | bytes 1048576 | tf_op jit(solution)/shard_map/pallas_call | solution.py:44
  (16 shorter events, 0.0 us)
Async XLA Ops:
  0.6 20.2 %collective-permute-start.1 = (bf16[8,16,8192]{2,1,0:T(8,128)(2,1)}, bf16[8,16,8192]{2,1,0:T(8,128)(2,1)S(1)}, u32[]{:S(2)}, u32[]{:S(2)}) collective-permute-start(bf16[8,16,8192]{2,1,0:T(8,128)(2,1)} %own.1), channel_id=1, source_target_pairs={{0,4},{4,0},{8,12},{12,8},{16,20},{20,16},{24,28},{28,24},{32,36},... | collective-permute-start | bytes 6291464 | tf_op jit(solution)/shard_map/ppermute | solution.py:362
  0.7 30.2 %collective-permute-start = (bf16[8,16,8192]{2,1,0:T(8,128)(2,1)}, bf16[8,16,8192]{2,1,0:T(8,128)(2,1)S(1)}, u32[]{:S(2)}, u32[]{:S(2)}) collective-permute-start(bf16[8,16,8192]{2,1,0:T(8,128)(2,1)} %own.1), channel_id=1, source_target_pairs={{4,8},{12,16},{20,24},{28,32},{36,40},{44,48},{52,56},{60,64},{68,... | collective-permute-start | bytes 6291464 | tf_op jit(solution)/shard_map/ppermute | solution.py:361
  15.2 1.3 %collective-permute-start.2 = (bf16[128,128]{1,0:T(8,128)(2,1)S(1)}, bf16[128,128]{1,0:T(8,128)(2,1)S(1)}, u32[]{:S(2)}, u32[]{:S(2)}) collective-permute-start(bf16[128,128]{1,0:T(8,128)(2,1)S(1)} %get-tuple-element.33), channel_id=1, source_target_pairs={{0,4},{4,0},{8,12},{12,8},{16,20},{20,16},{24,28},{28,24},{32,36},... | collective-permute-start | bytes 98312 | tf_op jit(solution)/shard_map/ppermute | solution.py:391
  16.5 4.4 %slice-start = ((s8[8388608]{0:T(1024)(128)(4,1)}), s8[4194304]{0:T(1024)(128)(4,1)S(1)}, s32[]{:S(2)}) async-start(s8[8388608]{0:T(1024)(128)(4,1)} %bitcast.1), calls=%async_computation | async-start | bytes 8388608
  16.8 4.0 %copy-start = (bf16[8,16,8192]{2,1,0:T(8,128)(2,1)S(1)}, bf16[8,16,8192]{2,1,0:T(8,128)(2,1)}, u32[]{:S(2)}) copy-start(bf16[8,16,8192]{2,1,0:T(8,128)(2,1)} %own.1) | copy-start | bytes 6291460
  16.8 1.3 %collective-permute-start.3 = (bf16[256,128]{1,0:T(8,128)(2,1)S(1)}, bf16[256,128]{1,0:T(8,128)(2,1)S(1)}, u32[]{:S(2)}, u32[]{:S(2)}) collective-permute-start(bf16[256,128]{1,0:T(8,128)(2,1)S(1)} %get-tuple-element.35), channel_id=1, source_target_pairs={{0,4},{4,0},{8,12},{12,8},{16,20},{20,16},{24,28},{28,24},{32,36},... | collective-permute-start | bytes 196616 | tf_op jit(solution)/shard_map/ppermute | solution.py:400
  18.2 2.7 %slice-start.1 = ((s8[8388608]{0:T(1024)(128)(4,1)}), s8[4194304]{0:T(1024)(128)(4,1)S(1)}, s32[]{:S(2)}) async-start(s8[8388608]{0:T(1024)(128)(4,1)} %bitcast.1), calls=%async_computation.1 | async-start | bytes 8388608
  20.8 10.1 %copy-start.1 = (f32[16,2048]{1,0:T(8,128)S(1)}, f32[16,2048]{1,0:T(8,128)}, u32[]{:S(2)}) copy-start(f32[16,2048]{1,0:T(8,128)} %incident.1) | copy-start | bytes 393220
  31.8 2.3 %collective-permute-start.4 = (bf16[16,128]{1,0:T(8,128)(2,1)S(1)}, bf16[16,128]{1,0:T(8,128)(2,1)S(1)}, u32[]{:S(2)}, u32[]{:S(2)}) collective-permute-start(bf16[16,128]{1,0:T(8,128)(2,1)S(1)} %get-tuple-element.36), channel_id=1, source_target_pairs={{0,4},{4,0},{8,12},{12,8},{16,20},{20,16},{24,28},{28,24},{32,36},... | collective-permute-start | bytes 12296 | tf_op jit(solution)/shard_map/ppermute | solution.py:423
  34.4 1.4 %collective-permute-start.5 = (bf16[16,128]{1,0:T(8,128)(2,1)S(1)}, bf16[16,128]{1,0:T(8,128)(2,1)S(1)}, u32[]{:S(2)}, u32[]{:S(2)}) collective-permute-start(bf16[16,128]{1,0:T(8,128)(2,1)S(1)} %get-tuple-element.40), channel_id=1, source_target_pairs={{0,4},{4,0},{8,12},{12,8},{16,20},{20,16},{24,28},{28,24},{32,36},... | collective-permute-start | bytes 12296 | tf_op jit(solution)/shard_map/ppermute | solution.py:434
  36.1 13.6 %collective-permute-start.7 = (bf16[432,128]{1,0:T(8,128)(2,1)S(1)}, bf16[432,128]{1,0:T(8,128)(2,1)S(1)}, u32[]{:S(2)}, u32[]{:S(2)}) collective-permute-start(bf16[432,128]{1,0:T(8,128)(2,1)S(1)} %get-tuple-element.44), channel_id=1, source_target_pairs={{4,8},{12,16},{20,24},{28,32},{36,40},{44,48},{52,56},{60,64},{68,... | collective-permute-start | bytes 331784 | tf_op jit(solution)/shard_map/ppermute | solution.py:444
  42.4 7.3 %collective-permute-start.8 = (bf16[16,128]{1,0:T(8,128)(2,1)S(1)}, bf16[16,128]{1,0:T(8,128)(2,1)S(1)}, u32[]{:S(2)}, u32[]{:S(2)}) collective-permute-start(bf16[16,128]{1,0:T(8,128)(2,1)S(1)} %get-tuple-element.45), channel_id=1, source_target_pairs={{4,16},{12,24},{20,32},{28,40},{36,48},{44,56},{52,64},{60,72},{68... | collective-permute-start | bytes 12296 | tf_op jit(solution)/shard_map/ppermute | solution.py:445
  48.1 4.1 %collective-permute-start.6 = (bf16[16,128]{1,0:T(8,128)(2,1)S(1)}, bf16[16,128]{1,0:T(8,128)(2,1)S(1)}, u32[]{:S(2)}, u32[]{:S(2)}) collective-permute-start(bf16[16,128]{1,0:T(8,128)(2,1)S(1)} %get-tuple-element.41), channel_id=1, source_target_pairs={{0,4},{4,0},{8,12},{12,8},{16,20},{20,16},{24,28},{28,24},{32,36},... | collective-permute-start | bytes 12296 | tf_op jit(solution)/shard_map/ppermute | solution.py:455
  49.9 2.3 %collective-permute-start.9 = (bf16[32,128]{1,0:T(8,128)(2,1)S(1)}, bf16[32,128]{1,0:T(8,128)(2,1)S(1)}, u32[]{:S(2)}, u32[]{:S(2)}) collective-permute-start(bf16[32,128]{1,0:T(8,128)(2,1)S(1)} %get-tuple-element.46.mine), channel_id=1, source_target_pairs={{0,4},{4,0},{8,12},{12,8},{16,20},{20,16},{24,28},{28,24},{32,36},... | collective-permute-start | bytes 24584 | tf_op jit(solution)/shard_map/ppermute | solution.py:468
  53.5 6.0 %collective-permute-start.12 = (bf16[16,2048]{1,0:T(8,128)(2,1)S(1)}, bf16[16,2048]{1,0:T(8,128)(2,1)S(1)}, u32[]{:S(2)}, u32[]{:S(2)}) collective-permute-start(bf16[16,2048]{1,0:T(8,128)(2,1)S(1)} %get-tuple-element.49.x), channel_id=1, source_target_pairs={{0,3},{1,2},{2,1},{3,0},{4,7},{5,6},{6,5},{7,4},{8,11},{9,10},{10,... | collective-permute-start | bytes 196616 | tf_op jit(solution)/shard_map/ppermute | solution.py:479
  56.1 6.3 %collective-permute-start.11 = (bf16[16,2048]{1,0:T(8,128)(2,1)S(1)}, bf16[16,2048]{1,0:T(8,128)(2,1)S(1)}, u32[]{:S(2)}, u32[]{:S(2)}) collective-permute-start(bf16[16,2048]{1,0:T(8,128)(2,1)S(1)} %get-tuple-element.49.x), channel_id=1, source_target_pairs={{0,2},{1,3},{2,0},{3,1},{4,6},{5,7},{6,4},{7,5},{8,10},{9,11},{10,... | collective-permute-start | bytes 196616 | tf_op jit(solution)/shard_map/ppermute | solution.py:479
  56.7 5.6 %collective-permute-start.10 = (bf16[16,2048]{1,0:T(8,128)(2,1)S(1)}, bf16[16,2048]{1,0:T(8,128)(2,1)S(1)}, u32[]{:S(2)}, u32[]{:S(2)}) collective-permute-start(bf16[16,2048]{1,0:T(8,128)(2,1)S(1)} %get-tuple-element.49.x), channel_id=1, source_target_pairs={{0,1},{1,0},{2,3},{3,2},{4,5},{5,4},{6,7},{7,6},{8,9},{9,8},{10,11... | collective-permute-start | bytes 196616 | tf_op jit(solution)/shard_map/ppermute | solution.py:479

commit v3 on v2

--- a/solution.py
+++ b/solution.py
@@ -15,6 +15,7 @@
 EDGE = OWN + BLK
 PATCH = 4 * OWN
 COLS = PATCH // BLK
+HALF = OWN // 2
 UNROLL = 32
 ROWS = 256
 NT = (((1,), (1,)), ((), ()))
@@ -284,42 +285,39 @@
     own_coupling(x[...], near, out)
 
 
-def side_body(near, side, coupling, rhs, inv, y_out, inner):
+def side_body(near, side, coupling, rhs, inv, x, y_out, far):
     at = places()
     for rows in chunks():
         part = coupling[:, rows] + nt(side[...], near[rows, at["side_cols"]])
         y_out[:, rows] = ((rhs[:, rows] - part) * inv[:, rows]).astype(jnp.bfloat16)
-    inner[...] = y_out[:, at["inner"]]
-
-
-def early_body(near, x, y, side, rhs, inv, corners, near_by, far):
+    far[...] = x[:, pl.ds(pl.multiple_of(core_parity() * HALF, HALF), HALF)]
+
+
+def early_body(near, x, y, side, rhs, inv, near_by):
     at = places()
     rows = pl.ds(pl.multiple_of(core_parity() * (OWN - BLK), BLK), BLK)
-    part = nt(y[...], near[rows, BLK:EDGE]) + nt(side[...], near[rows, at["side_cols"]])
+    part = nt(y[...], near[rows, BLK:EDGE]) + nt(side[:, at["outer"]], near[rows, at["side_cols"]])
     third = (rhs[:, at["outer"]] - part) * inv[:, at["outer"]]
     near_by[:WAVES] = x[:, at["outer"]]
     near_by[WAVES : 2 * WAVES] = y[:, at["outer"]]
-    near_by[2 * WAVES : 3 * WAVES] = third.astype(jnp.bfloat16)
-    near_by[3 * WAVES :] = corners[...]
-    far[...] = x[:, at["outer"]]
+    near_by[2 * WAVES :] = third.astype(jnp.bfloat16)
 
 
 def whole_body(near, x, side, rhs, inv, y_out, inner):
     at = places()
     for rows in chunks():
-        part = nt(x[...], near[rows, BLK:EDGE]) + nt(side[...], near[rows, at["side_cols"]])
+        part = nt(x[...], near[rows, BLK:EDGE]) + nt(side[:, at["outer"]], near[rows, at["side_cols"]])
         y_out[:, rows] = ((rhs[:, rows] - part) * inv[:, rows]).astype(jnp.bfloat16)
     inner[...] = y_out[:, at["inner"]]
 
 
-def edges_body(near_by, far, first, x, y, shared, third):
+def edges_body(near_by, far, corners, first, x, y, shared, third):
     at = places()
     one, mine = near_by[:WAVES], x[:, at["outer"]]
     mine_2 = y[:, at["outer"]].astype(jnp.float32) + nn(one, first[:, at["outer"]])
-    corners = near_by[3 * WAVES :]
     two = near_by[WAVES : 2 * WAVES].astype(jnp.float32) + nn(mine, corners[:BLK])
-    three = near_by[2 * WAVES : 3 * WAVES].astype(jnp.float32) + nn(mine, corners[BLK : 2 * BLK])
-    three = three + nn(far[...], corners[2 * BLK :]) + nn(mine_2.astype(jnp.bfloat16), corners[:BLK])
+    three = near_by[2 * WAVES :].astype(jnp.float32) + nn(mine, corners[BLK : 2 * BLK])
+    three = three + nn(far[:, lanes((1 - core_parity()) * (HALF - BLK))], corners[2 * BLK :]) + nn(mine_2.astype(jnp.bfloat16), corners[:BLK])
     shared[:WAVES] = one
     shared[WAVES:] = two.astype(jnp.bfloat16)
     third[...] = three.astype(jnp.bfloat16)
@@ -339,9 +337,9 @@
         x_out[:, rows] = x.astype(jnp.bfloat16)
 
 
-def join_body(x, one, two, three, out):
+def join_body(x, one, three, two, out):
     group = lax.axis_index("grp")
-    for k, part in enumerate((x, one, two, three)):
+    for k, part in zip((0, 1, 3, 2), (x, one, three, two)):
         owner = group ^ k
         out[:, pl.ds(pl.multiple_of(owner * OWN, OWN), OWN)] = part[...]
 
@@ -392,6 +390,7 @@
         product * 16,
         2**20,
     )
+    corners = lax.ppermute(corners, "patch", links)
     third = call(
         response_3_body,
         bf16(2 * BLK, OWN),
@@ -422,27 +421,27 @@
     )
     edge = lax.ppermute(inner, "patch", chip)
     coupling = call(own_body, f32(WAVES, OWN), [VMEM] * 2, VMEM, (x, near), product * 16, 8 * 2**20)
-    y, inner = call(
+    y, far = call(
         side_body,
-        (bf16(WAVES, OWN), bf16(WAVES, BLK)),
-        [VMEM] * 5,
+        (bf16(WAVES, OWN), bf16(WAVES, HALF)),
+        [VMEM] * 6,
         (VMEM,) * 2,
-        (near, edge, coupling, rhs, inv),
+        (near, edge, coupling, rhs, inv, x),
         product,
         2**19,
     )
-    edge = lax.ppermute(inner, "patch", chip)
-    near_by, far = call(
+    edge = lax.ppermute(y, "patch", chip)
+    far = lax.ppermute(far, "patch", beyond)
+    near_by = call(
         early_body,
-        (bf16(3 * WAVES + 3 * BLK, BLK), bf16(WAVES, BLK)),
-        [VMEM] * 7,
-        (VMEM,) * 2,
-        (near, x, y, edge, rhs, inv, corners),
+        bf16(3 * WAVES, BLK),
+        [VMEM] * 6,
+        VMEM,
+        (near, x, y, edge, rhs, inv),
         product,
         2**19,
     )
     near_by = lax.ppermute(near_by, "patch", links)
-    far = lax.ppermute(far, "patch", beyond)
     y_3, inner = call(
         whole_body,
         (bf16(WAVES, OWN), bf16(WAVES, BLK)),
@@ -459,9 +458,9 @@
     shared, mine_3 = call(
         edges_body,
         (bf16(2 * WAVES, BLK), bf16(WAVES, BLK)),
-        [VMEM] * 5,
+        [VMEM] * 6,
         (VMEM,) * 2,
-        (near_by, far, first, x, y),
+        (near_by, far, corners, first, x, y),
         product // 100,
         2**17,
     )
@@ -476,7 +475,7 @@
         2**21,
     )
     turns = [
-        lax.ppermute(x, "grp", [(i, i ^ k) for i in range(4)]) for k in (1, 2, 3)
+        lax.ppermute(x, "grp", [(i, i ^ k) for i in range(4)]) for k in (1, 3, 2)
     ]
     newest = call(
         join_body, bf16(WAVES, PATCH), [VMEM] * 4, VMEM, (x, *turns), 0, 2**20

time: 63.8 us -> 60.6 us (0.950)
  waiting for transfers between devices: 18.5 us -> 12.8 us
  starting transfers between devices: 21.1 us -> 22.6 us
  Pallas kernels: 22.1 us -> 23.5 us
    ppermute x0 -> x2, starting transfers between devices: none -> 3.09 us  [the longest x1 2.52 us: body(): corners = lax.ppermute(corners, 'patch', links)]
    ppermute x1, starting transfers between devices: 6.28 us -> 3.75 us  [body(): near_by = lax.ppermute(near_by, 'patch', links)]
    ppermute x1, waiting for transfers between devices: 9.09 us -> 6.68 us  [body(): cross = lax.ppermute(history, 'patch', links)]
    ppermute x1, waiting for transfers between devices: 1.55 us -> 0.01 us  [body(): far = lax.ppermute(far, 'patch', beyond)]
    pallas_call x13, Pallas kernels: 22.1 us -> 23.5 us  [call(): pl.pallas_call(body, out_shape=out, in_specs=ins, out_specs=outs, scratch...]
    ppermute x2, waiting for transfers between devices: 2.29 us -> 1.2 us  [body(): lax.ppermute(inner, 'patch', chip)]
    ppermute x3 -> x2, waiting for transfers between devices: 0.83 us -> 0.01 us  [body(): edge = lax.ppermute(inner, 'patch', chip)]
  transfers between devices with their start and end apart: 13 -> 14, of which waited for: 7 -> 4; matrix products, arithmetic and copies ran while one was open for 0% -> 0% of each run, Pallas kernels for 30% -> 36%
where the time goes in v3:
time: 60.6 us; the launch traced here: 60.4 us
  Pallas kernels  23.5 us (39%)
  starting transfers between devices  22.6 us (37%)
  waiting for transfers between devices  12.8 us (21%)
  between operations  1.47 us (2%)
    pallas_call x13, Pallas kernels, call(): pl.pallas_call(body, out_shape=out, in_specs=ins, out_specs=outs, scratch...  23.5 us
    ppermute x1, waiting for transfers between devices, body(): cross = lax.ppermute(history, 'patch', links)  6.68 us
    ppermute x1, starting transfers between devices, body(): cross = lax.ppermute(history, 'patch', links)  6.3 us
    ppermute x3, waiting for transfers between devices, body(): lax.ppermute(x, 'grp', [(i, i ^ k) for i in range(4)])  4.9 us
    ppermute x3, starting transfers between devices, body(): lax.ppermute(x, 'grp', [(i, i ^ k) for i in range(4)])  4.51 us
    ppermute x1, starting transfers between devices, body(): near_by = lax.ppermute(near_by, 'patch', links)  3.75 us
    ppermute x1, starting transfers between devices, body(): far = lax.ppermute(far, 'patch', beyond)  3.49 us
    ppermute x1, starting transfers between devices, body(): corners = lax.ppermute(corners, 'patch', links)  2.52 us
  transfers between devices with their start and end apart: 14, of which 4 were waited for; matrix products, arithmetic and copies ran while one was open for 0% of the time, Pallas kernels for 36%

profile of v3, /device:TPU:6, one launch (start us, length us, event | category | flops | bytes accessed | tf_op | source)
XLA Modules:
  0.0 60.4 jit_solution(2631492544168625560)
XLA Ops:
  0.6 0.1 collective-permute-start.1
  0.7 6.3 %collective-permute-start = (bf16[8,16,8192]{2,1,0:T(8,128)(2,1)}, bf16[8,16,8192]{2,1,0:T(8,128)(2,1)S(1)}, u32[]{:S(2)}, u32[]{:S(2)}) collective-permute-start(bf16[8,16,8192]{2,1,0:T(8,128)(2,1)} %own.1), channel_id=1, source_target_pairs={{4,8},{12,16},{20,24},{28,32},{36,40},{44,48},{52,56},{60,64},{68,... | collective-permute-start | bytes 6291464 | tf_op jit(solution)/shard_map/ppermute | solution.py:359
  7.7 7.5 %shard_map.104 = (bf16[2048,2304]{1,0:T(8,128)(2,1)S(1)}, f32[16,2048]{1,0:T(8,128)S(1)}, bf16[128,2048]{1,0:T(8,128)(2,1)S(1)}, bf16[128,2048]{1,0:T(8,128)(2,1...) custom-call(s32[1]{0:T(128)S(6)} %copy.11.live, s32[256]{0:T(256)} %row_hbm.1, ...), custom_call_target="tpu_custom_call" | custom-call | flops 1207959552 | bytes 8388608 | tf_op jit(solution)/shard_map/pallas_call | solution.py:45
  15.2 0.1 collective-permute-start.2
  15.3 1.2 %collective-permute-done.2.side = bf16[128,128]{1,0:T(8,128)(2,1)S(1)} collective-permute-done((bf16[128,128]{1,0:T(8,128)(2,1)S(1)}, bf16[128,128]{1,0:T(8,128)(2,1)S(1)}, u32[]{:S(2)}, u32[]{:S(2)}) %collective-permute-start.2) | collective-permute-done | bytes 32800 | tf_op jit(solution)/shard_map/ppermute | solution.py:389
  16.5 0.3 shard_map.106
  16.8 0.2 collective-permute-start.3
  17.1 2.5 %collective-permute-start.9 = (bf16[384,128]{1,0:T(8,128)(2,1)S(1)}, bf16[384,128]{1,0:T(8,128)(2,1)S(1)}, u32[]{:S(2)}, u32[]{:S(2)}) collective-permute-start(bf16[384,128]{1,0:T(8,128)(2,1)S(1)} %get-tuple-element.41), channel_id=1, source_target_pairs={{4,8},{12,16},{20,24},{28,32},{36,40},{44,48},{52,56},{60,64},{68,... | collective-permute-start | bytes 294920 | tf_op jit(solution)/shard_map/ppermute | solution.py:393
  19.6 0.0 slice-start.1
  19.6 2.6 %shard_map.107.after.third = bf16[256,2048]{1,0:T(8,128)(2,1)S(1)} custom-call(bf16[2048,2304]{1,0:T(8,128)(2,1)S(1)} %get-tuple-element.24.near, f32[1,2048]{1,0:T(1,128)S(1)} %get-tuple-element.28.inv, bf16[256,2048]{1,0:T(8,128)(2,1)S(1)} %get-tuple-element.32.both, bf16[256,128]{1,0:T(8,128)(2,1)S(1)} %collective-permute-done.3.side), custom_call_target="tpu_custom_call" | custom-call | flops 2147483648 | bytes 8388608 | tf_op jit(solution)/shard_map/pallas_call | solution.py:45
  22.3 1.9 %shard_map.105.acc = f32[16,16,128]{2,1,0:T(8,128)S(1)} custom-call(s32[320]{0:T(512)S(4)} %get-tuple-element.26.codes, bf16[256,128,128]{2,1,0:T(8,128)(2,1)S(1)} %bitcast.2, bf16[8,16,8192]{2,1,0:T(8,128)(2,1)S(1)} %copy-done, bf16[8,16,8192]{2,1,0:T(8,128)(2,1)S(1)} %collective-permute-done.1.side), custom_call_target="tpu_custom_call" | custom-call | flops 2000000000 | bytes 10000000 | tf_op jit(solution)/shard_map/pallas_call | solution.py:45
  24.3 6.7 %collective-permute-done.cross = bf16[8,16,8192]{2,1,0:T(8,128)(2,1)S(1)} collective-permute-done((bf16[8,16,8192]{2,1,0:T(8,128)(2,1)}, bf16[8,16,8192]{2,1,0:T(8,128)(2,1)S(1)}, u32[]{:S(2)}, u32[]{:S(2)}) %collective-permute-start) | collective-permute-done | bytes 2097184 | tf_op jit(solution)/shard_map/ppermute | solution.py:359
  31.0 1.4 %shard_map.108 = (f32[16,2048]{1,0:T(8,128)S(1)}, bf16[16,2048]{1,0:T(8,128)(2,1)S(1)}, bf16[16,128]{1,0:T(8,128)(2,1)S(1)}) custom-call(s32[320]{0:T(512)S(4)} %get-tuple-element.25.codes, bf16[256,128,128]{2,1,0:T(8,128)(2,1)S(1)} %bitcast.2, bf16[2048,2304]{1,0:T(8,128)(2,1)S(1)} %get-tuple-element.24.near, ...), custom_call_target="tpu_custom_call" | custom-call | flops 1000000000 | bytes 1000000 | tf_op jit(solution)/shard_map/pallas_call | solution.py:45
  32.3 0.1 collective-permute-start.4
  32.4 2.3 %shard_map.109.coupling = f32[16,2048]{1,0:T(8,128)S(1)} custom-call(bf16[16,2048]{1,0:T(8,128)(2,1)S(1)} %get-tuple-element.35.x, bf16[2048,2304]{1,0:T(8,128)(2,1)S(1)} %get-tuple-element.24.near), custom_call_target="tpu_custom_call" | custom-call | flops 134217728 | bytes 8388608 | tf_op jit(solution)/shard_map/pallas_call | solution.py:45
  34.7 0.3 shard_map.110
  34.9 0.6 collective-permute-start.5
  35.5 3.5 %collective-permute-start.8 = (bf16[16,1024]{1,0:T(8,128)(2,1)S(1)}, bf16[16,1024]{1,0:T(8,128)(2,1)S(1)}, u32[]{:S(2)}, u32[]{:S(2)}) collective-permute-start(bf16[16,1024]{1,0:T(8,128)(2,1)S(1)} %get-tuple-element.40), channel_id=1, source_target_pairs={{4,16},{12,24},{20,32},{28,40},{36,48},{44,56},{52,64},{60,72},{68... | collective-permute-start | bytes 98312 | tf_op jit(solution)/shard_map/ppermute | solution.py:434
  39.0 0.2 shard_map.113
  39.2 3.7 %collective-permute-start.7 = (bf16[48,128]{1,0:T(8,128)(2,1)S(1)}, bf16[48,128]{1,0:T(8,128)(2,1)S(1)}, u32[]{:S(2)}, u32[]{:S(2)}) collective-permute-start(bf16[48,128]{1,0:T(8,128)(2,1)S(1)} %shard_map.113), channel_id=1, source_target_pairs={{4,8},{12,16},{20,24},{28,32},{36,40},{44,48},{52,56},{60,64},{68,... | collective-permute-start | bytes 36872 | tf_op jit(solution)/shard_map/ppermute | solution.py:444
  43.0 2.4 %shard_map.111 = (bf16[16,2048]{1,0:T(8,128)(2,1)S(1)}, bf16[16,128]{1,0:T(8,128)(2,1)S(1)}) custom-call(bf16[2048,2304]{1,0:T(8,128)(2,1)S(1)} %get-tuple-element.24.near, bf16[16,2048]{1,0:T(8,128)(2,1)S(1)} %get-tuple-element.37.x.y, bf16[16,2048]{1,0:T(8,128)(2,1)S(1)} %collective-permute-done.5.side, f32[16,2048]{1,0:T(8,128)S(1)} %get-tuple-element.36.rhs, ...), custom_call_target="tpu_custom_call" | custom-call | flops 134217728 | bytes 8388608 | tf_op jit(solution)/shard_map/pallas_call | solution.py:45
  45.4 1.0 %collective-permute-start.6 = (bf16[16,128]{1,0:T(8,128)(2,1)S(1)}, bf16[16,128]{1,0:T(8,128)(2,1)S(1)}, u32[]{:S(2)}, u32[]{:S(2)}) collective-permute-start(bf16[16,128]{1,0:T(8,128)(2,1)S(1)} %get-tuple-element.38), channel_id=1, source_target_pairs={{0,4},{4,0},{8,12},{12,8},{16,20},{20,16},{24,28},{28,24},{32,36},... | collective-permute-start | bytes 12296 | tf_op jit(solution)/shard_map/ppermute | solution.py:454
  46.4 0.0 collective-permute-done.7.near_by
  46.4 0.3 shard_map.114
  46.7 0.0 collective-permute-start.10
  46.7 2.3 %shard_map.112.coupling = f32[16,2048]{1,0:T(8,128)S(1)} custom-call(bf16[16,2048]{1,0:T(8,128)(2,1)S(1)} %get-tuple-element.39.x, bf16[2048,2304]{1,0:T(8,128)(2,1)S(1)} %get-tuple-element.24.near), custom_call_target="tpu_custom_call" | custom-call | flops 134217728 | bytes 8388608 | tf_op jit(solution)/shard_map/pallas_call | solution.py:45
  49.0 1.3 %shard_map.115 = (f32[16,2048]{1,0:T(8,128)}, bf16[16,2048]{1,0:T(8,128)(2,1)S(1)}) custom-call(bf16[2048,2304]{1,0:T(8,128)(2,1)S(1)} %get-tuple-element.24.near, bf16[16,128]{1,0:T(8,128)(2,1)S(1)} %collective-permute-done.6.side, f32[16,2048]{1,0:T(8,128)S(1)} %shard_map.112.coupling, f32[16,2048]{1,0:T(8,128)S(1)} %get-tuple-element.36.rhs, ...), custom_call_target="tpu_custom_call" | custom-call | flops 33554432 | bytes 2097152 | tf_op jit(solution)/shard_map/pallas_call | solution.py:45
  50.3 3.9 %collective-permute-start.13 = (bf16[16,2048]{1,0:T(8,128)(2,1)S(1)}, bf16[16,2048]{1,0:T(8,128)(2,1)S(1)}, u32[]{:S(2)}, u32[]{:S(2)}) collective-permute-start(bf16[16,2048]{1,0:T(8,128)(2,1)S(1)} %get-tuple-element.45.x), channel_id=1, source_target_pairs={{0,2},{1,3},{2,0},{3,1},{4,6},{5,7},{6,4},{7,5},{8,10},{9,11},{10,... | collective-permute-start | bytes 196616 | tf_op jit(solution)/shard_map/ppermute | solution.py:478
  54.2 0.6 collective-permute-start.12
  54.8 2.2 %collective-permute-done.13.two = bf16[16,2048]{1,0:T(8,128)(2,1)S(1)} collective-permute-done((bf16[16,2048]{1,0:T(8,128)(2,1)S(1)}, bf16[16,2048]{1,0:T(8,128)(2,1)S(1)}, u32[]{:S(2)}, u32[]{:S(2)}) %collective-permute-start.13) | collective-permute-done | bytes 65568 | tf_op jit(solution)/shard_map/ppermute | solution.py:478
  57.0 2.7 %collective-permute-done.12.three = bf16[16,2048]{1,0:T(8,128)(2,1)S(1)} collective-permute-done((bf16[16,2048]{1,0:T(8,128)(2,1)S(1)}, bf16[16,2048]{1,0:T(8,128)(2,1)S(1)}, u32[]{:S(2)}, u32[]{:S(2)}) %collective-permute-start.12) | collective-permute-done | bytes 65568 | tf_op jit(solution)/shard_map/ppermute | solution.py:478
  59.7 0.7 %shard_map.116 = bf16[16,8192]{1,0:T(8,128)(2,1)} custom-call(bf16[16,2048]{1,0:T(8,128)(2,1)S(1)} %get-tuple-element.45.x, bf16[16,2048]{1,0:T(8,128)(2,1)S(1)} %collective-permute-done.11.one, bf16[16,2048]{1,0:T(8,128)(2,1)S(1)} %collective-permute-done.12.three, bf16[16,2048]{1,0:T(8,128)(2,1)S(1)} %collective-permute-done.13.two), custom_call_target="tpu_custom_call" | custom-call | bytes 1048576 | tf_op jit(solution)/shard_map/pallas_call | solution.py:45
  (18 shorter events, 0.0 us)
Async XLA Ops:
  0.6 21.7 %collective-permute-start.1 = (bf16[8,16,8192]{2,1,0:T(8,128)(2,1)}, bf16[8,16,8192]{2,1,0:T(8,128)(2,1)S(1)}, u32[]{:S(2)}, u32[]{:S(2)}) collective-permute-start(bf16[8,16,8192]{2,1,0:T(8,128)(2,1)} %own.1), channel_id=1, source_target_pairs={{0,4},{4,0},{8,12},{12,8},{16,20},{20,16},{24,28},{28,24},{32,36},... | collective-permute-start | bytes 6291464 | tf_op jit(solution)/shard_map/ppermute | solution.py:360
  0.7 30.2 %collective-permute-start = (bf16[8,16,8192]{2,1,0:T(8,128)(2,1)}, bf16[8,16,8192]{2,1,0:T(8,128)(2,1)S(1)}, u32[]{:S(2)}, u32[]{:S(2)}) collective-permute-start(bf16[8,16,8192]{2,1,0:T(8,128)(2,1)} %own.1), channel_id=1, source_target_pairs={{4,8},{12,16},{20,24},{28,32},{36,40},{44,48},{52,56},{60,64},{68,... | collective-permute-start | bytes 6291464 | tf_op jit(solution)/shard_map/ppermute | solution.py:359
  15.2 1.3 %collective-permute-start.2 = (bf16[128,128]{1,0:T(8,128)(2,1)S(1)}, bf16[128,128]{1,0:T(8,128)(2,1)S(1)}, u32[]{:S(2)}, u32[]{:S(2)}) collective-permute-start(bf16[128,128]{1,0:T(8,128)(2,1)S(1)} %get-tuple-element.31), channel_id=1, source_target_pairs={{0,4},{4,0},{8,12},{12,8},{16,20},{20,16},{24,28},{28,24},{32,36},... | collective-permute-start | bytes 98312 | tf_op jit(solution)/shard_map/ppermute | solution.py:389
  16.5 5.8 %slice-start = ((s8[8388608]{0:T(1024)(128)(4,1)}), s8[4194304]{0:T(1024)(128)(4,1)S(1)}, s32[]{:S(2)}) async-start(s8[8388608]{0:T(1024)(128)(4,1)} %bitcast.1), calls=%async_computation | async-start | bytes 8388608
  16.8 5.5 %copy-start = (bf16[8,16,8192]{2,1,0:T(8,128)(2,1)S(1)}, bf16[8,16,8192]{2,1,0:T(8,128)(2,1)}, u32[]{:S(2)}) copy-start(bf16[8,16,8192]{2,1,0:T(8,128)(2,1)} %own.1) | copy-start | bytes 6291460
  16.8 2.8 %collective-permute-start.3 = (bf16[256,128]{1,0:T(8,128)(2,1)S(1)}, bf16[256,128]{1,0:T(8,128)(2,1)S(1)}, u32[]{:S(2)}, u32[]{:S(2)}) collective-permute-start(bf16[256,128]{1,0:T(8,128)(2,1)S(1)} %get-tuple-element.33), channel_id=1, source_target_pairs={{0,4},{4,0},{8,12},{12,8},{16,20},{20,16},{24,28},{28,24},{32,36},... | collective-permute-start | bytes 196616 | tf_op jit(solution)/shard_map/ppermute | solution.py:399
  17.1 29.3 %collective-permute-start.9 = (bf16[384,128]{1,0:T(8,128)(2,1)S(1)}, bf16[384,128]{1,0:T(8,128)(2,1)S(1)}, u32[]{:S(2)}, u32[]{:S(2)}) collective-permute-start(bf16[384,128]{1,0:T(8,128)(2,1)S(1)} %get-tuple-element.41), channel_id=1, source_target_pairs={{4,8},{12,16},{20,24},{28,32},{36,40},{44,48},{52,56},{60,64},{68,... | collective-permute-start | bytes 294920 | tf_op jit(solution)/shard_map/ppermute | solution.py:393
  19.6 2.7 %slice-start.1 = ((s8[8388608]{0:T(1024)(128)(4,1)}), s8[4194304]{0:T(1024)(128)(4,1)S(1)}, s32[]{:S(2)}) async-start(s8[8388608]{0:T(1024)(128)(4,1)} %bitcast.1), calls=%async_computation.1 | async-start | bytes 8388608
  22.3 8.7 %copy-start.1 = (f32[16,2048]{1,0:T(8,128)S(1)}, f32[16,2048]{1,0:T(8,128)}, u32[]{:S(2)}) copy-start(f32[16,2048]{1,0:T(8,128)} %incident.1) | copy-start | bytes 393220
  32.3 2.3 %collective-permute-start.4 = (bf16[16,128]{1,0:T(8,128)(2,1)S(1)}, bf16[16,128]{1,0:T(8,128)(2,1)S(1)}, u32[]{:S(2)}, u32[]{:S(2)}) collective-permute-start(bf16[16,128]{1,0:T(8,128)(2,1)S(1)} %get-tuple-element.34), channel_id=1, source_target_pairs={{0,4},{4,0},{8,12},{12,8},{16,20},{20,16},{24,28},{28,24},{32,36},... | collective-permute-start | bytes 12296 | tf_op jit(solution)/shard_map/ppermute | solution.py:422
  34.9 4.1 %collective-permute-start.5 = (bf16[16,2048]{1,0:T(8,128)(2,1)S(1)}, bf16[16,2048]{1,0:T(8,128)(2,1)S(1)}, u32[]{:S(2)}, u32[]{:S(2)}) collective-permute-start(bf16[16,2048]{1,0:T(8,128)(2,1)S(1)} %get-tuple-element.37.x.y), channel_id=1, source_target_pairs={{0,4},{4,0},{8,12},{12,8},{16,20},{20,16},{24,28},{28,24},{32,36},... | collective-permute-start | bytes 196616 | tf_op jit(solution)/shard_map/ppermute | solution.py:433
  35.5 10.9 %collective-permute-start.8 = (bf16[16,1024]{1,0:T(8,128)(2,1)S(1)}, bf16[16,1024]{1,0:T(8,128)(2,1)S(1)}, u32[]{:S(2)}, u32[]{:S(2)}) collective-permute-start(bf16[16,1024]{1,0:T(8,128)(2,1)S(1)} %get-tuple-element.40), channel_id=1, source_target_pairs={{4,16},{12,24},{20,32},{28,40},{36,48},{44,56},{52,64},{60,72},{68... | collective-permute-start | bytes 98312 | tf_op jit(solution)/shard_map/ppermute | solution.py:434
  39.2 7.2 %collective-permute-start.7 = (bf16[48,128]{1,0:T(8,128)(2,1)S(1)}, bf16[48,128]{1,0:T(8,128)(2,1)S(1)}, u32[]{:S(2)}, u32[]{:S(2)}) collective-permute-start(bf16[48,128]{1,0:T(8,128)(2,1)S(1)} %shard_map.113), channel_id=1, source_target_pairs={{4,8},{12,16},{20,24},{28,32},{36,40},{44,48},{52,56},{60,64},{68,... | collective-permute-start | bytes 36872 | tf_op jit(solution)/shard_map/ppermute | solution.py:444
  45.4 3.5 %collective-permute-start.6 = (bf16[16,128]{1,0:T(8,128)(2,1)S(1)}, bf16[16,128]{1,0:T(8,128)(2,1)S(1)}, u32[]{:S(2)}, u32[]{:S(2)}) collective-permute-start(bf16[16,128]{1,0:T(8,128)(2,1)S(1)} %get-tuple-element.38), channel_id=1, source_target_pairs={{0,4},{4,0},{8,12},{12,8},{16,20},{20,16},{24,28},{28,24},{32,36},... | collective-permute-start | bytes 12296 | tf_op jit(solution)/shard_map/ppermute | solution.py:454
  46.7 2.3 %collective-permute-start.10 = (bf16[32,128]{1,0:T(8,128)(2,1)S(1)}, bf16[32,128]{1,0:T(8,128)(2,1)S(1)}, u32[]{:S(2)}, u32[]{:S(2)}) collective-permute-start(bf16[32,128]{1,0:T(8,128)(2,1)S(1)} %get-tuple-element.42.mine), channel_id=1, source_target_pairs={{0,4},{4,0},{8,12},{12,8},{16,20},{20,16},{24,28},{28,24},{32,36},... | collective-permute-start | bytes 24584 | tf_op jit(solution)/shard_map/ppermute | solution.py:467
  50.3 6.7 %collective-permute-start.13 = (bf16[16,2048]{1,0:T(8,128)(2,1)S(1)}, bf16[16,2048]{1,0:T(8,128)(2,1)S(1)}, u32[]{:S(2)}, u32[]{:S(2)}) collective-permute-start(bf16[16,2048]{1,0:T(8,128)(2,1)S(1)} %get-tuple-element.45.x), channel_id=1, source_target_pairs={{0,2},{1,3},{2,0},{3,1},{4,6},{5,7},{6,4},{7,5},{8,10},{9,11},{10,... | collective-permute-start | bytes 196616 | tf_op jit(solution)/shard_map/ppermute | solution.py:478
  54.2 5.5 %collective-permute-start.12 = (bf16[16,2048]{1,0:T(8,128)(2,1)S(1)}, bf16[16,2048]{1,0:T(8,128)(2,1)S(1)}, u32[]{:S(2)}, u32[]{:S(2)}) collective-permute-start(bf16[16,2048]{1,0:T(8,128)(2,1)S(1)} %get-tuple-element.45.x), channel_id=1, source_target_pairs={{0,3},{1,2},{2,1},{3,0},{4,7},{5,6},{6,5},{7,4},{8,11},{9,10},{10,... | collective-permute-start | bytes 196616 | tf_op jit(solution)/shard_map/ppermute | solution.py:478
  54.8 4.9 %collective-permute-start.11 = (bf16[16,2048]{1,0:T(8,128)(2,1)S(1)}, bf16[16,2048]{1,0:T(8,128)(2,1)S(1)}, u32[]{:S(2)}, u32[]{:S(2)}) collective-permute-start(bf16[16,2048]{1,0:T(8,128)(2,1)S(1)} %get-tuple-element.45.x), channel_id=1, source_target_pairs={{0,1},{1,0},{2,3},{3,2},{4,5},{5,4},{6,7},{7,6},{8,9},{9,8},{10,11... | collective-permute-start | bytes 196616 | tf_op jit(solution)/shard_map/ppermute | solution.py:478

commit v4 on v3

--- a/solution.py
+++ b/solution.py
@@ -15,8 +15,8 @@
 EDGE = OWN + BLK
 PATCH = 4 * OWN
 COLS = PATCH // BLK
-HALF = OWN // 2
 UNROLL = 32
+DIRECT = 4
 ROWS = 256
 NT = (((1,), (1,)), ((), ()))
 
@@ -100,7 +100,7 @@
     return out
 
 
-def home_body(codes, values, own, side, acc):
+def home_body(codes, values, own, side, after, acc):
     acc[...] = jnp.zeros_like(acc)
 
     def block_of(code):
@@ -191,50 +191,51 @@
     return jnp.dot(a, b, preferred_element_type=jnp.float32)
 
 
-def response_1_body(
-    live, row_hbm, col_hbm, delay_hbm, self_hbm, near_hbm, history,
-    near, coupling, first, second, inner, inv, home_codes, far_codes,
-    edge, newest, slot_row, slot_col, slot_delay, sems,
+def lists_body(
+    live, row_hbm, col_hbm, delay_hbm, self_hbm, history, near_hbm,
+    near, inv, newest, home_codes, far_codes, slot_row, slot_col, slot_delay, sems,
 ):
-    parity, group = core_parity(), lax.axis_index("grp")
-    at = places()
-    start = pl.multiple_of(group * OWN, OWN)
+    start = pl.multiple_of(lax.axis_index("grp") * OWN, OWN)
     pairs = [
-        (near_hbm.at[:, at["cross_cols"]], edge),
-        (self_hbm, inv),
-        (history.at[0, :, pl.ds(start, OWN)], newest),
         (row_hbm, slot_row),
         (col_hbm, slot_col),
         (delay_hbm, slot_delay),
+        (self_hbm, inv),
+        (history.at[0, :, pl.ds(start, OWN)], newest),
     ] + [(near_hbm.at[rows], near.at[rows]) for rows in spans()]
     copies = [pltpu.make_async_copy(a, b, sems.at[i]) for i, (a, b) in enumerate(pairs)]
     for copy in copies:
         copy.start()
+    for copy in copies[:5]:
+        copy.wait()
+    inv[...] = 1.0 / inv[...]
+    parity, limit = core_parity(), live[0]
+
+    def some(i, counts):
+        return sort_slots(
+            [i * 16 + k for k in range(16)], parity, limit, counts,
+            slot_row, slot_col, slot_delay, home_codes, far_codes,
+        )
+
+    counts = lax.fori_loop(0, SLOTS // 16, some, (jnp.int32(0), jnp.int32(0)))
+    close_lists(counts, home_codes, far_codes)
+    for copy in copies[5:]:
+        copy.wait()
+
+
+def response_1_body(near, inv, newest, first, coupling, second, inner):
+    at = places()
     eye = jnp.where(
         lax.broadcasted_iota(jnp.int32, (BLK, BLK), 0) == lax.broadcasted_iota(jnp.int32, (BLK, BLK), 1), 1.0, 0.0
     ).astype(jnp.bfloat16)
-    copies[1].wait()
-    inv[...] = 1.0 / inv[...]
-    copies[0].wait()
-    for rows in chunks():
-        first[:, rows] = (-nt(eye, edge[rows]) * inv[:, rows]).astype(jnp.bfloat16)
-    for copy in copies[2:6]:
-        copy.wait()
+    for rows in chunks():
+        first[:, rows] = (-nt(eye, near[rows, at["cross_cols"]]) * inv[:, rows]).astype(jnp.bfloat16)
     inner[...] = first[:, at["inner"]]
-    limit = live[0]
-    counts = (jnp.int32(0), jnp.int32(0))
     both = jnp.concatenate([first[...], newest[...]], axis=0)
-    share = SLOTS // len(chunks())
-    for i, (rows, copy) in enumerate(zip(chunks(), copies[6:])):
-        copy.wait()
-        counts = sort_slots(
-            range(i * share, (i + 1) * share), parity, limit, counts,
-            slot_row, slot_col, slot_delay, home_codes, far_codes,
-        )
+    for rows in chunks():
         made = nt(both, near[rows, BLK:EDGE])
         second[:, rows] = (-made[:BLK] * inv[:, rows]).astype(jnp.bfloat16)
         coupling[:, rows] = made[BLK:]
-    close_lists(counts, home_codes, far_codes)
 
 
 def response_2_body(near, inv, first, second, side, both, inner, corners):
@@ -255,17 +256,32 @@
         third[:, rows] = (-made * inv[:, rows]).astype(jnp.bfloat16)
 
 
+def parts_body(history, half, direct, sems):
+    role = lax.rem(lax.axis_index("grp"), 2)
+    copies = [
+        pltpu.make_async_copy(history.at[pl.ds(DIRECT + 2 * role, 2)], half, sems.at[0]),
+        pltpu.make_async_copy(history.at[pl.ds(0, DIRECT)], direct, sems.at[1]),
+    ]
+    for copy in copies:
+        copy.start()
+    for copy in copies:
+        copy.wait()
+
+
 def second_body(
-    codes, values, near, cross, side, acc, coupling, incident, inv, after,
+    codes, values, near, cross, mine, other, side, acc, coupling, incident, inv, after,
     rhs, x_out, inner, total,
 ):
     parity, group = core_parity(), lax.axis_index("grp")
+    role = lax.rem(group, 2)
     total[...] = acc[...]
 
     def block_of(code):
         delay = (code >> 12) & 7
         at = pl.multiple_of(((code >> 15) & 63) * BLK, BLK)
-        return cross[delay, :, pl.ds(at, BLK)]
+        low, half = delay & 1, (delay >> 1) & 1
+        late = jnp.where(half == role, mine[low, :, pl.ds(at, BLK)], other[low, :, pl.ds(at, BLK)])
+        return jnp.where(delay < DIRECT, cross[delay & (DIRECT - 1), :, pl.ds(at, BLK)], late)
 
     add_slots(codes[0], _Shifted(codes), values, total, block_of)
     for r in range(RB):
@@ -290,49 +306,56 @@
     for rows in chunks():
         part = coupling[:, rows] + nt(side[...], near[rows, at["side_cols"]])
         y_out[:, rows] = ((rhs[:, rows] - part) * inv[:, rows]).astype(jnp.bfloat16)
-    far[...] = x[:, pl.ds(pl.multiple_of(core_parity() * HALF, HALF), HALF)]
-
-
-def early_body(near, x, y, side, rhs, inv, near_by):
+    far[:WAVES] = y_out[...]
+    far[WAVES:] = x[...]
+
+
+def early_body(near, x, y, side, rhs, inv, corners, near_by):
     at = places()
     rows = pl.ds(pl.multiple_of(core_parity() * (OWN - BLK), BLK), BLK)
-    part = nt(y[...], near[rows, BLK:EDGE]) + nt(side[:, at["outer"]], near[rows, at["side_cols"]])
+    part = nt(y[...], near[rows, BLK:EDGE]) + nt(side[:WAVES, at["outer"]], near[rows, at["side_cols"]])
     third = (rhs[:, at["outer"]] - part) * inv[:, at["outer"]]
     near_by[:WAVES] = x[:, at["outer"]]
     near_by[WAVES : 2 * WAVES] = y[:, at["outer"]]
-    near_by[2 * WAVES :] = third.astype(jnp.bfloat16)
+    near_by[2 * WAVES : 3 * WAVES] = third.astype(jnp.bfloat16)
+    near_by[3 * WAVES :] = corners[...]
 
 
 def whole_body(near, x, side, rhs, inv, y_out, inner):
     at = places()
     for rows in chunks():
-        part = nt(x[...], near[rows, BLK:EDGE]) + nt(side[:, at["outer"]], near[rows, at["side_cols"]])
+        part = nt(x[...], near[rows, BLK:EDGE]) + nt(side[:WAVES, at["outer"]], near[rows, at["side_cols"]])
         y_out[:, rows] = ((rhs[:, rows] - part) * inv[:, rows]).astype(jnp.bfloat16)
     inner[...] = y_out[:, at["inner"]]
 
 
-def edges_body(near_by, far, corners, first, x, y, shared, third):
+def edges_body(near_by, far, first, x, y, after, after_too, shared, third):
     at = places()
     one, mine = near_by[:WAVES], x[:, at["outer"]]
     mine_2 = y[:, at["outer"]].astype(jnp.float32) + nn(one, first[:, at["outer"]])
+    corners = near_by[3 * WAVES :]
     two = near_by[WAVES : 2 * WAVES].astype(jnp.float32) + nn(mine, corners[:BLK])
-    three = near_by[2 * WAVES :].astype(jnp.float32) + nn(mine, corners[BLK : 2 * BLK])
-    three = three + nn(far[:, lanes((1 - core_parity()) * (HALF - BLK))], corners[2 * BLK :]) + nn(mine_2.astype(jnp.bfloat16), corners[:BLK])
+    three = near_by[2 * WAVES : 3 * WAVES].astype(jnp.float32) + nn(mine, corners[BLK : 2 * BLK])
+    three = three + nn(far[WAVES:, at["inner"]], corners[2 * BLK :]) + nn(mine_2.astype(jnp.bfloat16), corners[:BLK])
     shared[:WAVES] = one
     shared[WAVES:] = two.astype(jnp.bfloat16)
     third[...] = three.astype(jnp.bfloat16)
 
 
-def last_body(
-    near, side, coupling, rhs, inv, mine, mine_3, other, first, both, third, current, x_out
-):
-    at = places()
-    one = jnp.concatenate([mine[:WAVES], other[:WAVES]], axis=1)
-    two = jnp.concatenate([mine[WAVES:], other[WAVES:]], axis=1)
+def own_part_body(near, side, coupling, rhs, inv, mine, mine_3, first, both, third, out):
+    at = places()
+    edges = jnp.concatenate([mine[:WAVES], mine[WAVES:]], axis=1)
     for rows in chunks():
         part = coupling[:, rows] + nt(side[...], near[rows, at["side_cols"]])
-        y = (rhs[:, rows] - part) * inv[:, rows]
-        x = y + (nn(one, third[:, rows]) + nn(two, both[:, rows]) + nn(mine_3[...], first[:, rows]))
+        response = jnp.concatenate([third[:BLK, rows], both[:BLK, rows]], axis=0)
+        out[:, rows] = (rhs[:, rows] - part) * inv[:, rows] + (nn(edges, response) + nn(mine_3[...], first[:, rows]))
+
+
+def last_body(partial, other, both, third, current, x_out):
+    edges = jnp.concatenate([other[:WAVES], other[WAVES:]], axis=1)
+    for rows in chunks():
+        response = jnp.concatenate([third[BLK:, rows], both[BLK:, rows]], axis=0)
+        x = partial[:, rows] + nn(edges, response)
         current[:, rows] = x
         x_out[:, rows] = x.astype(jnp.bfloat16)
 
@@ -356,31 +379,54 @@
     beyond = beyond + [(b, a) for a, b in beyond]
     product = 2 * OWN * OWN
 
-    cross = lax.ppermute(history, "patch", links)
+    pairs = [
+        (p * 4 + (g + p) % 4, p * 4 + ((g ^ 1) + p) % 4) for p in range(count) for g in range(4)
+    ]
+    half, direct = call(
+        parts_body,
+        (bf16(2, WAVES, PATCH), bf16(DIRECT, WAVES, PATCH)),
+        [HBM],
+        (HBM, HBM),
+        (in_hbm(history),),
+        1,
+        3 * 2**20,
+        [pltpu.SemaphoreType.DMA((2,))],
+    )
+    mine = lax.ppermute(half, "patch", links)
+    cross = lax.ppermute(direct, "patch", links)
     side = lax.ppermute(history, "patch", chip)
-    values = in_vmem(ret_values)
     codes = pltpu.SMEM((SLOTS + 2 * UNROLL,), jnp.int32)
 
-    near, coupling, first, second, inner, inv, home_codes, far_codes = call(
-        response_1_body,
-        (pltpu.VMEM((OWN, EDGE + BLK), jnp.bfloat16), f32(WAVES, OWN), bf16(BLK, OWN), bf16(BLK, OWN),
-         bf16(BLK, BLK), f32(1, OWN), codes, codes),
+    near, inv, newest, home_codes, far_codes = call(
+        lists_body,
+        (pltpu.VMEM((OWN, EDGE + BLK), jnp.bfloat16), f32(1, OWN), bf16(WAVES, OWN), codes, codes),
         [SMEM] + [HBM] * 6,
-        (VMEM,) * 6 + (SMEM,) * 2,
-        (live_count,) + tuple(in_hbm(x) for x in (slot_row, slot_col, slot_delay, inv, near_field, history)),
-        product * 144,
-        8 * 2**20,
+        (VMEM,) * 3 + (SMEM,) * 2,
+        (live_count,)
+        + tuple(in_hbm(x) for x in (slot_row, slot_col, slot_delay, inv, history, near_field)),
+        10**6,
+        12 * 10**6,
         [
-            pltpu.VMEM((OWN, BLK), jnp.bfloat16),
-            pltpu.VMEM((WAVES, OWN), jnp.bfloat16),
             pltpu.SMEM((SLOTS,), jnp.int32),
             pltpu.SMEM((SLOTS,), jnp.int32),
             pltpu.SMEM((SLOTS,), jnp.int32),
-            pltpu.SemaphoreType.DMA((6 + OWN // ROWS,)),
+            pltpu.SemaphoreType.DMA((5 + OWN // ROWS,)),
         ],
     )
     near = in_vmem(near)
+    mine, newest = lax.optimization_barrier((mine, newest))
+    other = lax.ppermute(mine, ("patch", "grp"), pairs)
     home_codes, far_codes = (pltpu.with_memory_space_constraint(x, pltpu.SMEM) for x in (home_codes, far_codes))
+    first, coupling, second, inner = call(
+        response_1_body,
+        (bf16(BLK, OWN), f32(WAVES, OWN), bf16(BLK, OWN), bf16(BLK, BLK)),
+        [VMEM] * 3,
+        (VMEM,) * 4,
+        (near, inv, newest),
+        product * 144,
+        12 * 10**6,
+    )
+    values, own = in_vmem(ret_values), in_vmem(history)
     both, inner, corners = call(
         response_2_body,
         (bf16(2 * BLK, OWN), bf16(2 * BLK, BLK), bf16(3 * BLK, BLK)),
@@ -390,7 +436,6 @@
         product * 16,
         2**20,
     )
-    corners = lax.ppermute(corners, "patch", links)
     third = call(
         response_3_body,
         bf16(2 * BLK, OWN),
@@ -403,18 +448,18 @@
     acc = call(
         home_body,
         f32(RB, WAVES, BLK),
-        [SMEM] + [VMEM] * 3,
+        [SMEM] + [VMEM] * 3 + [HBM],
         VMEM,
-        (home_codes, values, in_vmem(history), in_vmem(side)),
+        (home_codes, values, own, in_vmem(side), third),
         2 * 10**9,
         10 * 10**6,
     )
     rhs, x, inner = call(
         second_body,
         (f32(WAVES, OWN), bf16(WAVES, OWN), bf16(WAVES, BLK)),
-        [SMEM] + [VMEM] * 8 + [HBM],
+        [SMEM] + [VMEM] * 10 + [HBM],
         (VMEM,) * 3,
-        (far_codes, values, near, in_vmem(cross), in_vmem(side), acc, coupling, incident, inv, third),
+        (far_codes, values, near, in_vmem(cross), in_vmem(mine), in_vmem(other), in_vmem(side), acc, coupling, incident, inv, third),
         10**9,
         10**6,
         [pltpu.VMEM((RB, WAVES, BLK), jnp.float32)],
@@ -423,21 +468,21 @@
     coupling = call(own_body, f32(WAVES, OWN), [VMEM] * 2, VMEM, (x, near), product * 16, 8 * 2**20)
     y, far = call(
         side_body,
-        (bf16(WAVES, OWN), bf16(WAVES, HALF)),
+        (bf16(WAVES, OWN), bf16(2 * WAVES, OWN)),
         [VMEM] * 6,
         (VMEM,) * 2,
         (near, edge, coupling, rhs, inv, x),
         product,
         2**19,
     )
-    edge = lax.ppermute(y, "patch", chip)
+    edge = lax.ppermute(far, "patch", chip)
     far = lax.ppermute(far, "patch", beyond)
     near_by = call(
         early_body,
-        bf16(3 * WAVES, BLK),
-        [VMEM] * 6,
+        bf16(3 * WAVES + 3 * BLK, BLK),
+        [VMEM] * 7,
         VMEM,
-        (near, x, y, edge, rhs, inv),
+        (near, x, y, edge, rhs, inv, corners),
         product,
         2**19,
     )
@@ -458,21 +503,30 @@
     shared, mine_3 = call(
         edges_body,
         (bf16(2 * WAVES, BLK), bf16(WAVES, BLK)),
-        [VMEM] * 6,
+        [VMEM] * 5 + [HBM] * 2,
         (VMEM,) * 2,
-        (near_by, far, corners, first, x, y),
+        (near_by, far, first, x, y, coupling, edge),
         product // 100,
         2**17,
     )
     other = lax.ppermute(shared, "patch", chip)
+    partial = call(
+        own_part_body,
+        f32(WAVES, OWN),
+        [VMEM] * 10,
+        VMEM,
+        (near, edge, coupling, rhs, inv, shared, mine_3, first, both, third),
+        product * 3,
+        2**21,
+    )
     current, x = call(
         last_body,
         (f32(WAVES, OWN), bf16(WAVES, OWN)),
-        [VMEM] * 11,
+        [VMEM] * 4,
         (VMEM,) * 2,
-        (near, edge, coupling, rhs, inv, shared, mine_3, other, first, both, third),
-        product * 4,
-        2**21,
+        (partial, other, both, third),
+        product * 2,
+        2**20,
     )
     turns = [
         lax.ppermute(x, "grp", [(i, i ^ k) for i in range(4)]) for k in (1, 3, 2)

time: 60.6 us -> 57.9 us (0.955); the launches traced: 60.4 us -> 57.1 us
  waiting for transfers between devices: 12.8 us -> 7.41 us
  Pallas kernels: 23.5 us -> 25.4 us
    ppermute x3 -> x4, waiting for transfers between devices: 6.68 us -> 0.39 us  [the longest x1 0.39 us: body(): mine = lax.ppermute(half, 'patch', links)]
    pallas_call x13 -> x16, Pallas kernels: 23.5 us -> 25.4 us  [call(): pl.pallas_call(body, out_shape=out, in_specs=ins, out_specs=outs, scratch...]
    ppermute x2, waiting for transfers between devices: 1.2 us -> 2.29 us  [body(): lax.ppermute(inner, 'patch', chip)]
    ppermute x3, starting transfers between devices: 4.51 us -> 3.49 us  [body(): lax.ppermute(x, 'grp', [(i, i ^ k) for i in range(4)])]
    ppermute x1, starting transfers between devices: 3.49 us -> 4.47 us  [body(): far = lax.ppermute(far, 'patch', beyond)]
    ppermute x1, starting transfers between devices: 3.75 us -> 2.83 us  [body(): near_by = lax.ppermute(near_by, 'patch', links)]
    ppermute x3, waiting for transfers between devices: 4.9 us -> 4.03 us  [body(): lax.ppermute(x, 'grp', [(i, i ^ k) for i in range(4)])]
    ppermute x1, waiting for transfers between devices: 0.01 us -> 0.69 us  [body(): other = lax.ppermute(shared, 'patch', chip)]
  transfers between devices with their start and end apart: 14 -> 15, of which waited for: 4 -> 6; matrix products, arithmetic and copies ran while one was open for 0% -> 0% of each run, Pallas kernels for 36% -> 37%
where the time goes in v4:
time: 57.9 us; the launch traced here: 57.1 us
  Pallas kernels  25.4 us (44%)
  starting transfers between devices  22.8 us (39%)
  waiting for transfers between devices  7.41 us (13%)
  between operations  1.48 us (3%)
    pallas_call x16, Pallas kernels, call(): pl.pallas_call(body, out_shape=out, in_specs=ins, out_specs=outs, scratch...  25.4 us
    ppermute x1, starting transfers between devices, body(): mine = lax.ppermute(half, 'patch', links)  6.3 us
    ppermute x1, starting transfers between devices, body(): far = lax.ppermute(far, 'patch', beyond)  4.47 us
    ppermute x3, waiting for transfers between devices, body(): lax.ppermute(x, 'grp', [(i, i ^ k) for i in range(4)])  4.03 us
    ppermute x3, starting transfers between devices, body(): lax.ppermute(x, 'grp', [(i, i ^ k) for i in range(4)])  3.49 us
    ppermute x1, starting transfers between devices, body(): near_by = lax.ppermute(near_by, 'patch', links)  2.83 us
    ppermute x2, waiting for transfers between devices, body(): lax.ppermute(inner, 'patch', chip)  2.29 us
    ppermute x1, starting transfers between devices, body(): cross = lax.ppermute(direct, 'patch', links)  1.92 us
  transfers between devices with their start and end apart: 15, of which 6 were waited for; matrix products, arithmetic and copies ran while one was open for 0% of the time, Pallas kernels for 37%

profile of v4, /device:TPU:6, one launch (start us, length us, event | category | flops | bytes accessed | tf_op | source)
XLA Modules:
  0.0 57.1 jit_solution(1166523687221911453)
XLA Ops:
  0.7 1.4 %shard_map.105 = (bf16[2,16,8192]{2,1,0:T(8,128)(2,1)S(1)}, bf16[4,16,8192]{2,1,0:T(8,128)(2,1)S(1)}) custom-call(bf16[8,16,8192]{2,1,0:T(8,128)(2,1)} %own.1), custom_call_target="tpu_custom_call" | custom-call | flops 1 | bytes 3145728 | tf_op jit(solution)/shard_map/pallas_call | solution.py:45
  2.1 6.3 %collective-permute-start.1 = (bf16[2,16,8192]{2,1,0:T(8,128)(2,1)S(1)}, bf16[2,16,8192]{2,1,0:T(8,128)(2,1)S(1)}, u32[]{:S(2)}, u32[]{:S(2)}) collective-permute-start(bf16[2,16,8192]{2,1,0:T(8,128)(2,1)S(1)} %get-tuple-element.32), channel_id=1, source_target_pairs={{4,8},{12,16},{20,24},{28,32},{36,40},{44,48},{52,56},{60,64},{68,... | collective-permute-start | bytes 1572872 | tf_op jit(solution)/shard_map/ppermute | solution.py:395
  8.5 1.9 %collective-permute-start = (bf16[4,16,8192]{2,1,0:T(8,128)(2,1)S(1)}, bf16[4,16,8192]{2,1,0:T(8,128)(2,1)S(1)}, u32[]{:S(2)}, u32[]{:S(2)}) collective-permute-start(bf16[4,16,8192]{2,1,0:T(8,128)(2,1)S(1)} %get-tuple-element.31), channel_id=1, source_target_pairs={{4,8},{12,16},{20,24},{28,32},{36,40},{44,48},{52,56},{60,64},{68,... | collective-permute-start | bytes 3145736 | tf_op jit(solution)/shard_map/ppermute | solution.py:396
  11.0 3.9 %shard_map.104 = (bf16[2048,2304]{1,0:T(8,128)(2,1)S(1)}, f32[1,2048]{1,0:T(1,128)S(1)}, bf16[16,2048]{1,0:T(8,128)(2,1)S(1)}, s32[320]{0:T(512)S(4)}, s32[320]{0:T(512)S(4)}) custom-call(s32[1]{0:T(128)S(6)} %copy.11.live, s32[256]{0:T(256)} %row_hbm.1, s32[256]{0:T(256)} %col_hbm.1, s32[256]{0:T(256)} %delay_hbm.1, f32[1,2048]{1,0:T(1,128)} %bitcast.3, ...), custom_call_target="tpu_custom_call" | custom-call | flops 1000000 | bytes 12000000 | tf_op jit(solution)/shard_map/pallas_call | solution.py:45
  14.9 0.4 collective-permute-done.1.mine
  15.3 1.6 %collective-permute-start.2 = (bf16[2,16,8192]{2,1,0:T(8,128)(2,1)S(1)}, bf16[2,16,8192]{2,1,0:T(8,128)(2,1)S(1)}, u32[]{:S(2)}, u32[]{:S(2)}) collective-permute-start(bf16[2,16,8192]{2,1,0:T(8,128)(2,1)S(1)} %collective-permute-done.1.mine), channel_id=1, source_target_pairs={{0,1},{1,0},{2,3},{3,2},{5,6},{6,5},{7,4},{4,7},{10,11},{11,10},{8... | collective-permute-start | bytes 1572872 | tf_op jit(solution)/shard_map/ppermute | solution.py:418
  16.9 3.0 %shard_map.106 = (bf16[128,2048]{1,0:T(8,128)(2,1)S(1)}, f32[16,2048]{1,0:T(8,128)S(1)}, bf16[128,2048]{1,0:T(8,128)(2,1)S(1)}, bf16[128,128]{1,0:T(8,128)(2,1)S(1)}) custom-call(bf16[2048,2304]{1,0:T(8,128)(2,1)S(1)} %get-tuple-element.29.near, f32[1,2048]{1,0:T(1,128)S(1)} %get-tuple-element.36.inv, bf16[16,2048]{1,0:T(8,128)(2,1)S(1)} %get-tuple-element.37.newest), custom_call_target="tpu_custom_call" | custom-call | flops 1207959552 | bytes 12000000 | tf_op jit(solution)/shard_map/pallas_call | solution.py:45
  20.0 1.2 %collective-permute-done.4.side = bf16[128,128]{1,0:T(8,128)(2,1)S(1)} collective-permute-done((bf16[128,128]{1,0:T(8,128)(2,1)S(1)}, bf16[128,128]{1,0:T(8,128)(2,1)S(1)}, u32[]{:S(2)}, u32[]{:S(2)}) %collective-permute-start.4) | collective-permute-done | bytes 32800 | tf_op jit(solution)/shard_map/ppermute | solution.py:435
  21.2 0.3 shard_map.107
  21.8 1.1 %collective-permute-done.5.side = bf16[256,128]{1,0:T(8,128)(2,1)S(1)} collective-permute-done((bf16[256,128]{1,0:T(8,128)(2,1)S(1)}, bf16[256,128]{1,0:T(8,128)(2,1)S(1)}, u32[]{:S(2)}, u32[]{:S(2)}) %collective-permute-start.5) | collective-permute-done | bytes 65568 | tf_op jit(solution)/shard_map/ppermute | solution.py:444
  22.9 2.6 %shard_map.108.after.third = bf16[256,2048]{1,0:T(8,128)(2,1)S(1)} custom-call(bf16[2048,2304]{1,0:T(8,128)(2,1)S(1)} %get-tuple-element.29.near, f32[1,2048]{1,0:T(1,128)S(1)} %get-tuple-element.36.inv, bf16[256,2048]{1,0:T(8,128)(2,1)S(1)} %get-tuple-element.41.both, bf16[256,128]{1,0:T(8,128)(2,1)S(1)} %collective-permute-done.5.side), custom_call_target="tpu_custom_call" | custom-call | flops 2147483648 | bytes 8388608 | tf_op jit(solution)/shard_map/pallas_call | solution.py:45
  25.6 2.4 %shard_map.109.acc = f32[16,16,128]{2,1,0:T(8,128)S(1)} custom-call(s32[320]{0:T(512)S(4)} %get-tuple-element.35.codes, bf16[256,128,128]{2,1,0:T(8,128)(2,1)S(1)} %bitcast.2, bf16[8,16,8192]{2,1,0:T(8,128)(2,1)S(1)} %copy-done, bf16[8,16,8192]{2,1,0:T(8,128)(2,1)S(1)} %collective-permute-done.3.side, bf16[256,2048]{1,0:T(8,128)(2,1)S(1)} %shard_map.108.after.third), custom_call_target="tpu_custom_call" | custom-call | flops 2000000000 | bytes 10000000 | tf_op jit(solution)/shard_map/pallas_call | solution.py:45
  28.1 1.8 %shard_map.110 = (f32[16,2048]{1,0:T(8,128)S(1)}, bf16[16,2048]{1,0:T(8,128)(2,1)S(1)}, bf16[16,128]{1,0:T(8,128)(2,1)S(1)}) custom-call(s32[320]{0:T(512)S(4)} %get-tuple-element.30.codes, bf16[256,128,128]{2,1,0:T(8,128)(2,1)S(1)} %bitcast.2, bf16[2048,2304]{1,0:T(8,128)(2,1)S(1)} %get-tuple-element.29.near, ...), custom_call_target="tpu_custom_call" | custom-call | flops 1000000000 | bytes 1000000 | tf_op jit(solution)/shard_map/pallas_call | solution.py:45
  29.9 0.7 %collective-permute-start.6 = (bf16[16,128]{1,0:T(8,128)(2,1)S(1)}, bf16[16,128]{1,0:T(8,128)(2,1)S(1)}, u32[]{:S(2)}, u32[]{:S(2)}) collective-permute-start(bf16[16,128]{1,0:T(8,128)(2,1)S(1)} %get-tuple-element.44), channel_id=1, source_target_pairs={{0,4},{4,0},{8,12},{12,8},{16,20},{20,16},{24,28},{28,24},{32,36},... | collective-permute-start | bytes 12296 | tf_op jit(solution)/shard_map/ppermute | solution.py:467
  30.6 2.3 %shard_map.111.coupling = f32[16,2048]{1,0:T(8,128)S(1)} custom-call(bf16[16,2048]{1,0:T(8,128)(2,1)S(1)} %get-tuple-element.45.x, bf16[2048,2304]{1,0:T(8,128)(2,1)S(1)} %get-tuple-element.29.near), custom_call_target="tpu_custom_call" | custom-call | flops 134217728 | bytes 8388608 | tf_op jit(solution)/shard_map/pallas_call | solution.py:45
  32.8 0.3 shard_map.112
  33.2 4.5 %collective-permute-start.10 = (bf16[32,2048]{1,0:T(8,128)(2,1)S(1)}, bf16[32,2048]{1,0:T(8,128)(2,1)S(1)}, u32[]{:S(2)}, u32[]{:S(2)}) collective-permute-start(bf16[32,2048]{1,0:T(8,128)(2,1)S(1)} %get-tuple-element.48), channel_id=1, source_target_pairs={{4,16},{12,24},{20,32},{28,40},{36,48},{44,56},{52,64},{60,72},{68... | collective-permute-start | bytes 393224 | tf_op jit(solution)/shard_map/ppermute | solution.py:479
  37.7 0.2 shard_map.115
  37.9 2.8 %collective-permute-start.9 = (bf16[432,128]{1,0:T(8,128)(2,1)S(1)}, bf16[432,128]{1,0:T(8,128)(2,1)S(1)}, u32[]{:S(2)}, u32[]{:S(2)}) collective-permute-start(bf16[432,128]{1,0:T(8,128)(2,1)S(1)} %shard_map.115), channel_id=1, source_target_pairs={{4,8},{12,16},{20,24},{28,32},{36,40},{44,48},{52,56},{60,64},{68,... | collective-permute-start | bytes 331784 | tf_op jit(solution)/shard_map/ppermute | solution.py:489
  40.8 2.4 %shard_map.113 = (bf16[16,2048]{1,0:T(8,128)(2,1)S(1)}, bf16[16,128]{1,0:T(8,128)(2,1)S(1)}) custom-call(bf16[2048,2304]{1,0:T(8,128)(2,1)S(1)} %get-tuple-element.29.near, bf16[16,2048]{1,0:T(8,128)(2,1)S(1)} %get-tuple-element.47.x.y, bf16[32,2048]{1,0:T(8,128)(2,1)S(1)} %collective-permute-done.7.side, f32[16,2048]{1,0:T(8,128)S(1)} %get-tuple-element.46.rhs, ...), custom_call_target="tpu_custom_call" | custom-call | flops 134217728 | bytes 8388608 | tf_op jit(solution)/shard_map/pallas_call | solution.py:45
  43.2 1.0 %collective-permute-start.8 = (bf16[16,128]{1,0:T(8,128)(2,1)S(1)}, bf16[16,128]{1,0:T(8,128)(2,1)S(1)}, u32[]{:S(2)}, u32[]{:S(2)}) collective-permute-start(bf16[16,128]{1,0:T(8,128)(2,1)S(1)} %get-tuple-element.49), channel_id=1, source_target_pairs={{0,4},{4,0},{8,12},{12,8},{16,20},{20,16},{24,28},{28,24},{32,36},... | collective-permute-start | bytes 12296 | tf_op jit(solution)/shard_map/ppermute | solution.py:499
  44.2 2.3 %shard_map.114.after.coupling = f32[16,2048]{1,0:T(8,128)S(1)} custom-call(bf16[16,2048]{1,0:T(8,128)(2,1)S(1)} %get-tuple-element.50.x, bf16[2048,2304]{1,0:T(8,128)(2,1)S(1)} %get-tuple-element.29.near), custom_call_target="tpu_custom_call" | custom-call | flops 134217728 | bytes 8388608 | tf_op jit(solution)/shard_map/pallas_call | solution.py:45
  46.5 0.3 shard_map.116
  46.7 0.5 shard_map.117.partial
  47.2 0.7 %collective-permute-done.11.other = bf16[32,128]{1,0:T(8,128)(2,1)S(1)} collective-permute-done((bf16[32,128]{1,0:T(8,128)(2,1)S(1)}, bf16[32,128]{1,0:T(8,128)(2,1)S(1)}, u32[]{:S(2)}, u32[]{:S(2)}) %collective-permute-start.11) | collective-permute-done | bytes 8224 | tf_op jit(solution)/shard_map/ppermute | solution.py:512
  47.9 0.9 %shard_map.118 = (f32[16,2048]{1,0:T(8,128)}, bf16[16,2048]{1,0:T(8,128)(2,1)S(1)}) custom-call(f32[16,2048]{1,0:T(8,128)S(1)} %shard_map.117.partial, bf16[32,128]{1,0:T(8,128)(2,1)S(1)} %collective-permute-done.11.other, bf16[256,2048]{1,0:T(8,128)(2,1)S(1)} %get-tuple-element.41.both, bf16[256,2048]{1,0:T(8,128)(2,1)S(1)} %shard_map.108.after.third), custom_call_target="tpu_custom_call" | custom-call | flops 16777216 | bytes 1048576 | tf_op jit(solution)/shard_map/pallas_call | solution.py:45
  48.8 2.0 %collective-permute-start.14 = (bf16[16,2048]{1,0:T(8,128)(2,1)S(1)}, bf16[16,2048]{1,0:T(8,128)(2,1)S(1)}, u32[]{:S(2)}, u32[]{:S(2)}) collective-permute-start(bf16[16,2048]{1,0:T(8,128)(2,1)S(1)} %get-tuple-element.55.x), channel_id=1, source_target_pairs={{0,2},{1,3},{2,0},{3,1},{4,6},{5,7},{6,4},{7,5},{8,10},{9,11},{10,... | collective-permute-start | bytes 196616 | tf_op jit(solution)/shard_map/ppermute | solution.py:532
  50.9 0.5 collective-permute-start.13
  51.4 0.9 %collective-permute-start.12 = (bf16[16,2048]{1,0:T(8,128)(2,1)S(1)}, bf16[16,2048]{1,0:T(8,128)(2,1)S(1)}, u32[]{:S(2)}, u32[]{:S(2)}) collective-permute-start(bf16[16,2048]{1,0:T(8,128)(2,1)S(1)} %get-tuple-element.55.x), channel_id=1, source_target_pairs={{0,1},{1,0},{2,3},{3,2},{4,5},{5,4},{6,7},{7,6},{8,9},{9,8},{10,11... | collective-permute-start | bytes 196616 | tf_op jit(solution)/shard_map/ppermute | solution.py:532
  52.3 2.3 %collective-permute-done.14.two = bf16[16,2048]{1,0:T(8,128)(2,1)S(1)} collective-permute-done((bf16[16,2048]{1,0:T(8,128)(2,1)S(1)}, bf16[16,2048]{1,0:T(8,128)(2,1)S(1)}, u32[]{:S(2)}, u32[]{:S(2)}) %collective-permute-start.14) | collective-permute-done | bytes 65568 | tf_op jit(solution)/shard_map/ppermute | solution.py:532
  54.6 1.7 %collective-permute-done.13.three = bf16[16,2048]{1,0:T(8,128)(2,1)S(1)} collective-permute-done((bf16[16,2048]{1,0:T(8,128)(2,1)S(1)}, bf16[16,2048]{1,0:T(8,128)(2,1)S(1)}, u32[]{:S(2)}, u32[]{:S(2)}) %collective-permute-start.13) | collective-permute-done | bytes 65568 | tf_op jit(solution)/shard_map/ppermute | solution.py:532
  56.3 0.7 %shard_map.119 = bf16[16,8192]{1,0:T(8,128)(2,1)} custom-call(bf16[16,2048]{1,0:T(8,128)(2,1)S(1)} %get-tuple-element.55.x, bf16[16,2048]{1,0:T(8,128)(2,1)S(1)} %collective-permute-done.12.one, bf16[16,2048]{1,0:T(8,128)(2,1)S(1)} %collective-permute-done.13.three, bf16[16,2048]{1,0:T(8,128)(2,1)S(1)} %collective-permute-done.14.two), custom_call_target="tpu_custom_call" | custom-call | bytes 1048576 | tf_op jit(solution)/shard_map/pallas_call | solution.py:45
  (23 shorter events, 0.6 us)
Async XLA Ops:
  0.6 25.0 %collective-permute-start.3 = (bf16[8,16,8192]{2,1,0:T(8,128)(2,1)}, bf16[8,16,8192]{2,1,0:T(8,128)(2,1)S(1)}, u32[]{:S(2)}, u32[]{:S(2)}) collective-permute-start(bf16[8,16,8192]{2,1,0:T(8,128)(2,1)} %own.1), channel_id=1, source_target_pairs={{0,4},{4,0},{8,12},{12,8},{16,20},{20,16},{24,28},{28,24},{32,36},... | collective-permute-start | bytes 6291464 | tf_op jit(solution)/shard_map/ppermute | solution.py:397
  2.1 13.2 %collective-permute-start.1 = (bf16[2,16,8192]{2,1,0:T(8,128)(2,1)S(1)}, bf16[2,16,8192]{2,1,0:T(8,128)(2,1)S(1)}, u32[]{:S(2)}, u32[]{:S(2)}) collective-permute-start(bf16[2,16,8192]{2,1,0:T(8,128)(2,1)S(1)} %get-tuple-element.32), channel_id=1, source_target_pairs={{4,8},{12,16},{20,24},{28,32},{36,40},{44,48},{52,56},{60,64},{68,... | collective-permute-start | bytes 1572872 | tf_op jit(solution)/shard_map/ppermute | solution.py:395
  8.5 19.6 %collective-permute-start = (bf16[4,16,8192]{2,1,0:T(8,128)(2,1)S(1)}, bf16[4,16,8192]{2,1,0:T(8,128)(2,1)S(1)}, u32[]{:S(2)}, u32[]{:S(2)}) collective-permute-start(bf16[4,16,8192]{2,1,0:T(8,128)(2,1)S(1)} %get-tuple-element.31), channel_id=1, source_target_pairs={{4,8},{12,16},{20,24},{28,32},{36,40},{44,48},{52,56},{60,64},{68,... | collective-permute-start | bytes 3145736 | tf_op jit(solution)/shard_map/ppermute | solution.py:396
  15.3 12.7 %collective-permute-start.2 = (bf16[2,16,8192]{2,1,0:T(8,128)(2,1)S(1)}, bf16[2,16,8192]{2,1,0:T(8,128)(2,1)S(1)}, u32[]{:S(2)}, u32[]{:S(2)}) collective-permute-start(bf16[2,16,8192]{2,1,0:T(8,128)(2,1)S(1)} %collective-permute-done.1.mine), channel_id=1, source_target_pairs={{0,1},{1,0},{2,3},{3,2},{5,6},{6,5},{7,4},{4,7},{10,11},{11,10},{8... | collective-permute-start | bytes 1572872 | tf_op jit(solution)/shard_map/ppermute | solution.py:418
  19.9 1.3 %collective-permute-start.4 = (bf16[128,128]{1,0:T(8,128)(2,1)S(1)}, bf16[128,128]{1,0:T(8,128)(2,1)S(1)}, u32[]{:S(2)}, u32[]{:S(2)}) collective-permute-start(bf16[128,128]{1,0:T(8,128)(2,1)S(1)} %get-tuple-element.40), channel_id=1, source_target_pairs={{0,4},{4,0},{8,12},{12,8},{16,20},{20,16},{24,28},{28,24},{32,36},... | collective-permute-start | bytes 98312 | tf_op jit(solution)/shard_map/ppermute | solution.py:435
  21.2 4.4 %slice-start = ((s8[8388608]{0:T(1024)(128)(4,1)}), s8[4194304]{0:T(1024)(128)(4,1)S(1)}, s32[]{:S(2)}) async-start(s8[8388608]{0:T(1024)(128)(4,1)} %bitcast.1), calls=%async_computation | async-start | bytes 8388608
  21.6 4.0 %copy-start = (bf16[8,16,8192]{2,1,0:T(8,128)(2,1)S(1)}, bf16[8,16,8192]{2,1,0:T(8,128)(2,1)}, u32[]{:S(2)}) copy-start(bf16[8,16,8192]{2,1,0:T(8,128)(2,1)} %own.1) | copy-start | bytes 6291460
  21.6 1.3 %collective-permute-start.5 = (bf16[256,128]{1,0:T(8,128)(2,1)S(1)}, bf16[256,128]{1,0:T(8,128)(2,1)S(1)}, u32[]{:S(2)}, u32[]{:S(2)}) collective-permute-start(bf16[256,128]{1,0:T(8,128)(2,1)S(1)} %get-tuple-element.42), channel_id=1, source_target_pairs={{0,4},{4,0},{8,12},{12,8},{16,20},{20,16},{24,28},{28,24},{32,36},... | collective-permute-start | bytes 196616 | tf_op jit(solution)/shard_map/ppermute | solution.py:444
  22.9 2.7 %slice-start.1 = ((s8[8388608]{0:T(1024)(128)(4,1)}), s8[4194304]{0:T(1024)(128)(4,1)S(1)}, s32[]{:S(2)}) async-start(s8[8388608]{0:T(1024)(128)(4,1)} %bitcast.1), calls=%async_computation.1 | async-start | bytes 8388608
  25.6 2.5 %copy-start.1 = (f32[16,2048]{1,0:T(8,128)S(1)}, f32[16,2048]{1,0:T(8,128)}, u32[]{:S(2)}) copy-start(f32[16,2048]{1,0:T(8,128)} %incident.1) | copy-start | bytes 393220
  29.9 2.9 %collective-permute-start.6 = (bf16[16,128]{1,0:T(8,128)(2,1)S(1)}, bf16[16,128]{1,0:T(8,128)(2,1)S(1)}, u32[]{:S(2)}, u32[]{:S(2)}) collective-permute-start(bf16[16,128]{1,0:T(8,128)(2,1)S(1)} %get-tuple-element.44), channel_id=1, source_target_pairs={{0,4},{4,0},{8,12},{12,8},{16,20},{20,16},{24,28},{28,24},{32,36},... | collective-permute-start | bytes 12296 | tf_op jit(solution)/shard_map/ppermute | solution.py:467
  33.1 4.6 %collective-permute-start.7 = (bf16[32,2048]{1,0:T(8,128)(2,1)S(1)}, bf16[32,2048]{1,0:T(8,128)(2,1)S(1)}, u32[]{:S(2)}, u32[]{:S(2)}) collective-permute-start(bf16[32,2048]{1,0:T(8,128)(2,1)S(1)} %get-tuple-element.48), channel_id=1, source_target_pairs={{0,4},{4,0},{8,12},{12,8},{16,20},{20,16},{24,28},{28,24},{32,36},... | collective-permute-start | bytes 393224 | tf_op jit(solution)/shard_map/ppermute | solution.py:478
  33.2 13.2 %collective-permute-start.10 = (bf16[32,2048]{1,0:T(8,128)(2,1)S(1)}, bf16[32,2048]{1,0:T(8,128)(2,1)S(1)}, u32[]{:S(2)}, u32[]{:S(2)}) collective-permute-start(bf16[32,2048]{1,0:T(8,128)(2,1)S(1)} %get-tuple-element.48), channel_id=1, source_target_pairs={{4,16},{12,24},{20,32},{28,40},{36,48},{44,56},{52,64},{60,72},{68... | collective-permute-start | bytes 393224 | tf_op jit(solution)/shard_map/ppermute | solution.py:479
  37.9 8.5 %collective-permute-start.9 = (bf16[432,128]{1,0:T(8,128)(2,1)S(1)}, bf16[432,128]{1,0:T(8,128)(2,1)S(1)}, u32[]{:S(2)}, u32[]{:S(2)}) collective-permute-start(bf16[432,128]{1,0:T(8,128)(2,1)S(1)} %shard_map.115), channel_id=1, source_target_pairs={{4,8},{12,16},{20,24},{28,32},{36,40},{44,48},{52,56},{60,64},{68,... | collective-permute-start | bytes 331784 | tf_op jit(solution)/shard_map/ppermute | solution.py:489
  43.2 3.2 %collective-permute-start.8 = (bf16[16,128]{1,0:T(8,128)(2,1)S(1)}, bf16[16,128]{1,0:T(8,128)(2,1)S(1)}, u32[]{:S(2)}, u32[]{:S(2)}) collective-permute-start(bf16[16,128]{1,0:T(8,128)(2,1)S(1)} %get-tuple-element.49), channel_id=1, source_target_pairs={{0,4},{4,0},{8,12},{12,8},{16,20},{20,16},{24,28},{28,24},{32,36},... | collective-permute-start | bytes 12296 | tf_op jit(solution)/shard_map/ppermute | solution.py:499
  46.7 1.2 %collective-permute-start.11 = (bf16[32,128]{1,0:T(8,128)(2,1)S(1)}, bf16[32,128]{1,0:T(8,128)(2,1)S(1)}, u32[]{:S(2)}, u32[]{:S(2)}) collective-permute-start(bf16[32,128]{1,0:T(8,128)(2,1)S(1)} %get-tuple-element.52.mine), channel_id=1, source_target_pairs={{0,4},{4,0},{8,12},{12,8},{16,20},{20,16},{24,28},{28,24},{32,36},... | collective-permute-start | bytes 24584 | tf_op jit(solution)/shard_map/ppermute | solution.py:512
  48.8 5.8 %collective-permute-start.14 = (bf16[16,2048]{1,0:T(8,128)(2,1)S(1)}, bf16[16,2048]{1,0:T(8,128)(2,1)S(1)}, u32[]{:S(2)}, u32[]{:S(2)}) collective-permute-start(bf16[16,2048]{1,0:T(8,128)(2,1)S(1)} %get-tuple-element.55.x), channel_id=1, source_target_pairs={{0,2},{1,3},{2,0},{3,1},{4,6},{5,7},{6,4},{7,5},{8,10},{9,11},{10,... | collective-permute-start | bytes 196616 | tf_op jit(solution)/shard_map/ppermute | solution.py:532
  50.9 5.5 %collective-permute-start.13 = (bf16[16,2048]{1,0:T(8,128)(2,1)S(1)}, bf16[16,2048]{1,0:T(8,128)(2,1)S(1)}, u32[]{:S(2)}, u32[]{:S(2)}) collective-permute-start(bf16[16,2048]{1,0:T(8,128)(2,1)S(1)} %get-tuple-element.55.x), channel_id=1, source_target_pairs={{0,3},{1,2},{2,1},{3,0},{4,7},{5,6},{6,5},{7,4},{8,11},{9,10},{10,... | collective-permute-start | bytes 196616 | tf_op jit(solution)/shard_map/ppermute | solution.py:532
  51.4 5.0 %collective-permute-start.12 = (bf16[16,2048]{1,0:T(8,128)(2,1)S(1)}, bf16[16,2048]{1,0:T(8,128)(2,1)S(1)}, u32[]{:S(2)}, u32[]{:S(2)}) collective-permute-start(bf16[16,2048]{1,0:T(8,128)(2,1)S(1)} %get-tuple-element.55.x), channel_id=1, source_target_pairs={{0,1},{1,0},{2,3},{3,2},{4,5},{5,4},{6,7},{7,6},{8,9},{9,8},{10,11... | collective-permute-start | bytes 196616 | tf_op jit(solution)/shard_map/ppermute | solution.py:532

commit v5 on v4

--- a/solution.py
+++ b/solution.py
@@ -230,30 +230,31 @@
     ).astype(jnp.bfloat16)
     for rows in chunks():
         first[:, rows] = (-nt(eye, near[rows, at["cross_cols"]]) * inv[:, rows]).astype(jnp.bfloat16)
-    inner[...] = first[:, at["inner"]]
     both = jnp.concatenate([first[...], newest[...]], axis=0)
     for rows in chunks():
         made = nt(both, near[rows, BLK:EDGE])
         second[:, rows] = (-made[:BLK] * inv[:, rows]).astype(jnp.bfloat16)
         coupling[:, rows] = made[BLK:]
-
-
-def response_2_body(near, inv, first, second, side, both, inner, corners):
+    rows = pl.ds(pl.multiple_of((1 - core_parity()) * (OWN - BLK), BLK), BLK)
+    step = -nt(eye, near[rows, at["side_cols"]]) * inv[:, at["inner"]]
+    inner[:BLK] = first[:, at["inner"]]
+    inner[BLK : 2 * BLK] = second[:, at["inner"]]
+    inner[2 * BLK :] = step.astype(jnp.bfloat16)
+
+
+def response_23_body(near, inv, first, second, side, both, third, corners):
     at = places()
     both[:BLK] = second[...]
     for rows in chunks():
-        both[BLK:, rows] = (-nt(side[...], near[rows, at["side_cols"]]) * inv[:, rows]).astype(jnp.bfloat16)
-    inner[...] = both[:, at["inner"]]
+        made = nt(side[:BLK], near[rows, at["side_cols"]])
+        both[BLK:, rows] = (-made * inv[:, rows]).astype(jnp.bfloat16)
+    crossed = nn(first[:, at["inner"]], side[2 * BLK :]).astype(jnp.bfloat16)
+    turned = jnp.concatenate([crossed, side[BLK : 2 * BLK]], axis=0)
+    for rows in chunks():
+        made = nt(both[...], near[rows, BLK:EDGE]) + nt(turned, near[rows, at["side_cols"]])
+        third[:, rows] = (-made * inv[:, rows]).astype(jnp.bfloat16)
     corners[:BLK] = first[:, at["outer"]]
     corners[BLK:] = both[:, at["outer"]]
-
-
-def response_3_body(near, inv, both, side, third):
-    at = places()
-    turned = jnp.concatenate([side[BLK:], side[:BLK]], axis=0)
-    for rows in chunks():
-        made = nt(both[...], near[rows, BLK:EDGE]) + nt(turned, near[rows, at["side_cols"]])
-        third[:, rows] = (-made * inv[:, rows]).astype(jnp.bfloat16)
 
 
 def parts_body(history, half, direct, sems):
@@ -360,11 +361,18 @@
         x_out[:, rows] = x.astype(jnp.bfloat16)
 
 
-def join_body(x, one, three, two, out):
+def join_body(x, one, three, two, out, sems):
     group = lax.axis_index("grp")
-    for k, part in zip((0, 1, 3, 2), (x, one, three, two)):
-        owner = group ^ k
-        out[:, pl.ds(pl.multiple_of(owner * OWN, OWN), OWN)] = part[...]
+    copies = [
+        pltpu.make_async_copy(
+            part, out.at[:, pl.ds(pl.multiple_of((group ^ k) * OWN, OWN), OWN)], sems.at[k]
+        )
+        for k, part in zip((0, 1, 3, 2), (x, one, three, two))
+    ]
+    for copy in copies:
+        copy.start()
+    for copy in copies:
+        copy.wait()
 
 
 def body(
@@ -419,7 +427,7 @@
     home_codes, far_codes = (pltpu.with_memory_space_constraint(x, pltpu.SMEM) for x in (home_codes, far_codes))
     first, coupling, second, inner = call(
         response_1_body,
-        (bf16(BLK, OWN), f32(WAVES, OWN), bf16(BLK, OWN), bf16(BLK, BLK)),
+        (bf16(BLK, OWN), f32(WAVES, OWN), bf16(BLK, OWN), bf16(3 * BLK, BLK)),
         [VMEM] * 3,
         (VMEM,) * 4,
         (near, inv, newest),
@@ -427,21 +435,12 @@
         12 * 10**6,
     )
     values, own = in_vmem(ret_values), in_vmem(history)
-    both, inner, corners = call(
-        response_2_body,
-        (bf16(2 * BLK, OWN), bf16(2 * BLK, BLK), bf16(3 * BLK, BLK)),
+    both, third, corners = call(
+        response_23_body,
+        (bf16(2 * BLK, OWN), bf16(2 * BLK, OWN), bf16(3 * BLK, BLK)),
         [VMEM] * 5,
         (VMEM,) * 3,
         (near, inv, first, second, lax.ppermute(inner, "patch", chip)),
-        product * 16,
-        2**20,
-    )
-    third = call(
-        response_3_body,
-        bf16(2 * BLK, OWN),
-        [VMEM] * 4,
-        VMEM,
-        (near, inv, both, lax.ppermute(inner, "patch", chip)),
         product * 256,
         8 * 2**20,
     )
@@ -521,7 +520,7 @@
     )
     current, x = call(
         last_body,
-        (f32(WAVES, OWN), bf16(WAVES, OWN)),
+        (pltpu.VMEM((WAVES, OWN), jnp.float32), bf16(WAVES, OWN)),
         [VMEM] * 4,
         (VMEM,) * 2,
         (partial, other, both, third),
@@ -532,7 +531,14 @@
         lax.ppermute(x, "grp", [(i, i ^ k) for i in range(4)]) for k in (1, 3, 2)
     ]
     newest = call(
-        join_body, bf16(WAVES, PATCH), [VMEM] * 4, VMEM, (x, *turns), 0, 2**20
+        join_body,
+        bf16(WAVES, PATCH),
+        [VMEM] * 4,
+        HBM,
+        (x, *turns),
+        0,
+        2**20,
+        [pltpu.SemaphoreType.DMA((4,))],
     )
     return current, newest
 

time: 57.9 us -> 56.4 us (0.974); the launches traced: 57.1 us -> 56.4 us
  Pallas kernels: 25.4 us -> 23.3 us
  waiting for transfers between devices: 7.41 us -> 8.34 us
  local copies, waits for them, and re-layouts: 0.02 us -> 0.67 us
    pallas_call x16 -> x15, Pallas kernels: 25.4 us -> 23.3 us  [call(): pl.pallas_call(body, out_shape=out, in_specs=ins, out_specs=outs, scratch...]
    ppermute x1, starting transfers between devices: 4.47 us -> 5.54 us  [body(): far = lax.ppermute(far, 'patch', beyond)]
    ppermute x2, starting transfers between devices: 1.66 us -> 0.63 us  [body(): edge = lax.ppermute(inner, 'patch', chip)]
    ppermute x2 -> x1, waiting for transfers between devices: 2.29 us -> 1.29 us  [body(): lax.ppermute(inner, 'patch', chip)]
    ppermute x1, waiting for transfers between devices: 0.01 us -> 0.98 us  [body(): near_by = lax.ppermute(near_by, 'patch', links)]
    ppermute x1, waiting for transfers between devices: 0.01 us -> 0.87 us  [body(): cross = lax.ppermute(direct, 'patch', links)]
    ppermute x1, starting transfers between devices: 2.83 us -> 1.97 us  [body(): near_by = lax.ppermute(near_by, 'patch', links)]
    unnamed x8 -> x9, local copies, waits for them, and re-layouts: 0.02 us -> 0.67 us
  transfers between devices with their start and end apart: 15 -> 14, of which waited for: 6 -> 7; matrix products, arithmetic and copies ran while one was open for 0% -> 1% of each run, Pallas kernels for 37% -> 36%
where the time goes in v5:
time: 56.4 us
  Pallas kernels  23.3 us (41%)
  starting transfers between devices  22.6 us (40%)
  waiting for transfers between devices  8.34 us (15%)
  between operations  1.45 us (3%)
  local copies, waits for them, and re-layouts  0.67 us (1%)
    pallas_call x15, Pallas kernels, call(): pl.pallas_call(body, out_shape=out, in_specs=ins, out_specs=outs, scratch...  23.3 us
    ppermute x1, starting transfers between devices, body(): mine = lax.ppermute(half, 'patch', links)  6.3 us
    ppermute x1, starting transfers between devices, body(): far = lax.ppermute(far, 'patch', beyond)  5.54 us
    ppermute x3, waiting for transfers between devices, body(): lax.ppermute(x, 'grp', [(i, i ^ k) for i in range(4)])  4.12 us
    ppermute x3, starting transfers between devices, body(): lax.ppermute(x, 'grp', [(i, i ^ k) for i in range(4)])  3.93 us
    ppermute x1, starting transfers between devices, body(): near_by = lax.ppermute(near_by, 'patch', links)  1.97 us
    ppermute x1, starting transfers between devices, body(): cross = lax.ppermute(direct, 'patch', links)  1.92 us
    ppermute x1, starting transfers between devices, body(): other = lax.ppermute(mine, ('patch', 'grp'), pairs)  1.58 us
  transfers between devices with their start and end apart: 14, of which 7 were waited for; matrix products, arithmetic and copies ran while one was open for 1% of the time, Pallas kernels for 36%

profile of v5, /device:TPU:6, one launch (start us, length us, event | category | flops | bytes accessed | tf_op | source)
XLA Modules:
  0.0 56.4 jit_solution(15230146262957559534)
XLA Ops:
  0.7 1.4 %shard_map.105 = (bf16[2,16,8192]{2,1,0:T(8,128)(2,1)S(1)}, bf16[4,16,8192]{2,1,0:T(8,128)(2,1)S(1)}) custom-call(bf16[8,16,8192]{2,1,0:T(8,128)(2,1)} %own.1), custom_call_target="tpu_custom_call" | custom-call | flops 1 | bytes 3145728 | tf_op jit(solution)/shard_map/pallas_call | solution.py:45
  2.1 6.3 %collective-permute-start.1 = (bf16[2,16,8192]{2,1,0:T(8,128)(2,1)S(1)}, bf16[2,16,8192]{2,1,0:T(8,128)(2,1)S(1)}, u32[]{:S(2)}, u32[]{:S(2)}) collective-permute-start(bf16[2,16,8192]{2,1,0:T(8,128)(2,1)S(1)} %get-tuple-element.32), channel_id=1, source_target_pairs={{4,8},{12,16},{20,24},{28,32},{36,40},{44,48},{52,56},{60,64},{68,... | collective-permute-start | bytes 1572872 | tf_op jit(solution)/shard_map/ppermute | solution.py:403
  8.5 1.9 %collective-permute-start = (bf16[4,16,8192]{2,1,0:T(8,128)(2,1)S(1)}, bf16[4,16,8192]{2,1,0:T(8,128)(2,1)S(1)}, u32[]{:S(2)}, u32[]{:S(2)}) collective-permute-start(bf16[4,16,8192]{2,1,0:T(8,128)(2,1)S(1)} %get-tuple-element.31), channel_id=1, source_target_pairs={{4,8},{12,16},{20,24},{28,32},{36,40},{44,48},{52,56},{60,64},{68,... | collective-permute-start | bytes 3145736 | tf_op jit(solution)/shard_map/ppermute | solution.py:404
  11.0 3.9 %shard_map.104 = (bf16[2048,2304]{1,0:T(8,128)(2,1)S(1)}, f32[1,2048]{1,0:T(1,128)S(1)}, bf16[16,2048]{1,0:T(8,128)(2,1)S(1)}, s32[320]{0:T(512)S(4)}, s32[320]{0:T(512)S(4)}) custom-call(s32[1]{0:T(128)S(6)} %copy.12.live, s32[256]{0:T(256)} %row_hbm.1, s32[256]{0:T(256)} %col_hbm.1, s32[256]{0:T(256)} %delay_hbm.1, f32[1,2048]{1,0:T(1,128)} %bitcast.3, ...), custom_call_target="tpu_custom_call" | custom-call | flops 1000000 | bytes 12000000 | tf_op jit(solution)/shard_map/pallas_call | solution.py:45
  14.9 0.4 collective-permute-done.1.mine
  15.3 1.6 %collective-permute-start.2 = (bf16[2,16,8192]{2,1,0:T(8,128)(2,1)S(1)}, bf16[2,16,8192]{2,1,0:T(8,128)(2,1)S(1)}, u32[]{:S(2)}, u32[]{:S(2)}) collective-permute-start(bf16[2,16,8192]{2,1,0:T(8,128)(2,1)S(1)} %collective-permute-done.1.mine), channel_id=1, source_target_pairs={{0,1},{1,0},{2,3},{3,2},{5,6},{6,5},{7,4},{4,7},{10,11},{11,10},{8... | collective-permute-start | bytes 1572872 | tf_op jit(solution)/shard_map/ppermute | solution.py:426
  16.9 3.1 %shard_map.106 = (bf16[128,2048]{1,0:T(8,128)(2,1)S(1)}, f32[16,2048]{1,0:T(8,128)S(1)}, bf16[128,2048]{1,0:T(8,128)(2,1)S(1)}, bf16[384,128]{1,0:T(8,128)(2,1)S(1)}) custom-call(bf16[2048,2304]{1,0:T(8,128)(2,1)S(1)} %get-tuple-element.29.near, f32[1,2048]{1,0:T(1,128)S(1)} %get-tuple-element.36.inv, bf16[16,2048]{1,0:T(8,128)(2,1)S(1)} %get-tuple-element.37.newest), custom_call_target="tpu_custom_call" | custom-call | flops 1207959552 | bytes 12000000 | tf_op jit(solution)/shard_map/pallas_call | solution.py:45
  20.1 1.3 %collective-permute-done.4.side = bf16[384,128]{1,0:T(8,128)(2,1)S(1)} collective-permute-done((bf16[384,128]{1,0:T(8,128)(2,1)S(1)}, bf16[384,128]{1,0:T(8,128)(2,1)S(1)}, u32[]{:S(2)}, u32[]{:S(2)}) %collective-permute-start.4) | collective-permute-done | bytes 98336 | tf_op jit(solution)/shard_map/ppermute | solution.py:443
  21.4 2.9 %shard_map.107 = (bf16[256,2048]{1,0:T(8,128)(2,1)S(1)}, bf16[256,2048]{1,0:T(8,128)(2,1)S(1)}, bf16[384,128]{1,0:T(8,128)(2,1)S(1)}) custom-call(bf16[2048,2304]{1,0:T(8,128)(2,1)S(1)} %get-tuple-element.29.near, f32[1,2048]{1,0:T(1,128)S(1)} %get-tuple-element.36.inv, bf16[128,2048]{1,0:T(8,128)(2,1)S(1)} %get-tuple-element.38.first, ...), custom_call_target="tpu_custom_call" | custom-call | flops 2147483648 | bytes 8388608 | tf_op jit(solution)/shard_map/pallas_call | solution.py:45
  24.4 1.5 %shard_map.108.acc = f32[16,16,128]{2,1,0:T(8,128)S(1)} custom-call(s32[320]{0:T(512)S(4)} %get-tuple-element.35.codes, bf16[256,128,128]{2,1,0:T(8,128)(2,1)S(1)} %bitcast.2, bf16[8,16,8192]{2,1,0:T(8,128)(2,1)S(1)} %copy-done, bf16[8,16,8192]{2,1,0:T(8,128)(2,1)S(1)} %collective-permute-done.3.side, bf16[256,2048]{1,0:T(8,128)(2,1)S(1)} %get-tuple-element.41.after.third), custom_call_target="tpu_custom_call" | custom-call | flops 2000000000 | bytes 10000000 | tf_op jit(solution)/shard_map/pallas_call | solution.py:45
  25.8 0.9 %collective-permute-done.cross = bf16[4,16,8192]{2,1,0:T(8,128)(2,1)S(1)} collective-permute-done((bf16[4,16,8192]{2,1,0:T(8,128)(2,1)S(1)}, bf16[4,16,8192]{2,1,0:T(8,128)(2,1)S(1)}, u32[]{:S(2)}, u32[]{:S(2)}) %collective-permute-start) | collective-permute-done | bytes 1048608 | tf_op jit(solution)/shard_map/ppermute | solution.py:404
  26.7 1.4 %shard_map.109 = (f32[16,2048]{1,0:T(8,128)S(1)}, bf16[16,2048]{1,0:T(8,128)(2,1)S(1)}, bf16[16,128]{1,0:T(8,128)(2,1)S(1)}) custom-call(s32[320]{0:T(512)S(4)} %get-tuple-element.30.codes, bf16[256,128,128]{2,1,0:T(8,128)(2,1)S(1)} %bitcast.2, bf16[2048,2304]{1,0:T(8,128)(2,1)S(1)} %get-tuple-element.29.near, ...), custom_call_target="tpu_custom_call" | custom-call | flops 1000000000 | bytes 1000000 | tf_op jit(solution)/shard_map/pallas_call | solution.py:45
  28.1 2.3 %shard_map.110.coupling = f32[16,2048]{1,0:T(8,128)S(1)} custom-call(bf16[16,2048]{1,0:T(8,128)(2,1)S(1)} %get-tuple-element.44.x, bf16[2048,2304]{1,0:T(8,128)(2,1)S(1)} %get-tuple-element.29.near), custom_call_target="tpu_custom_call" | custom-call | flops 134217728 | bytes 8388608 | tf_op jit(solution)/shard_map/pallas_call | solution.py:45
  30.4 0.3 shard_map.111
  30.6 0.6 %collective-permute-start.6 = (bf16[32,2048]{1,0:T(8,128)(2,1)S(1)}, bf16[32,2048]{1,0:T(8,128)(2,1)S(1)}, u32[]{:S(2)}, u32[]{:S(2)}) collective-permute-start(bf16[32,2048]{1,0:T(8,128)(2,1)S(1)} %get-tuple-element.47), channel_id=1, source_target_pairs={{0,4},{4,0},{8,12},{12,8},{16,20},{20,16},{24,28},{28,24},{32,36},... | collective-permute-start | bytes 393224 | tf_op jit(solution)/shard_map/ppermute | solution.py:477
  31.2 5.5 %collective-permute-start.9 = (bf16[32,2048]{1,0:T(8,128)(2,1)S(1)}, bf16[32,2048]{1,0:T(8,128)(2,1)S(1)}, u32[]{:S(2)}, u32[]{:S(2)}) collective-permute-start(bf16[32,2048]{1,0:T(8,128)(2,1)S(1)} %get-tuple-element.47), channel_id=1, source_target_pairs={{4,16},{12,24},{20,32},{28,40},{36,48},{44,56},{52,64},{60,72},{68... | collective-permute-start | bytes 393224 | tf_op jit(solution)/shard_map/ppermute | solution.py:478
  36.8 0.2 shard_map.114
  37.0 2.0 %collective-permute-start.8 = (bf16[432,128]{1,0:T(8,128)(2,1)S(1)}, bf16[432,128]{1,0:T(8,128)(2,1)S(1)}, u32[]{:S(2)}, u32[]{:S(2)}) collective-permute-start(bf16[432,128]{1,0:T(8,128)(2,1)S(1)} %shard_map.114), channel_id=1, source_target_pairs={{4,8},{12,16},{20,24},{28,32},{36,40},{44,48},{52,56},{60,64},{68,... | collective-permute-start | bytes 331784 | tf_op jit(solution)/shard_map/ppermute | solution.py:488
  39.0 2.4 %shard_map.112 = (bf16[16,2048]{1,0:T(8,128)(2,1)S(1)}, bf16[16,128]{1,0:T(8,128)(2,1)S(1)}) custom-call(bf16[2048,2304]{1,0:T(8,128)(2,1)S(1)} %get-tuple-element.29.near, bf16[16,2048]{1,0:T(8,128)(2,1)S(1)} %get-tuple-element.46.x.y, bf16[32,2048]{1,0:T(8,128)(2,1)S(1)} %collective-permute-done.6.side, f32[16,2048]{1,0:T(8,128)S(1)} %get-tuple-element.45.rhs, ...), custom_call_target="tpu_custom_call" | custom-call | flops 134217728 | bytes 8388608 | tf_op jit(solution)/shard_map/pallas_call | solution.py:45
  41.4 0.6 %collective-permute-start.7 = (bf16[16,128]{1,0:T(8,128)(2,1)S(1)}, bf16[16,128]{1,0:T(8,128)(2,1)S(1)}, u32[]{:S(2)}, u32[]{:S(2)}) collective-permute-start(bf16[16,128]{1,0:T(8,128)(2,1)S(1)} %get-tuple-element.48), channel_id=1, source_target_pairs={{0,4},{4,0},{8,12},{12,8},{16,20},{20,16},{24,28},{28,24},{32,36},... | collective-permute-start | bytes 12296 | tf_op jit(solution)/shard_map/ppermute | solution.py:498
  42.0 2.3 %shard_map.113.after.coupling = f32[16,2048]{1,0:T(8,128)S(1)} custom-call(bf16[16,2048]{1,0:T(8,128)(2,1)S(1)} %get-tuple-element.49.x, bf16[2048,2304]{1,0:T(8,128)(2,1)S(1)} %get-tuple-element.29.near), custom_call_target="tpu_custom_call" | custom-call | flops 134217728 | bytes 8388608 | tf_op jit(solution)/shard_map/pallas_call | solution.py:45
  44.3 1.0 %collective-permute-done.8.near_by = bf16[432,128]{1,0:T(8,128)(2,1)S(1)} collective-permute-done((bf16[432,128]{1,0:T(8,128)(2,1)S(1)}, bf16[432,128]{1,0:T(8,128)(2,1)S(1)}, u32[]{:S(2)}, u32[]{:S(2)}) %collective-permute-start.8) | collective-permute-done | bytes 110624 | tf_op jit(solution)/shard_map/ppermute | solution.py:488
  45.2 0.3 shard_map.115
  45.5 0.5 shard_map.116.partial
  46.0 0.7 %collective-permute-done.10.other = bf16[32,128]{1,0:T(8,128)(2,1)S(1)} collective-permute-done((bf16[32,128]{1,0:T(8,128)(2,1)S(1)}, bf16[32,128]{1,0:T(8,128)(2,1)S(1)}, u32[]{:S(2)}, u32[]{:S(2)}) %collective-permute-start.10) | collective-permute-done | bytes 8224 | tf_op jit(solution)/shard_map/ppermute | solution.py:511
  46.7 0.2 shard_map.117
  46.9 3.2 %collective-permute-start.13 = (bf16[16,2048]{1,0:T(8,128)(2,1)S(1)}, bf16[16,2048]{1,0:T(8,128)(2,1)S(1)}, u32[]{:S(2)}, u32[]{:S(2)}) collective-permute-start(bf16[16,2048]{1,0:T(8,128)(2,1)S(1)} %get-tuple-element.55.x), channel_id=1, source_target_pairs={{0,2},{1,3},{2,0},{3,1},{4,6},{5,7},{6,4},{7,5},{8,10},{9,11},{10,... | collective-permute-start | bytes 196616 | tf_op jit(solution)/shard_map/ppermute | solution.py:531
  50.2 0.7 %collective-permute-start.12 = (bf16[16,2048]{1,0:T(8,128)(2,1)S(1)}, bf16[16,2048]{1,0:T(8,128)(2,1)S(1)}, u32[]{:S(2)}, u32[]{:S(2)}) collective-permute-start(bf16[16,2048]{1,0:T(8,128)(2,1)S(1)} %get-tuple-element.55.x), channel_id=1, source_target_pairs={{0,3},{1,2},{2,1},{3,0},{4,7},{5,6},{6,5},{7,4},{8,11},{9,10},{10,... | collective-permute-start | bytes 196616 | tf_op jit(solution)/shard_map/ppermute | solution.py:531
  50.9 0.7 %copy.11 = f32[16,2048]{1,0:T(8,128)} copy(f32[16,2048]{1,0:T(8,128)S(1)} %get-tuple-element.56) | data formatting | bytes 262144
  51.5 1.2 %collective-permute-done.13.two = bf16[16,2048]{1,0:T(8,128)(2,1)S(1)} collective-permute-done((bf16[16,2048]{1,0:T(8,128)(2,1)S(1)}, bf16[16,2048]{1,0:T(8,128)(2,1)S(1)}, u32[]{:S(2)}, u32[]{:S(2)}) %collective-permute-start.13) | collective-permute-done | bytes 65568 | tf_op jit(solution)/shard_map/ppermute | solution.py:531
  52.8 2.9 %collective-permute-done.12.three = bf16[16,2048]{1,0:T(8,128)(2,1)S(1)} collective-permute-done((bf16[16,2048]{1,0:T(8,128)(2,1)S(1)}, bf16[16,2048]{1,0:T(8,128)(2,1)S(1)}, u32[]{:S(2)}, u32[]{:S(2)}) %collective-permute-start.12) | collective-permute-done | bytes 65568 | tf_op jit(solution)/shard_map/ppermute | solution.py:531
  55.6 0.7 %shard_map.118 = bf16[16,8192]{1,0:T(8,128)(2,1)} custom-call(bf16[16,2048]{1,0:T(8,128)(2,1)S(1)} %get-tuple-element.55.x, bf16[16,2048]{1,0:T(8,128)(2,1)S(1)} %collective-permute-done.11.one, bf16[16,2048]{1,0:T(8,128)(2,1)S(1)} %collective-permute-done.12.three, bf16[16,2048]{1,0:T(8,128)(2,1)S(1)} %collective-permute-done.13.two), custom_call_target="tpu_custom_call" | custom-call | bytes 1048576 | tf_op jit(solution)/shard_map/pallas_call | solution.py:45
  (21 shorter events, 0.3 us)
Async XLA Ops:
  0.6 23.7 %collective-permute-start.3 = (bf16[8,16,8192]{2,1,0:T(8,128)(2,1)}, bf16[8,16,8192]{2,1,0:T(8,128)(2,1)S(1)}, u32[]{:S(2)}, u32[]{:S(2)}) collective-permute-start(bf16[8,16,8192]{2,1,0:T(8,128)(2,1)} %own.1), channel_id=1, source_target_pairs={{0,4},{4,0},{8,12},{12,8},{16,20},{20,16},{24,28},{28,24},{32,36},... | collective-permute-start | bytes 6291464 | tf_op jit(solution)/shard_map/ppermute | solution.py:405
  2.1 13.2 %collective-permute-start.1 = (bf16[2,16,8192]{2,1,0:T(8,128)(2,1)S(1)}, bf16[2,16,8192]{2,1,0:T(8,128)(2,1)S(1)}, u32[]{:S(2)}, u32[]{:S(2)}) collective-permute-start(bf16[2,16,8192]{2,1,0:T(8,128)(2,1)S(1)} %get-tuple-element.32), channel_id=1, source_target_pairs={{4,8},{12,16},{20,24},{28,32},{36,40},{44,48},{52,56},{60,64},{68,... | collective-permute-start | bytes 1572872 | tf_op jit(solution)/shard_map/ppermute | solution.py:403
  8.5 18.2 %collective-permute-start = (bf16[4,16,8192]{2,1,0:T(8,128)(2,1)S(1)}, bf16[4,16,8192]{2,1,0:T(8,128)(2,1)S(1)}, u32[]{:S(2)}, u32[]{:S(2)}) collective-permute-start(bf16[4,16,8192]{2,1,0:T(8,128)(2,1)S(1)} %get-tuple-element.31), channel_id=1, source_target_pairs={{4,8},{12,16},{20,24},{28,32},{36,40},{44,48},{52,56},{60,64},{68,... | collective-permute-start | bytes 3145736 | tf_op jit(solution)/shard_map/ppermute | solution.py:404
  15.3 11.4 %collective-permute-start.2 = (bf16[2,16,8192]{2,1,0:T(8,128)(2,1)S(1)}, bf16[2,16,8192]{2,1,0:T(8,128)(2,1)S(1)}, u32[]{:S(2)}, u32[]{:S(2)}) collective-permute-start(bf16[2,16,8192]{2,1,0:T(8,128)(2,1)S(1)} %collective-permute-done.1.mine), channel_id=1, source_target_pairs={{0,1},{1,0},{2,3},{3,2},{5,6},{6,5},{7,4},{4,7},{10,11},{11,10},{8... | collective-permute-start | bytes 1572872 | tf_op jit(solution)/shard_map/ppermute | solution.py:426
  16.9 7.4 %slice-start = ((s8[8388608]{0:T(1024)(128)(4,1)}), s8[4194304]{0:T(1024)(128)(4,1)S(1)}, s32[]{:S(2)}) async-start(s8[8388608]{0:T(1024)(128)(4,1)} %bitcast.1), calls=%async_computation | async-start | bytes 8388608
  16.9 7.5 %copy-start = (bf16[8,16,8192]{2,1,0:T(8,128)(2,1)S(1)}, bf16[8,16,8192]{2,1,0:T(8,128)(2,1)}, u32[]{:S(2)}) copy-start(bf16[8,16,8192]{2,1,0:T(8,128)(2,1)} %own.1) | copy-start | bytes 6291460
  20.0 1.4 %collective-permute-start.4 = (bf16[384,128]{1,0:T(8,128)(2,1)S(1)}, bf16[384,128]{1,0:T(8,128)(2,1)S(1)}, u32[]{:S(2)}, u32[]{:S(2)}) collective-permute-start(bf16[384,128]{1,0:T(8,128)(2,1)S(1)} %get-tuple-element.40), channel_id=1, source_target_pairs={{0,4},{4,0},{8,12},{12,8},{16,20},{20,16},{24,28},{28,24},{32,36},... | collective-permute-start | bytes 294920 | tf_op jit(solution)/shard_map/ppermute | solution.py:443
  21.3 3.0 %slice-start.1 = ((s8[8388608]{0:T(1024)(128)(4,1)}), s8[4194304]{0:T(1024)(128)(4,1)S(1)}, s32[]{:S(2)}) async-start(s8[8388608]{0:T(1024)(128)(4,1)} %bitcast.1), calls=%async_computation.1 | async-start | bytes 8388608
  24.3 2.4 %copy-start.1 = (f32[16,2048]{1,0:T(8,128)S(1)}, f32[16,2048]{1,0:T(8,128)}, u32[]{:S(2)}) copy-start(f32[16,2048]{1,0:T(8,128)} %incident.1) | copy-start | bytes 393220
  28.0 2.3 %collective-permute-start.5 = (bf16[16,128]{1,0:T(8,128)(2,1)S(1)}, bf16[16,128]{1,0:T(8,128)(2,1)S(1)}, u32[]{:S(2)}, u32[]{:S(2)}) collective-permute-start(bf16[16,128]{1,0:T(8,128)(2,1)S(1)} %get-tuple-element.43), channel_id=1, source_target_pairs={{0,4},{4,0},{8,12},{12,8},{16,20},{20,16},{24,28},{28,24},{32,36},... | collective-permute-start | bytes 12296 | tf_op jit(solution)/shard_map/ppermute | solution.py:466
  30.6 6.1 %collective-permute-start.6 = (bf16[32,2048]{1,0:T(8,128)(2,1)S(1)}, bf16[32,2048]{1,0:T(8,128)(2,1)S(1)}, u32[]{:S(2)}, u32[]{:S(2)}) collective-permute-start(bf16[32,2048]{1,0:T(8,128)(2,1)S(1)} %get-tuple-element.47), channel_id=1, source_target_pairs={{0,4},{4,0},{8,12},{12,8},{16,20},{20,16},{24,28},{28,24},{32,36},... | collective-permute-start | bytes 393224 | tf_op jit(solution)/shard_map/ppermute | solution.py:477
  31.2 13.0 %collective-permute-start.9 = (bf16[32,2048]{1,0:T(8,128)(2,1)S(1)}, bf16[32,2048]{1,0:T(8,128)(2,1)S(1)}, u32[]{:S(2)}, u32[]{:S(2)}) collective-permute-start(bf16[32,2048]{1,0:T(8,128)(2,1)S(1)} %get-tuple-element.47), channel_id=1, source_target_pairs={{4,16},{12,24},{20,32},{28,40},{36,48},{44,56},{52,64},{60,72},{68... | collective-permute-start | bytes 393224 | tf_op jit(solution)/shard_map/ppermute | solution.py:478
  37.0 8.2 %collective-permute-start.8 = (bf16[432,128]{1,0:T(8,128)(2,1)S(1)}, bf16[432,128]{1,0:T(8,128)(2,1)S(1)}, u32[]{:S(2)}, u32[]{:S(2)}) collective-permute-start(bf16[432,128]{1,0:T(8,128)(2,1)S(1)} %shard_map.114), channel_id=1, source_target_pairs={{4,8},{12,16},{20,24},{28,32},{36,40},{44,48},{52,56},{60,64},{68,... | collective-permute-start | bytes 331784 | tf_op jit(solution)/shard_map/ppermute | solution.py:488
  41.4 2.8 %collective-permute-start.7 = (bf16[16,128]{1,0:T(8,128)(2,1)S(1)}, bf16[16,128]{1,0:T(8,128)(2,1)S(1)}, u32[]{:S(2)}, u32[]{:S(2)}) collective-permute-start(bf16[16,128]{1,0:T(8,128)(2,1)S(1)} %get-tuple-element.48), channel_id=1, source_target_pairs={{0,4},{4,0},{8,12},{12,8},{16,20},{20,16},{24,28},{28,24},{32,36},... | collective-permute-start | bytes 12296 | tf_op jit(solution)/shard_map/ppermute | solution.py:498
  45.5 1.2 %collective-permute-start.10 = (bf16[32,128]{1,0:T(8,128)(2,1)S(1)}, bf16[32,128]{1,0:T(8,128)(2,1)S(1)}, u32[]{:S(2)}, u32[]{:S(2)}) collective-permute-start(bf16[32,128]{1,0:T(8,128)(2,1)S(1)} %get-tuple-element.51.mine), channel_id=1, source_target_pairs={{0,4},{4,0},{8,12},{12,8},{16,20},{20,16},{24,28},{28,24},{32,36},... | collective-permute-start | bytes 24584 | tf_op jit(solution)/shard_map/ppermute | solution.py:511
  46.9 5.8 %collective-permute-start.13 = (bf16[16,2048]{1,0:T(8,128)(2,1)S(1)}, bf16[16,2048]{1,0:T(8,128)(2,1)S(1)}, u32[]{:S(2)}, u32[]{:S(2)}) collective-permute-start(bf16[16,2048]{1,0:T(8,128)(2,1)S(1)} %get-tuple-element.55.x), channel_id=1, source_target_pairs={{0,2},{1,3},{2,0},{3,1},{4,6},{5,7},{6,4},{7,5},{8,10},{9,11},{10,... | collective-permute-start | bytes 196616 | tf_op jit(solution)/shard_map/ppermute | solution.py:531
  50.2 5.5 %collective-permute-start.12 = (bf16[16,2048]{1,0:T(8,128)(2,1)S(1)}, bf16[16,2048]{1,0:T(8,128)(2,1)S(1)}, u32[]{:S(2)}, u32[]{:S(2)}) collective-permute-start(bf16[16,2048]{1,0:T(8,128)(2,1)S(1)} %get-tuple-element.55.x), channel_id=1, source_target_pairs={{0,3},{1,2},{2,1},{3,0},{4,7},{5,6},{6,5},{7,4},{8,11},{9,10},{10,... | collective-permute-start | bytes 196616 | tf_op jit(solution)/shard_map/ppermute | solution.py:531
  50.9 4.8 %collective-permute-start.11 = (bf16[16,2048]{1,0:T(8,128)(2,1)S(1)}, bf16[16,2048]{1,0:T(8,128)(2,1)S(1)}, u32[]{:S(2)}, u32[]{:S(2)}) collective-permute-start(bf16[16,2048]{1,0:T(8,128)(2,1)S(1)} %get-tuple-element.55.x), channel_id=1, source_target_pairs={{0,1},{1,0},{2,3},{3,2},{4,5},{5,4},{6,7},{7,6},{8,9},{9,8},{10,11... | collective-permute-start | bytes 196616 | tf_op jit(solution)/shard_map/ppermute | solution.py:531

commit v6 on v5

--- a/solution.py
+++ b/solution.py
@@ -15,7 +15,7 @@
 EDGE = OWN + BLK
 PATCH = 4 * OWN
 COLS = PATCH // BLK
-UNROLL = 32
+UNROLL = 48
 DIRECT = 4
 ROWS = 256
 NT = (((1,), (1,)), ((), ()))

time: 56.4 us -> 56.4 us (level); the launches traced: 56.4 us -> 55.6 us
  waiting for transfers between devices: 8.34 us -> 6.06 us
  Pallas kernels: 23.3 us -> 24.3 us
  starting transfers between devices: 22.6 us -> 23.2 us
    ppermute x1, starting transfers between devices: 1.97 us -> 4.88 us  [body(): near_by = lax.ppermute(near_by, 'patch', links)]
    ppermute x1, starting transfers between devices: 5.54 us -> 2.83 us  [body(): far = lax.ppermute(far, 'patch', beyond)]
    ppermute x1, waiting for transfers between devices: 0.98 us -> 0.01 us  [body(): near_by = lax.ppermute(near_by, 'patch', links)]
    pallas_call x15, Pallas kernels: 23.3 us -> 24.3 us  [call(): pl.pallas_call(body, out_shape=out, in_specs=ins, out_specs=outs, scratch...]
  transfers between devices with their start and end apart: 14 -> 14, of which waited for: 7 -> 6; matrix products, arithmetic and copies ran while one was open for 1% -> 1% of each run, Pallas kernels for 36% -> 38%
where the time goes in v6:
time: 56.4 us; the launch traced here: 55.6 us
  Pallas kernels  24.3 us (43%)
  starting transfers between devices  23.2 us (41%)
  waiting for transfers between devices  6.06 us (11%)
  between operations  1.45 us (3%)
  local copies, waits for them, and re-layouts  0.67 us (1%)
    pallas_call x15, Pallas kernels, call(): pl.pallas_call(body, out_shape=out, in_specs=ins, out_specs=outs, scratch...  24.3 us
    ppermute x1, starting transfers between devices, body(): mine = lax.ppermute(half, 'patch', links)  6.3 us
    ppermute x1, starting transfers between devices, body(): near_by = lax.ppermute(near_by, 'patch', links)  4.88 us
    ppermute x3, starting transfers between devices, body(): lax.ppermute(x, 'grp', [(i, i ^ k) for i in range(4)])  4.32 us
    ppermute x3, waiting for transfers between devices, body(): lax.ppermute(x, 'grp', [(i, i ^ k) for i in range(4)])  3.76 us
    ppermute x1, starting transfers between devices, body(): far = lax.ppermute(far, 'patch', beyond)  2.83 us
    ppermute x1, starting transfers between devices, body(): cross = lax.ppermute(direct, 'patch', links)  1.92 us
    ppermute x1, starting transfers between devices, body(): other = lax.ppermute(mine, ('patch', 'grp'), pairs)  1.58 us
  transfers between devices with their start and end apart: 14, of which 6 were waited for; matrix products, arithmetic and copies ran while one was open for 1% of the time, Pallas kernels for 38%

profile of v6, /device:TPU:6, one launch (start us, length us, event | category | flops | bytes accessed | tf_op | source)
XLA Modules:
  0.0 55.6 jit_solution(15086995809599372659)
XLA Ops:
  0.7 1.4 %shard_map.105 = (bf16[2,16,8192]{2,1,0:T(8,128)(2,1)S(1)}, bf16[4,16,8192]{2,1,0:T(8,128)(2,1)S(1)}) custom-call(bf16[8,16,8192]{2,1,0:T(8,128)(2,1)} %own.1), custom_call_target="tpu_custom_call" | custom-call | flops 1 | bytes 3145728 | tf_op jit(solution)/shard_map/pallas_call | solution.py:45
  2.1 6.3 %collective-permute-start.1 = (bf16[2,16,8192]{2,1,0:T(8,128)(2,1)S(1)}, bf16[2,16,8192]{2,1,0:T(8,128)(2,1)S(1)}, u32[]{:S(2)}, u32[]{:S(2)}) collective-permute-start(bf16[2,16,8192]{2,1,0:T(8,128)(2,1)S(1)} %get-tuple-element.32), channel_id=1, source_target_pairs={{4,8},{12,16},{20,24},{28,32},{36,40},{44,48},{52,56},{60,64},{68,... | collective-permute-start | bytes 1572872 | tf_op jit(solution)/shard_map/ppermute | solution.py:403
  8.5 1.9 %collective-permute-start = (bf16[4,16,8192]{2,1,0:T(8,128)(2,1)S(1)}, bf16[4,16,8192]{2,1,0:T(8,128)(2,1)S(1)}, u32[]{:S(2)}, u32[]{:S(2)}) collective-permute-start(bf16[4,16,8192]{2,1,0:T(8,128)(2,1)S(1)} %get-tuple-element.31), channel_id=1, source_target_pairs={{4,8},{12,16},{20,24},{28,32},{36,40},{44,48},{52,56},{60,64},{68,... | collective-permute-start | bytes 3145736 | tf_op jit(solution)/shard_map/ppermute | solution.py:404
  11.0 4.0 %shard_map.104 = (bf16[2048,2304]{1,0:T(8,128)(2,1)S(1)}, f32[1,2048]{1,0:T(1,128)S(1)}, bf16[16,2048]{1,0:T(8,128)(2,1)S(1)}, s32[352]{0:T(512)S(4)}, s32[352]{0:T(512)S(4)}) custom-call(s32[1]{0:T(128)S(6)} %copy.12.live, s32[256]{0:T(256)} %row_hbm.1, s32[256]{0:T(256)} %col_hbm.1, s32[256]{0:T(256)} %delay_hbm.1, f32[1,2048]{1,0:T(1,128)} %bitcast.3, ...), custom_call_target="tpu_custom_call" | custom-call | flops 1000000 | bytes 12000000 | tf_op jit(solution)/shard_map/pallas_call | solution.py:45
  15.0 0.3 collective-permute-done.1.mine
  15.3 1.6 %collective-permute-start.2 = (bf16[2,16,8192]{2,1,0:T(8,128)(2,1)S(1)}, bf16[2,16,8192]{2,1,0:T(8,128)(2,1)S(1)}, u32[]{:S(2)}, u32[]{:S(2)}) collective-permute-start(bf16[2,16,8192]{2,1,0:T(8,128)(2,1)S(1)} %collective-permute-done.1.mine), channel_id=1, source_target_pairs={{0,1},{1,0},{2,3},{3,2},{5,6},{6,5},{7,4},{4,7},{10,11},{11,10},{8... | collective-permute-start | bytes 1572872 | tf_op jit(solution)/shard_map/ppermute | solution.py:426
  16.9 3.1 %shard_map.106 = (bf16[128,2048]{1,0:T(8,128)(2,1)S(1)}, f32[16,2048]{1,0:T(8,128)S(1)}, bf16[128,2048]{1,0:T(8,128)(2,1)S(1)}, bf16[384,128]{1,0:T(8,128)(2,1)S(1)}) custom-call(bf16[2048,2304]{1,0:T(8,128)(2,1)S(1)} %get-tuple-element.29.near, f32[1,2048]{1,0:T(1,128)S(1)} %get-tuple-element.36.inv, bf16[16,2048]{1,0:T(8,128)(2,1)S(1)} %get-tuple-element.37.newest), custom_call_target="tpu_custom_call" | custom-call | flops 1207959552 | bytes 12000000 | tf_op jit(solution)/shard_map/pallas_call | solution.py:45
  20.1 1.3 %collective-permute-done.4.side = bf16[384,128]{1,0:T(8,128)(2,1)S(1)} collective-permute-done((bf16[384,128]{1,0:T(8,128)(2,1)S(1)}, bf16[384,128]{1,0:T(8,128)(2,1)S(1)}, u32[]{:S(2)}, u32[]{:S(2)}) %collective-permute-start.4) | collective-permute-done | bytes 98336 | tf_op jit(solution)/shard_map/ppermute | solution.py:443
  21.4 2.9 %shard_map.107 = (bf16[256,2048]{1,0:T(8,128)(2,1)S(1)}, bf16[256,2048]{1,0:T(8,128)(2,1)S(1)}, bf16[384,128]{1,0:T(8,128)(2,1)S(1)}) custom-call(bf16[2048,2304]{1,0:T(8,128)(2,1)S(1)} %get-tuple-element.29.near, f32[1,2048]{1,0:T(1,128)S(1)} %get-tuple-element.36.inv, bf16[128,2048]{1,0:T(8,128)(2,1)S(1)} %get-tuple-element.38.first, ...), custom_call_target="tpu_custom_call" | custom-call | flops 2147483648 | bytes 8388608 | tf_op jit(solution)/shard_map/pallas_call | solution.py:45
  24.4 2.0 %shard_map.108.acc = f32[16,16,128]{2,1,0:T(8,128)S(1)} custom-call(s32[352]{0:T(512)S(4)} %get-tuple-element.35.codes, bf16[256,128,128]{2,1,0:T(8,128)(2,1)S(1)} %bitcast.2, bf16[8,16,8192]{2,1,0:T(8,128)(2,1)S(1)} %copy-done, bf16[8,16,8192]{2,1,0:T(8,128)(2,1)S(1)} %collective-permute-done.3.side, bf16[256,2048]{1,0:T(8,128)(2,1)S(1)} %get-tuple-element.41.after.third), custom_call_target="tpu_custom_call" | custom-call | flops 2000000000 | bytes 10000000 | tf_op jit(solution)/shard_map/pallas_call | solution.py:45
  26.4 0.3 collective-permute-done.cross
  26.7 1.7 %shard_map.109 = (f32[16,2048]{1,0:T(8,128)S(1)}, bf16[16,2048]{1,0:T(8,128)(2,1)S(1)}, bf16[16,128]{1,0:T(8,128)(2,1)S(1)}) custom-call(s32[352]{0:T(512)S(4)} %get-tuple-element.30.codes, bf16[256,128,128]{2,1,0:T(8,128)(2,1)S(1)} %bitcast.2, bf16[2048,2304]{1,0:T(8,128)(2,1)S(1)} %get-tuple-element.29.near, ...), custom_call_target="tpu_custom_call" | custom-call | flops 1000000000 | bytes 1000000 | tf_op jit(solution)/shard_map/pallas_call | solution.py:45
  28.5 2.3 %shard_map.110.coupling = f32[16,2048]{1,0:T(8,128)S(1)} custom-call(bf16[16,2048]{1,0:T(8,128)(2,1)S(1)} %get-tuple-element.44.x, bf16[2048,2304]{1,0:T(8,128)(2,1)S(1)} %get-tuple-element.29.near), custom_call_target="tpu_custom_call" | custom-call | flops 134217728 | bytes 8388608 | tf_op jit(solution)/shard_map/pallas_call | solution.py:45
  30.7 0.3 shard_map.111
  31.0 0.6 %collective-permute-start.6 = (bf16[32,2048]{1,0:T(8,128)(2,1)S(1)}, bf16[32,2048]{1,0:T(8,128)(2,1)S(1)}, u32[]{:S(2)}, u32[]{:S(2)}) collective-permute-start(bf16[32,2048]{1,0:T(8,128)(2,1)S(1)} %get-tuple-element.47), channel_id=1, source_target_pairs={{0,4},{4,0},{8,12},{12,8},{16,20},{20,16},{24,28},{28,24},{32,36},... | collective-permute-start | bytes 393224 | tf_op jit(solution)/shard_map/ppermute | solution.py:477
  31.6 2.8 %collective-permute-start.9 = (bf16[32,2048]{1,0:T(8,128)(2,1)S(1)}, bf16[32,2048]{1,0:T(8,128)(2,1)S(1)}, u32[]{:S(2)}, u32[]{:S(2)}) collective-permute-start(bf16[32,2048]{1,0:T(8,128)(2,1)S(1)} %get-tuple-element.47), channel_id=1, source_target_pairs={{4,16},{12,24},{20,32},{28,40},{36,48},{44,56},{52,64},{60,72},{68... | collective-permute-start | bytes 393224 | tf_op jit(solution)/shard_map/ppermute | solution.py:478
  34.4 0.2 shard_map.114
  34.6 4.9 %collective-permute-start.8 = (bf16[432,128]{1,0:T(8,128)(2,1)S(1)}, bf16[432,128]{1,0:T(8,128)(2,1)S(1)}, u32[]{:S(2)}, u32[]{:S(2)}) collective-permute-start(bf16[432,128]{1,0:T(8,128)(2,1)S(1)} %shard_map.114), channel_id=1, source_target_pairs={{4,8},{12,16},{20,24},{28,32},{36,40},{44,48},{52,56},{60,64},{68,... | collective-permute-start | bytes 331784 | tf_op jit(solution)/shard_map/ppermute | solution.py:488
  39.5 2.4 %shard_map.112 = (bf16[16,2048]{1,0:T(8,128)(2,1)S(1)}, bf16[16,128]{1,0:T(8,128)(2,1)S(1)}) custom-call(bf16[2048,2304]{1,0:T(8,128)(2,1)S(1)} %get-tuple-element.29.near, bf16[16,2048]{1,0:T(8,128)(2,1)S(1)} %get-tuple-element.46.x.y, bf16[32,2048]{1,0:T(8,128)(2,1)S(1)} %collective-permute-done.6.side, f32[16,2048]{1,0:T(8,128)S(1)} %get-tuple-element.45.rhs, ...), custom_call_target="tpu_custom_call" | custom-call | flops 134217728 | bytes 8388608 | tf_op jit(solution)/shard_map/pallas_call | solution.py:45
  42.0 0.2 collective-permute-start.7
  42.2 2.3 %shard_map.113.after.coupling = f32[16,2048]{1,0:T(8,128)S(1)} custom-call(bf16[16,2048]{1,0:T(8,128)(2,1)S(1)} %get-tuple-element.49.x, bf16[2048,2304]{1,0:T(8,128)(2,1)S(1)} %get-tuple-element.29.near), custom_call_target="tpu_custom_call" | custom-call | flops 134217728 | bytes 8388608 | tf_op jit(solution)/shard_map/pallas_call | solution.py:45
  44.4 0.3 shard_map.115
  44.7 0.3 collective-permute-start.10
  45.1 0.5 shard_map.116.partial
  45.5 0.4 collective-permute-done.10.other
  45.9 0.2 shard_map.117
  46.1 3.3 %collective-permute-start.13 = (bf16[16,2048]{1,0:T(8,128)(2,1)S(1)}, bf16[16,2048]{1,0:T(8,128)(2,1)S(1)}, u32[]{:S(2)}, u32[]{:S(2)}) collective-permute-start(bf16[16,2048]{1,0:T(8,128)(2,1)S(1)} %get-tuple-element.55.x), channel_id=1, source_target_pairs={{0,2},{1,3},{2,0},{3,1},{4,6},{5,7},{6,4},{7,5},{8,10},{9,11},{10,... | collective-permute-start | bytes 196616 | tf_op jit(solution)/shard_map/ppermute | solution.py:531
  49.4 1.1 %collective-permute-start.12 = (bf16[16,2048]{1,0:T(8,128)(2,1)S(1)}, bf16[16,2048]{1,0:T(8,128)(2,1)S(1)}, u32[]{:S(2)}, u32[]{:S(2)}) collective-permute-start(bf16[16,2048]{1,0:T(8,128)(2,1)S(1)} %get-tuple-element.55.x), channel_id=1, source_target_pairs={{0,3},{1,2},{2,1},{3,0},{4,7},{5,6},{6,5},{7,4},{8,11},{9,10},{10,... | collective-permute-start | bytes 196616 | tf_op jit(solution)/shard_map/ppermute | solution.py:531
  50.5 0.7 %copy.11 = f32[16,2048]{1,0:T(8,128)} copy(f32[16,2048]{1,0:T(8,128)S(1)} %get-tuple-element.56) | data formatting | bytes 262144
  51.1 0.9 %collective-permute-done.13.two = bf16[16,2048]{1,0:T(8,128)(2,1)S(1)} collective-permute-done((bf16[16,2048]{1,0:T(8,128)(2,1)S(1)}, bf16[16,2048]{1,0:T(8,128)(2,1)S(1)}, u32[]{:S(2)}, u32[]{:S(2)}) %collective-permute-start.13) | collective-permute-done | bytes 65568 | tf_op jit(solution)/shard_map/ppermute | solution.py:531
  52.0 2.8 %collective-permute-done.12.three = bf16[16,2048]{1,0:T(8,128)(2,1)S(1)} collective-permute-done((bf16[16,2048]{1,0:T(8,128)(2,1)S(1)}, bf16[16,2048]{1,0:T(8,128)(2,1)S(1)}, u32[]{:S(2)}, u32[]{:S(2)}) %collective-permute-start.12) | collective-permute-done | bytes 65568 | tf_op jit(solution)/shard_map/ppermute | solution.py:531
  54.9 0.7 %shard_map.118 = bf16[16,8192]{1,0:T(8,128)(2,1)} custom-call(bf16[16,2048]{1,0:T(8,128)(2,1)S(1)} %get-tuple-element.55.x, bf16[16,2048]{1,0:T(8,128)(2,1)S(1)} %collective-permute-done.11.one, bf16[16,2048]{1,0:T(8,128)(2,1)S(1)} %collective-permute-done.12.three, bf16[16,2048]{1,0:T(8,128)(2,1)S(1)} %collective-permute-done.13.two), custom_call_target="tpu_custom_call" | custom-call | bytes 1048576 | tf_op jit(solution)/shard_map/pallas_call | solution.py:45
  (21 shorter events, 0.3 us)
Async XLA Ops:
  0.6 23.7 %collective-permute-start.3 = (bf16[8,16,8192]{2,1,0:T(8,128)(2,1)}, bf16[8,16,8192]{2,1,0:T(8,128)(2,1)S(1)}, u32[]{:S(2)}, u32[]{:S(2)}) collective-permute-start(bf16[8,16,8192]{2,1,0:T(8,128)(2,1)} %own.1), channel_id=1, source_target_pairs={{0,4},{4,0},{8,12},{12,8},{16,20},{20,16},{24,28},{28,24},{32,36},... | collective-permute-start | bytes 6291464 | tf_op jit(solution)/shard_map/ppermute | solution.py:405
  2.1 13.2 %collective-permute-start.1 = (bf16[2,16,8192]{2,1,0:T(8,128)(2,1)S(1)}, bf16[2,16,8192]{2,1,0:T(8,128)(2,1)S(1)}, u32[]{:S(2)}, u32[]{:S(2)}) collective-permute-start(bf16[2,16,8192]{2,1,0:T(8,128)(2,1)S(1)} %get-tuple-element.32), channel_id=1, source_target_pairs={{4,8},{12,16},{20,24},{28,32},{36,40},{44,48},{52,56},{60,64},{68,... | collective-permute-start | bytes 1572872 | tf_op jit(solution)/shard_map/ppermute | solution.py:403
  8.5 18.2 %collective-permute-start = (bf16[4,16,8192]{2,1,0:T(8,128)(2,1)S(1)}, bf16[4,16,8192]{2,1,0:T(8,128)(2,1)S(1)}, u32[]{:S(2)}, u32[]{:S(2)}) collective-permute-start(bf16[4,16,8192]{2,1,0:T(8,128)(2,1)S(1)} %get-tuple-element.31), channel_id=1, source_target_pairs={{4,8},{12,16},{20,24},{28,32},{36,40},{44,48},{52,56},{60,64},{68,... | collective-permute-start | bytes 3145736 | tf_op jit(solution)/shard_map/ppermute | solution.py:404
  15.3 11.4 %collective-permute-start.2 = (bf16[2,16,8192]{2,1,0:T(8,128)(2,1)S(1)}, bf16[2,16,8192]{2,1,0:T(8,128)(2,1)S(1)}, u32[]{:S(2)}, u32[]{:S(2)}) collective-permute-start(bf16[2,16,8192]{2,1,0:T(8,128)(2,1)S(1)} %collective-permute-done.1.mine), channel_id=1, source_target_pairs={{0,1},{1,0},{2,3},{3,2},{5,6},{6,5},{7,4},{4,7},{10,11},{11,10},{8... | collective-permute-start | bytes 1572872 | tf_op jit(solution)/shard_map/ppermute | solution.py:426
  16.9 7.4 %slice-start = ((s8[8388608]{0:T(1024)(128)(4,1)}), s8[4194304]{0:T(1024)(128)(4,1)S(1)}, s32[]{:S(2)}) async-start(s8[8388608]{0:T(1024)(128)(4,1)} %bitcast.1), calls=%async_computation | async-start | bytes 8388608
  16.9 7.5 %copy-start = (bf16[8,16,8192]{2,1,0:T(8,128)(2,1)S(1)}, bf16[8,16,8192]{2,1,0:T(8,128)(2,1)}, u32[]{:S(2)}) copy-start(bf16[8,16,8192]{2,1,0:T(8,128)(2,1)} %own.1) | copy-start | bytes 6291460
  20.0 1.4 %collective-permute-start.4 = (bf16[384,128]{1,0:T(8,128)(2,1)S(1)}, bf16[384,128]{1,0:T(8,128)(2,1)S(1)}, u32[]{:S(2)}, u32[]{:S(2)}) collective-permute-start(bf16[384,128]{1,0:T(8,128)(2,1)S(1)} %get-tuple-element.40), channel_id=1, source_target_pairs={{0,4},{4,0},{8,12},{12,8},{16,20},{20,16},{24,28},{28,24},{32,36},... | collective-permute-start | bytes 294920 | tf_op jit(solution)/shard_map/ppermute | solution.py:443
  21.3 3.0 %slice-start.1 = ((s8[8388608]{0:T(1024)(128)(4,1)}), s8[4194304]{0:T(1024)(128)(4,1)S(1)}, s32[]{:S(2)}) async-start(s8[8388608]{0:T(1024)(128)(4,1)} %bitcast.1), calls=%async_computation.1 | async-start | bytes 8388608
  24.3 2.4 %copy-start.1 = (f32[16,2048]{1,0:T(8,128)S(1)}, f32[16,2048]{1,0:T(8,128)}, u32[]{:S(2)}) copy-start(f32[16,2048]{1,0:T(8,128)} %incident.1) | copy-start | bytes 393220
  28.4 2.3 %collective-permute-start.5 = (bf16[16,128]{1,0:T(8,128)(2,1)S(1)}, bf16[16,128]{1,0:T(8,128)(2,1)S(1)}, u32[]{:S(2)}, u32[]{:S(2)}) collective-permute-start(bf16[16,128]{1,0:T(8,128)(2,1)S(1)} %get-tuple-element.43), channel_id=1, source_target_pairs={{0,4},{4,0},{8,12},{12,8},{16,20},{20,16},{24,28},{28,24},{32,36},... | collective-permute-start | bytes 12296 | tf_op jit(solution)/shard_map/ppermute | solution.py:466
  31.0 3.4 %collective-permute-start.6 = (bf16[32,2048]{1,0:T(8,128)(2,1)S(1)}, bf16[32,2048]{1,0:T(8,128)(2,1)S(1)}, u32[]{:S(2)}, u32[]{:S(2)}) collective-permute-start(bf16[32,2048]{1,0:T(8,128)(2,1)S(1)} %get-tuple-element.47), channel_id=1, source_target_pairs={{0,4},{4,0},{8,12},{12,8},{16,20},{20,16},{24,28},{28,24},{32,36},... | collective-permute-start | bytes 393224 | tf_op jit(solution)/shard_map/ppermute | solution.py:477
  31.6 12.9 %collective-permute-start.9 = (bf16[32,2048]{1,0:T(8,128)(2,1)S(1)}, bf16[32,2048]{1,0:T(8,128)(2,1)S(1)}, u32[]{:S(2)}, u32[]{:S(2)}) collective-permute-start(bf16[32,2048]{1,0:T(8,128)(2,1)S(1)} %get-tuple-element.47), channel_id=1, source_target_pairs={{4,16},{12,24},{20,32},{28,40},{36,48},{44,56},{52,64},{60,72},{68... | collective-permute-start | bytes 393224 | tf_op jit(solution)/shard_map/ppermute | solution.py:478
  34.6 9.8 %collective-permute-start.8 = (bf16[432,128]{1,0:T(8,128)(2,1)S(1)}, bf16[432,128]{1,0:T(8,128)(2,1)S(1)}, u32[]{:S(2)}, u32[]{:S(2)}) collective-permute-start(bf16[432,128]{1,0:T(8,128)(2,1)S(1)} %shard_map.114), channel_id=1, source_target_pairs={{4,8},{12,16},{20,24},{28,32},{36,40},{44,48},{52,56},{60,64},{68,... | collective-permute-start | bytes 331784 | tf_op jit(solution)/shard_map/ppermute | solution.py:488
  42.0 2.5 %collective-permute-start.7 = (bf16[16,128]{1,0:T(8,128)(2,1)S(1)}, bf16[16,128]{1,0:T(8,128)(2,1)S(1)}, u32[]{:S(2)}, u32[]{:S(2)}) collective-permute-start(bf16[16,128]{1,0:T(8,128)(2,1)S(1)} %get-tuple-element.48), channel_id=1, source_target_pairs={{0,4},{4,0},{8,12},{12,8},{16,20},{20,16},{24,28},{28,24},{32,36},... | collective-permute-start | bytes 12296 | tf_op jit(solution)/shard_map/ppermute | solution.py:498
  44.7 1.2 %collective-permute-start.10 = (bf16[32,128]{1,0:T(8,128)(2,1)S(1)}, bf16[32,128]{1,0:T(8,128)(2,1)S(1)}, u32[]{:S(2)}, u32[]{:S(2)}) collective-permute-start(bf16[32,128]{1,0:T(8,128)(2,1)S(1)} %get-tuple-element.51.mine), channel_id=1, source_target_pairs={{0,4},{4,0},{8,12},{12,8},{16,20},{20,16},{24,28},{28,24},{32,36},... | collective-permute-start | bytes 24584 | tf_op jit(solution)/shard_map/ppermute | solution.py:511
  46.1 5.9 %collective-permute-start.13 = (bf16[16,2048]{1,0:T(8,128)(2,1)S(1)}, bf16[16,2048]{1,0:T(8,128)(2,1)S(1)}, u32[]{:S(2)}, u32[]{:S(2)}) collective-permute-start(bf16[16,2048]{1,0:T(8,128)(2,1)S(1)} %get-tuple-element.55.x), channel_id=1, source_target_pairs={{0,2},{1,3},{2,0},{3,1},{4,6},{5,7},{6,4},{7,5},{8,10},{9,11},{10,... | collective-permute-start | bytes 196616 | tf_op jit(solution)/shard_map/ppermute | solution.py:531
  49.4 5.5 %collective-permute-start.12 = (bf16[16,2048]{1,0:T(8,128)(2,1)S(1)}, bf16[16,2048]{1,0:T(8,128)(2,1)S(1)}, u32[]{:S(2)}, u32[]{:S(2)}) collective-permute-start(bf16[16,2048]{1,0:T(8,128)(2,1)S(1)} %get-tuple-element.55.x), channel_id=1, source_target_pairs={{0,3},{1,2},{2,1},{3,0},{4,7},{5,6},{6,5},{7,4},{8,11},{9,10},{10,... | collective-permute-start | bytes 196616 | tf_op jit(solution)/shard_map/ppermute | solution.py:531
  50.5 4.4 %collective-permute-start.11 = (bf16[16,2048]{1,0:T(8,128)(2,1)S(1)}, bf16[16,2048]{1,0:T(8,128)(2,1)S(1)}, u32[]{:S(2)}, u32[]{:S(2)}) collective-permute-start(bf16[16,2048]{1,0:T(8,128)(2,1)S(1)} %get-tuple-element.55.x), channel_id=1, source_target_pairs={{0,1},{1,0},{2,3},{3,2},{4,5},{5,4},{6,7},{7,6},{8,9},{9,8},{10,11... | collective-permute-start | bytes 196616 | tf_op jit(solution)/shard_map/ppermute | solution.py:531
